TPU v7x, 256 devices: a whole 4x4x8 slice. The times are simulated.
256 devices in a mesh: expert: 64 (over z, y, core), cross: 4 (over x).
Axes of the slice: x: 4, y: 4, z: 8, core: 2. Of those that a mesh axis runs over, the one named last changes fastest.
Arguments:
- tokens: bfloat16 [32768, 3072], P(('expert', 'cross')), may hold values from -6 to 6
- route_ids: int32 [32768, 2], P(('expert', 'cross')), may hold values from 0 to 63, all different within a row; in each aligned block of 128 rows (0 to 127, 128 to 255, ...) at most 6 rows name the same one
- route_weight: bfloat16 [32768, 2], P(('expert', 'cross')), may hold values from 0.19921875 to 1
- cotangent: bfloat16 [32768, 3072], P(('expert', 'cross')), may hold values from -1.1953125 to 1.1953125
- up_weight: bfloat16 [64, 3072, 1024], P('expert', 'cross'), may hold values from -0.109375 to 0.109375
- down_weight: bfloat16 [64, 1024, 3072], P('expert', None, 'cross'), may hold values from -0.1875 to 0.1875
Outputs:
- d_tokens: bfloat16 [32768, 3072], P(('expert', 'cross'))
- d_route: bfloat16 [32768, 2], P(('expert', 'cross'))
- grad_up: bfloat16 [64, 3072, 1024], P('expert', 'cross')
- grad_down: bfloat16 [64, 1024, 3072], P('expert', None, 'cross')
Inputs may be any that keep to these rules, and one draw needn't show every extreme that they name: `route_ids`: each row names 2 different experts. In each aligned block of 128 rows (the rows of one device) no expert is named by more than 6 rows, and in some block one expert is named by exactly 6 rows; every expert is named by some row.
All inputs are finite; a program needn't handle non-finite values.
Results may differ from a plain program's by a relative error of at most 0.015.
Values may be sent and summed in bfloat16 or wider, within the bound.
No kernel may reach another device: no remote copies, remote signals or barrier semaphores. Data moves between devices by JAX's collectives and lax.ppermute only.
A program may use at most 128 MiB of HBM per device.

v0:
```python
import functools

import jax
import jax.numpy as jnp
from jax import lax
from jax.experimental import pallas as pl
from jax.experimental.pallas import tpu as pltpu
from jax.sharding import PartitionSpec as P

CAP = 6
ROWS = 8
F32 = jnp.float32
BF16 = jnp.bfloat16
VMEM = pltpu.CompilerParams(vmem_limit_bytes=60 * 1024 * 1024)
NT = (((1,), (1,)), ((), ()))
TN = (((0,), (0,)), ((), ()))


def iota(shape, dim):
    return lax.broadcasted_iota(jnp.int32, shape, dim)


def dot(a, b, dims=None):
    if dims is None:
        return jnp.dot(a, b, preferred_element_type=F32)
    return lax.dot_general(a, b, dims, preferred_element_type=F32)


def slots(first, second):
    count = first.shape[1]
    down, across = iota((count, count), 0), iota((count, count), 1)
    eye = down == across
    earlier = (down < across).astype(F32)
    first_col = jnp.sum(jnp.where(eye, first, 0), axis=1, keepdims=True)
    second_col = jnp.sum(jnp.where(eye, second, 0), axis=1, keepdims=True)

    def total(hits):
        return jnp.sum(hits, axis=0, keepdims=True)

    rank_first = total((first_col == first).astype(F32) * earlier)
    rank_second = total((first_col == second).astype(F32)) + total(
        (second_col == second).astype(F32) * earlier
    )
    return (first, rank_first.astype(jnp.int32)), (second, rank_second.astype(jnp.int32))


def row_of(route):
    return route[0] * ROWS + route[1]


def rest_of(route):
    late = (route[1] >= 3).astype(jnp.int32)
    return route[0] * ROWS + CAP + late, route[1] - 3 * late


def chosen(hit_of, routes, shares):
    return sum(
        jnp.where(hit_of(route), share, 0.0) for route, share in zip(routes, shares)
    ).astype(BF16)


def packed_block(down, part, mine, last):
    def hit_of(route):
        row, column = rest_of(route)
        return (down == row) & (column == part)

    main = chosen(lambda route: down == row_of(route), mine[0], mine[1])
    left = jnp.concatenate([main, chosen(hit_of, last[0], last[1])], axis=1)
    return dot(left, jnp.concatenate([mine[2], last[2]], axis=0)).astype(BF16)


def block_at(place_ref, ref, delta):
    block = ref.shape[1] // 4
    start = lax.rem(place_ref[0] + delta, 4) * block
    return ref[:, pl.ds(pl.multiple_of(start, 128), block)]


def token_body(place_ref, ids_ref, values_ref, out_ref):
    count, width = values_ref.shape
    block = width // 4
    down = iota((out_ref.shape[0], count), 0)
    routes = slots(ids_ref[0:1, :], ids_ref[1:2, :])
    shares = (1.0, 1.0)
    last = (routes, shares, block_at(place_ref, values_ref, 3))
    for part in range(3):
        mine = (routes, shares, block_at(place_ref, values_ref, part))
        out_ref[:, part * block : (part + 1) * block] = packed_block(down, part, mine, last)


def dispatch_tokens(place, ids, values, experts):
    count, width = values.shape
    rows_all = experts * ROWS
    packed = 3 * width // 4
    vmem = pl.BlockSpec(memory_space=pltpu.VMEM)
    return pl.pallas_call(
        token_body,
        out_shape=jax.ShapeDtypeStruct((rows_all, packed), BF16),
        in_specs=[pl.BlockSpec(memory_space=pltpu.SMEM), vmem, vmem],
        out_specs=vmem,
        compiler_params=VMEM,
        cost_estimate=pl.CostEstimate(
            flops=4 * rows_all * count * packed,
            bytes_accessed=2 * (count * width + rows_all * packed),
            transcendentals=0,
        ),
    )(place, ids, values)


NOTES = 16


def slice_body(place_ref, ids_ref, weight_ref, values_ref, *out_refs):
    count, width = values_ref.shape
    block = width // 4
    row = iota((NOTES, count), 0)
    notes = jnp.zeros((NOTES, count), F32)
    for k in range(2):
        notes = jnp.where(row == k, ids_ref[k : k + 1, :].astype(F32), notes)
        notes = jnp.where(row == 2 + k, weight_ref[k : k + 1, :].astype(F32), notes)
    for delta, out_ref in enumerate(out_refs):
        out_ref[:count, :] = block_at(place_ref, values_ref, delta)
        out_ref[count:, :] = jnp.zeros((NOTES, block), BF16)
        out_ref[count:, :count] = notes.astype(BF16)


def slices(place, ids, weight, values):
    count, width = values.shape
    vmem = pl.BlockSpec(memory_space=pltpu.VMEM)
    return pl.pallas_call(
        slice_body,
        out_shape=[jax.ShapeDtypeStruct((count + NOTES, width // 4), BF16)] * 4,
        in_specs=[pl.BlockSpec(memory_space=pltpu.SMEM), vmem, vmem, vmem],
        out_specs=[vmem] * 4,
        compiler_params=VMEM,
        cost_estimate=pl.CostEstimate(
            flops=0, bytes_accessed=4 * count * width, transcendentals=0
        ),
    )(place, ids, weight, values)


def grad_body(s0, s1, s2, s3, out_ref):
    count = s0.shape[0] - NOTES
    block = s0.shape[1]
    down = iota((out_ref.shape[0], count), 0)
    groups = []
    for ref in (s0, s1, s2, s3):
        notes = ref[count:, :count].astype(F32)
        first, second = (notes[k : k + 1, :].astype(jnp.int32) for k in range(2))
        groups.append((slots(first, second), (notes[2:3, :], notes[3:4, :]), ref[:count, :]))
    for part in range(3):
        out_ref[:, part * block : (part + 1) * block] = packed_block(
            down, part, groups[part], groups[3]
        )


def dispatch_grads(parts, experts):
    count, block = parts[0].shape
    rows_all = experts * ROWS
    vmem = pl.BlockSpec(memory_space=pltpu.VMEM)
    return pl.pallas_call(
        grad_body,
        out_shape=jax.ShapeDtypeStruct((rows_all, 3 * block), BF16),
        in_specs=[vmem] * 4,
        out_specs=vmem,
        compiler_params=VMEM,
        cost_estimate=pl.CostEstimate(
            flops=12 * rows_all * count * block,
            bytes_accessed=2 * (4 * count + 3 * rows_all) * block,
            transcendentals=0,
        ),
    )(*parts)


def pickers(experts):
    rows, packed = experts * CAP, experts * ROWS
    at, column = iota((rows, packed), 0), iota((rows, packed), 1)
    expert = lax.shift_right_logical(at * 10923, 16)
    slot = at - expert * CAP
    late = (slot >= 3).astype(jnp.int32)
    main = (column == expert * ROWS + slot).astype(BF16)
    rest = [
        ((column == expert * ROWS + CAP + late) & (slot - 3 * late == part)).astype(BF16)
        for part in range(3)
    ]
    return main, rest


def packers(experts):
    rows, packed = experts * CAP, experts * ROWS
    at, column = iota((packed, rows), 1), iota((packed, rows), 0)
    expert = lax.shift_right_logical(at * 10923, 16)
    slot = at - expert * CAP
    late = (slot >= 3).astype(jnp.int32)
    main = (column == expert * ROWS + slot).astype(BF16)
    rest = [
        ((column == expert * ROWS + CAP + late) & (slot - 3 * late == part)).astype(BF16)
        for part in range(3)
    ]
    return main, rest


def group_size(rows_all):
    experts = rows_all // ROWS
    return min(32, experts)


def unpack(packed_ref, whole_refs):
    rows_all, packed = packed_ref.shape
    block = packed // 3
    size = group_size(rows_all)
    main, rest = pickers(size)
    for group in range(rows_all // (size * ROWS)):
        source = slice(group * size * ROWS, (group + 1) * size * ROWS)
        target = slice(group * size * CAP, (group + 1) * size * CAP)
        parts = [packed_ref[source, part * block : (part + 1) * block] for part in range(3)]
        for part in range(3):
            whole_refs[part][target, :] = dot(main, parts[part]).astype(BF16)
        whole_refs[3][target, :] = sum(dot(rest[part], parts[part]) for part in range(3)).astype(
            BF16
        )


def project_body(got_ref, down_ref, g0, g1, g2, g3, b0, b1, b2, b3):
    wholes = (g0, g1, g2, g3)
    unpack(got_ref, wholes)
    hidden_width = down_ref.shape[0]
    step = min(256, hidden_width)
    for j in range(hidden_width // step):
        at = slice(j * step, (j + 1) * step)
        weight = down_ref[at, :]
        for whole, out_ref in zip(wholes, (b0, b1, b2, b3)):
            out_ref[:, at] = dot(whole[...], weight, NT).astype(out_ref.dtype)


def project(got, down):
    rows_all, packed = got.shape
    rows = rows_all // ROWS * CAP
    block, hidden_width = packed // 3, down.shape[0]
    return pl.pallas_call(
        project_body,
        out_shape=[jax.ShapeDtypeStruct((rows, block), BF16)] * 4
        + [jax.ShapeDtypeStruct((rows, hidden_width), F32)]
        + [jax.ShapeDtypeStruct((rows, hidden_width), BF16)] * 3,
        in_specs=[pl.BlockSpec(memory_space=pltpu.VMEM)] * 2,
        out_specs=[pl.BlockSpec(memory_space=pltpu.VMEM)] * 8,
        compiler_params=VMEM,
        cost_estimate=pl.CostEstimate(
            flops=10 * rows * block * hidden_width,
            bytes_accessed=12 * rows * (block + hidden_width),
            transcendentals=0,
        ),
    )(got, down)


def hidden_body(
    got_ref, up0, up1, up2a, up2b, up3, b0, b1, b2, b3,
    x0, x1, x2, x3, hidden_ref, hgrad_ref, extra_ref,
):
    unpack(got_ref, (x0, x1, x2, x3))
    half = up2a.shape[0]
    rows, hidden_width = hidden_ref.shape
    step = min(256, hidden_width)
    score = jnp.zeros((rows, 1), F32)
    for j in range(hidden_width // step):
        at = slice(j * step, (j + 1) * step)
        pre_act = dot(x0[...], up0[:, at])
        pre_act += dot(x1[...], up1[:, at])
        pre_act += dot(x3[...], up3[:, at])
        pre_act += dot(x2[:, :half], up2a[:, at])
        pre_act += dot(x2[:, half:], up2b[:, at])
        back = b0[:, at] + b1[:, at].astype(F32) + b2[:, at].astype(F32) + b3[:, at].astype(F32)
        sigmoid_val = jax.nn.sigmoid(pre_act)
        hidden = (pre_act * sigmoid_val).astype(BF16)
        hidden_ref[:, at] = hidden
        slope = sigmoid_val * (1.0 + pre_act * (1.0 - sigmoid_val))
        hgrad_ref[:, at] = (back * slope).astype(BF16)
        score += jnp.sum(hidden.astype(F32) * back, axis=1, keepdims=True)
    high = score.astype(BF16)
    low = (score - high.astype(F32)).astype(BF16)
    lane = iota((rows, 128), 1)
    extra = jnp.where(lane == 0, high.astype(F32), jnp.where(lane == 1, low.astype(F32), 0.0))
    extra_ref[...] = extra.astype(BF16)


def hidden_grads_of(got, ups, backs):
    rows_all, packed = got.shape
    rows = rows_all // ROWS * CAP
    block, hidden_width = packed // 3, ups[0].shape[1]
    return pl.pallas_call(
        hidden_body,
        out_shape=[jax.ShapeDtypeStruct((rows, block), BF16)] * 4
        + [jax.ShapeDtypeStruct((rows, hidden_width), BF16)] * 2
        + [jax.ShapeDtypeStruct((rows, 128), BF16)],
        in_specs=[pl.BlockSpec(memory_space=pltpu.VMEM)] * 10,
        out_specs=[pl.BlockSpec(memory_space=pltpu.VMEM)] * 7,
        compiler_params=VMEM,
        cost_estimate=pl.CostEstimate(
            flops=10 * rows * block * hidden_width,
            bytes_accessed=24 * block * hidden_width,
            transcendentals=rows * hidden_width,
        ),
    )(got, *ups, *backs)


def input_body(hgrad_ref, extra_ref, up0, up1, up2a, up2b, up3, ret_ref):
    rows = hgrad_ref.shape[0]
    block = up0.shape[0]
    size = group_size(ret_ref.shape[0])
    main, rest = packers(size)
    groups = [
        (slice(g * size * CAP, (g + 1) * size * CAP), slice(g * size * ROWS, (g + 1) * size * ROWS))
        for g in range(rows // (size * CAP))
    ]
    whole = hgrad_ref[...]
    half_up = up2a.shape[0]
    chunk = min(384, half_up)
    for n in range(block // chunk):
        at = slice(n * chunk, (n + 1) * chunk)
        if (n + 1) * chunk <= half_up:
            opposite = up2a[at, :]
        else:
            opposite = up2b[n * chunk - half_up : (n + 1) * chunk - half_up, :]
        last = dot(whole, up3[at, :], NT).astype(BF16)
        for part, weight in enumerate((up0[at, :], up1[at, :], opposite)):
            here = dot(whole, weight, NT).astype(BF16)
            start = part * block + n * chunk
            for source, target in groups:
                ret_ref[target, start : start + chunk] = (
                    dot(main, here[source]) + dot(rest[part], last[source])
                ).astype(BF16)
    for source, target in groups:
        ret_ref[target, 3 * block :] = dot(main, extra_ref[source, :]).astype(BF16)


def input_grads(hgrad, extra, ups, experts):
    rows, hidden_width = hgrad.shape
    block = ups[0].shape[0]
    return pl.pallas_call(
        input_body,
        out_shape=jax.ShapeDtypeStruct((experts * ROWS, 3 * block + 128), BF16),
        in_specs=[pl.BlockSpec(memory_space=pltpu.VMEM)] * 7,
        out_specs=pl.BlockSpec(memory_space=pltpu.VMEM),
        compiler_params=VMEM,
        cost_estimate=pl.CostEstimate(
            flops=10 * rows * block * hidden_width,
            bytes_accessed=16 * block * hidden_width,
            transcendentals=0,
        ),
    )(hgrad, extra, *ups)


def combine_body(place_ref, ids_ref, weight_ref, ret_ref, dtok_ref, droute_ref):
    rows_all = ret_ref.shape[0]
    count, width = dtok_ref.shape
    block = width // 4
    routes = slots(ids_ref[0:1, :], ids_ref[1:2, :])
    eye = iota((count, count), 0) == iota((count, count), 1)

    def col(row):
        return jnp.sum(jnp.where(eye, row, jnp.zeros_like(row)), axis=1, keepdims=True)

    across = iota((count, rows_all), 1)
    hits = [(across == col(row_of(route))).astype(BF16) for route in routes]
    main = hits[0] + hits[1]
    rests = [rest_of(route) for route in routes]
    rest_rows = [col(row) for row, _ in rests]
    rest_parts = [col(part) for _, part in rests]

    def put(delta, values):
        start = lax.rem(place_ref[0] + delta, 4) * block
        dtok_ref[:, pl.ds(pl.multiple_of(start, 128), block)] = values.astype(BF16)

    last = jnp.zeros((count, block), F32)
    for part in range(3):
        got = ret_ref[:, part * block : (part + 1) * block]
        put(part, dot(main, got))
        pick = sum(
            ((across == row) & (column == part)).astype(F32)
            for row, column in zip(rest_rows, rest_parts)
        ).astype(BF16)
        last += dot(pick, got)
    put(3, last)
    extra = ret_ref[:, 3 * block :]
    lane = iota((count, 2), 1)
    out = jnp.zeros((count, 2), F32)
    for k in range(2):
        pair = dot(hits[k], extra)
        value = (pair[:, 0:1] + pair[:, 1:2]) / col(weight_ref[k : k + 1, :].astype(F32))
        out = jnp.where(lane == k, value, out)
    droute_ref[...] = out.astype(BF16)


def combine(place, ids, weight, ret, count, width):
    vmem = pl.BlockSpec(memory_space=pltpu.VMEM)
    return pl.pallas_call(
        combine_body,
        out_shape=[
            jax.ShapeDtypeStruct((count, width), BF16),
            jax.ShapeDtypeStruct((count, 2), BF16),
        ],
        in_specs=[pl.BlockSpec(memory_space=pltpu.SMEM), vmem, vmem, vmem],
        out_specs=[vmem, vmem],
        compiler_params=VMEM,
        cost_estimate=pl.CostEstimate(
            flops=4 * ret.shape[0] * count * width,
            bytes_accessed=2 * (count * width + ret.size),
            transcendentals=0,
        ),
    )(place, ids, weight, ret)


def outer_body(split_left, *refs):
    halves = refs[:5]
    wholes = refs[5:9]
    out_ref = refs[9]
    half = halves[2].shape[0]
    step = min(256, out_ref.shape[0])

    def one(j, carry):
        at = pl.ds(pl.multiple_of(j * step, step), step)

        def term(part, whole):
            if split_left:
                return dot(part[:, at], whole, TN)
            return dot(whole[:, at], part[...], TN)

        def of(ref):
            return ref[...] if split_left else ref

        total = term(halves[0], of(wholes[0]))
        total += term(halves[1], of(wholes[1]))
        total += term(halves[4], of(wholes[3]))
        if split_left:
            total += term(halves[2], wholes[2][:half, :])
            total += term(halves[3], wholes[2][half:, :])
        else:
            total += dot(wholes[2][:half, at], halves[2][...], TN)
            total += dot(wholes[2][half:, at], halves[3][...], TN)
        out_ref[at, :] = total.astype(BF16)
        return carry

    lax.fori_loop(0, out_ref.shape[0] // step, one, 0)


def outer(split_left, halves, wholes):
    split_width, whole_width = halves[0].shape[1], wholes[0].shape[1]
    shape = (split_width, whole_width) if split_left else (whole_width, split_width)
    return pl.pallas_call(
        functools.partial(outer_body, split_left),
        out_shape=jax.ShapeDtypeStruct(shape, BF16),
        in_specs=[pl.BlockSpec(memory_space=pltpu.VMEM)] * 9,
        out_specs=pl.BlockSpec(memory_space=pltpu.VMEM),
        compiler_params=VMEM,
        cost_estimate=pl.CostEstimate(
            flops=8 * wholes[0].shape[0] * split_width * whole_width,
            bytes_accessed=4 * 2 * wholes[0].shape[0] * (split_width + whole_width),
            transcendentals=0,
        ),
    )(*halves, *wholes)


def shift(values, by):
    count = lax.axis_size("cross")
    return lax.ppermute(values, "cross", [(i, (i + by) % count) for i in range(count)])


def near(own):
    return own, shift(own, -1), shift(own, 1)


def far(pieces):
    own, after, before = pieces
    half = own.shape[0] // 2
    return own, after, shift(before[:half], 1), shift(after[half:], -1), before


def transpose(parts):
    return parts[0], shift(parts[3], -1), shift(parts[2], 2), shift(parts[1], 1)


def exchange(values, experts):
    blocks = values.reshape(experts, ROWS, values.shape[1])
    return lax.all_to_all(blocks, "expert", split_axis=0, concat_axis=0, tiled=True).reshape(
        values.shape
    )


def shards(tokens, route_ids, route_weight, cotangent, up_weight, down_weight):
    experts = lax.axis_size("expert")
    count, width = tokens.shape
    place = lax.axis_index("cross").astype(jnp.int32).reshape(1)
    ids, weight = route_ids.T, route_weight.T
    cot_slices = transpose(slices(place, ids, weight, cotangent))
    got_grad = exchange(dispatch_grads(cot_slices, experts), experts)
    ups = far(near(up_weight[0]))
    sent_tokens = dispatch_tokens(place, ids, tokens, experts)
    sent_tokens, ups = lax.optimization_barrier((sent_tokens, ups))
    got_tokens = exchange(sent_tokens, experts)
    *grads, b0, b1, b2, b3 = project(got_grad, down_weight[0])
    backs = transpose((b0, b1, b2, b3))
    x0, x1, x2, x3, hidden, hidden_grad, extra = hidden_grads_of(got_tokens, ups, backs)
    ret = input_grads(hidden_grad, extra, ups, experts)
    back = exchange(ret, experts)
    hiddens = far(near(hidden))
    token_slices = transpose((x0, x1, x2, x3))
    hidden_grads = far(near(hidden_grad))
    grad_down = outer(True, hiddens, grads)
    grad_up = outer(False, hidden_grads, token_slices)
    d_tokens, d_route = combine(place, ids, weight, back, count, width)
    return d_tokens, d_route, grad_up[None], grad_down[None]


def solution(mesh):
    rows = P(("expert", "cross"), None)
    ups, downs = P("expert", "cross", None), P("expert", None, "cross")
    return jax.shard_map(
        shards,
        mesh=mesh,
        in_specs=(rows, rows, rows, rows, ups, downs),
        out_specs=(rows, rows, ups, downs),
        check_vma=False,
    )
```

profile of v0, /device:TPU:1, one launch (start us, length us, event | category | flops | bytes accessed | tf_op | source)
XLA Modules:
  0.0 287.2 jit_solution(18244885328790149684)
XLA Ops:
  0.6 2.1 shard_map.94
  2.8 3.3 %collective-permute-start.4 = (bf16[144,768]{1,0:T(8,128)(2,1)}, bf16[144,768]{1,0:T(8,128)(2,1)S(1)}, u32[]{:S(2)}, u32[]{:S(2)}) collective-permute-start(bf16[144,768]{1,0:T(8,128)(2,1)} %get-tuple-element.38), channel_id=1, source_target_pairs={{0,3},{1,0},{2,1},{3,2},{4,7},{5,4},{6,5},{7,6},{8,11},{9,8},{10,9... | collective-permute-start | bytes 663560 | tf_op jit(solution)/shard_map/ppermute | solution.py:464
  7.2 8.1 %collective-permute-done.4.s1 = bf16[144,768]{1,0:T(8,128)(2,1)S(1)} collective-permute-done((bf16[144,768]{1,0:T(8,128)(2,1)}, bf16[144,768]{1,0:T(8,128)(2,1)S(1)}, u32[]{:S(2)}, u32[]{:S(2)}) %collective-permute-start.4) | collective-permute-done | bytes 221216 | tf_op jit(solution)/shard_map/ppermute | solution.py:464
  15.3 4.6 %collective-permute-done.6.s3 = bf16[144,768]{1,0:T(8,128)(2,1)S(1)} collective-permute-done((bf16[144,768]{1,0:T(8,128)(2,1)}, bf16[144,768]{1,0:T(8,128)(2,1)S(1)}, u32[]{:S(2)}, u32[]{:S(2)}) %collective-permute-start.6) | collective-permute-done | bytes 221216 | tf_op jit(solution)/shard_map/ppermute | solution.py:464
  20.6 3.8 %shard_map.95 = bf16[512,2304]{1,0:T(8,128)(2,1)} custom-call(bf16[144,768]{1,0:T(8,128)(2,1)} %get-tuple-element.37.s0, bf16[144,768]{1,0:T(8,128)(2,1)} %copy-done.8, bf16[144,768]{1,0:T(8,128)(2,1)} %copy-done.9, bf16[144,768]{1,0:T(8,128)(2,1)} %copy-done.10), custom_call_target="tpu_custom_call" | custom-call | flops 679477248 | bytes 3244032 | tf_op jit(solution)/shard_map/pallas_call | solution.py:160
  24.4 12.1 %all-to-all-start.1 = ((bf16[64,8,2304]{2,1,0:T(8,128)(2,1)}), bf16[64,8,2304]{2,1,0:T(8,128)(2,1)S(1)}, u32[]{:S(2)}, u32[]{:S(2)}) async-start(bf16[64,8,2304]{2,1,0:T(8,128)(2,1)} %bitcast.14), calls=%async_computation.1 | async-start | bytes 4718592 | tf_op jit(solution)/shard_map/all_to_all | solution.py:483
  36.6 2.7 collective-permute-start
  39.3 34.3 %collective-permute-done.1.up3 = bf16[768,1024]{1,0:T(8,128)(2,1)S(1)} collective-permute-done((bf16[768,1024]{1,0:T(8,128)(2,1)}, bf16[768,1024]{1,0:T(8,128)(2,1)S(1)}, u32[]{:S(2)}, u32[]{:S(2)}) %collective-permute-start.1) | collective-permute-done | bytes 1572896 | tf_op jit(solution)/shard_map/ppermute | solution.py:464
  76.6 2.7 collective-permute-start.3
  79.3 3.6 %shard_map.93 = bf16[512,2304]{1,0:T(8,128)(2,1)} custom-call(s32[1]{0:T(128)} %bitcast.place_ref, s32[2,128]{1,0:T(2,128)} %bitcast.24, bf16[128,3072]{1,0:T(8,128)(2,1)} %values_ref.2), custom_call_target="tpu_custom_call" | custom-call | flops 603979776 | bytes 3145728 | tf_op jit(solution)/shard_map/pallas_call | solution.py:95
  82.9 10.8 %collective-permute-done.2.up2a = bf16[384,1024]{1,0:T(8,128)(2,1)S(1)} collective-permute-done((bf16[384,1024]{1,0:T(8,128)(2,1)}, bf16[384,1024]{1,0:T(8,128)(2,1)S(1)}, u32[]{:S(2)}, u32[]{:S(2)}) %collective-permute-start.2) | collective-permute-done | bytes 786464 | tf_op jit(solution)/shard_map/ppermute | solution.py:464
  96.3 12.5 %all-to-all-start = ((bf16[64,8,2304]{2,1,0:T(8,128)(2,1)}), bf16[64,8,2304]{2,1,0:T(8,128)(2,1)S(1)}, u32[]{:S(2)}, u32[]{:S(2)}) async-start(bf16[64,8,2304]{2,1,0:T(8,128)(2,1)} %bitcast.13), calls=%async_computation | async-start | bytes 4718592 | tf_op jit(solution)/shard_map/all_to_all | solution.py:483
  108.9 7.4 %shard_map.96 = (bf16[384,768]{1,0:T(8,128)(2,1)}, bf16[384,768]{1,0:T(8,128)(2,1)}, bf16[384,768]{1,0:T(8,128)(2,1)}, bf16[384,768]{1,0:T(8,128)(2,1)}, f32[384...) custom-call(bf16[512,2304]{1,0:T(8,128)(2,1)} %bitcast.18, ...), custom_call_target="tpu_custom_call" | custom-call | flops 3019898880 | bytes 8257536 | tf_op jit(solution)/shard_map/pallas_call | solution.py:239
  116.3 3.4 %collective-permute-start.7 = (bf16[384,1024]{1,0:T(8,128)(2,1)}, bf16[384,1024]{1,0:T(8,128)(2,1)S(1)}, u32[]{:S(2)}, u32[]{:S(2)}) collective-permute-start(bf16[384,1024]{1,0:T(8,128)(2,1)} %get-tuple-element.42), channel_id=1, source_target_pairs={{0,3},{1,0},{2,1},{3,2},{4,7},{5,4},{6,5},{7,6},{8,11},{9,8},{10,9... | collective-permute-start | bytes 2359304 | tf_op jit(solution)/shard_map/ppermute | solution.py:464
  120.3 32.6 %collective-permute-done.7.b1 = bf16[384,1024]{1,0:T(8,128)(2,1)S(1)} collective-permute-done((bf16[384,1024]{1,0:T(8,128)(2,1)}, bf16[384,1024]{1,0:T(8,128)(2,1)S(1)}, u32[]{:S(2)}, u32[]{:S(2)}) %collective-permute-start.7) | collective-permute-done | bytes 786464 | tf_op jit(solution)/shard_map/ppermute | solution.py:464
  153.9 3.3 %collective-permute-done.9.b3 = bf16[384,1024]{1,0:T(8,128)(2,1)} collective-permute-done((bf16[384,1024]{1,0:T(8,128)(2,1)}, bf16[384,1024]{1,0:T(8,128)(2,1)}, u32[]{:S(2)}, u32[]{:S(2)}) %collective-permute-start.9) | collective-permute-done | bytes 786464 | tf_op jit(solution)/shard_map/ppermute | solution.py:464
  157.2 6.9 %all-to-all-done = bf16[64,8,2304]{2,1,0:T(8,128)(2,1)S(1)} async-done(((bf16[64,8,2304]{2,1,0:T(8,128)(2,1)}), bf16[64,8,2304]{2,1,0:T(8,128)(2,1)S(1)}, u32[]{:S(2)}, u32[]{:S(2)}) %all-to-all-start) | async-done | bytes 2359328 | tf_op jit(solution)/shard_map/all_to_all | solution.py:483
  165.5 10.3 %shard_map.97 = (bf16[384,768]{1,0:T(8,128)(2,1)}, bf16[384,768]{1,0:T(8,128)(2,1)}, bf16[384,768]{1,0:T(8,128)(2,1)}, bf16[384,768]{1,0:T(8,128)(2,1)}, bf16[38...) custom-call(bf16[512,2304]{1,0:T(8,128)(2,1)} %bitcast.15, bf16[768,1024]{1,0:T(8,128)(2,1)} %bitcast.21, ...), custom_call_target="tpu_custom_call" | custom-call | flops 3019898880 | bytes 18874368 | tf_op jit(solution)/shard_map/pallas_call | solution.py:289
  175.8 9.7 %shard_map.98 = bf16[512,2432]{1,0:T(8,128)(2,1)} custom-call(bf16[384,1024]{1,0:T(8,128)(2,1)} %get-tuple-element.45.hgrad_ref.refs_0_, bf16[384,128]{1,0:T(8,128)(2,1)} %get-tuple-element.46.extra_ref, bf16[768,1024]{1,0:T(8,128)(2,1)} %bitcast.22, bf16[768,1024]{1,0:T(8,128)(2,1)} %copy-done.2, bf16[384,1024]{1,0:T(8,128)(2,1)} %copy-done.5, ...), custom_call_target="tpu_custom_call" | custom-call | flops 3019898880 | bytes 12582912 | tf_op jit(solution)/shard_map/pallas_call | solution.py:338
  185.5 7.3 %all-to-all-start.2 = ((bf16[64,8,2432]{2,1,0:T(8,128)(2,1)}), bf16[64,8,2432]{2,1,0:T(8,128)(2,1)S(1)}, u32[]{:S(2)}, u32[]{:S(2)}) async-start(bf16[64,8,2432]{2,1,0:T(8,128)(2,1)} %bitcast.17), calls=%async_computation.2 | async-start | bytes 4980736 | tf_op jit(solution)/shard_map/all_to_all | solution.py:483
  192.9 3.5 %collective-permute-start.17 = (bf16[384,1024]{1,0:T(8,128)(2,1)}, bf16[384,1024]{1,0:T(8,128)(2,1)S(1)}, u32[]{:S(2)}, u32[]{:S(2)}) collective-permute-start(bf16[384,1024]{1,0:T(8,128)(2,1)} %get-tuple-element.53.refs_0_), channel_id=1, source_target_pairs={{0,3},{1,0},{2,1},{3,2},{4,7},{5,4},{6,5},{7,6},{8,11},{9,8},{10,9... | collective-permute-start | bytes 2359304 | tf_op jit(solution)/shard_map/ppermute | solution.py:464
  196.4 2.7 collective-permute-start.10
  199.0 15.0 %collective-permute-done.18.refs_4_ = bf16[384,1024]{1,0:T(8,128)(2,1)S(1)} collective-permute-done((bf16[384,1024]{1,0:T(8,128)(2,1)}, bf16[384,1024]{1,0:T(8,128)(2,1)S(1)}, u32[]{:S(2)}, u32[]{:S(2)}) %collective-permute-start.18) | collective-permute-done | bytes 786464 | tf_op jit(solution)/shard_map/ppermute | solution.py:464
  214.2 2.7 collective-permute-start.20
  217.0 13.9 %collective-permute-done.11.refs_4_ = bf16[384,1024]{1,0:T(8,128)(2,1)S(1)} collective-permute-done((bf16[384,1024]{1,0:T(8,128)(2,1)S(1)}, bf16[384,1024]{1,0:T(8,128)(2,1)S(1)}, u32[]{:S(2)}, u32[]{:S(2)}) %collective-permute-start.11) | collective-permute-done | bytes 786464 | tf_op jit(solution)/shard_map/ppermute | solution.py:464
  232.6 6.6 %collective-permute-done.19.refs_2_ = bf16[192,1024]{1,0:T(8,128)(2,1)S(1)} collective-permute-done((bf16[192,1024]{1,0:T(8,128)(2,1)S(1)}, bf16[192,1024]{1,0:T(8,128)(2,1)S(1)}, u32[]{:S(2)}, u32[]{:S(2)}) %collective-permute-start.19) | collective-permute-done | bytes 393248 | tf_op jit(solution)/shard_map/ppermute | solution.py:464
  239.3 2.7 collective-permute-start.13
  242.0 7.8 %shard_map.101 = bf16[1024,768]{1,0:T(8,128)(2,1)} custom-call(bf16[384,1024]{1,0:T(8,128)(2,1)} %get-tuple-element.53.refs_0_, bf16[384,1024]{1,0:T(8,128)(2,1)} %copy-done.14, bf16[192,1024]{1,0:T(8,128)(2,1)} %copy-done.17, bf16[192,1024]{1,0:T(8,128)(2,1)} %copy-done.18, bf16[384,1024]{1,0:T(8,128)(2,1)} %copy-done.13, ...), custom_call_target="tpu_custom_call" | custom-call | flops 2415919104 | bytes 5505024 | tf_op jit(solution)/shard_map/pallas_call | solution.py:448
  249.8 13.8 %collective-permute-done.14.refs_6_ = bf16[384,768]{1,0:T(8,128)(2,1)} collective-permute-done((bf16[384,768]{1,0:T(8,128)(2,1)}, bf16[384,768]{1,0:T(8,128)(2,1)}, u32[]{:S(2)}, u32[]{:S(2)}) %collective-permute-start.14) | collective-permute-done | bytes 589856 | tf_op jit(solution)/shard_map/ppermute | solution.py:464
  264.6 8.5 %collective-permute-done.12.refs_2_ = bf16[192,1024]{1,0:T(8,128)(2,1)} collective-permute-done((bf16[192,1024]{1,0:T(8,128)(2,1)S(1)}, bf16[192,1024]{1,0:T(8,128)(2,1)}, u32[]{:S(2)}, u32[]{:S(2)}) %collective-permute-start.12) | collective-permute-done | bytes 393248 | tf_op jit(solution)/shard_map/ppermute | solution.py:464
  273.1 7.5 %shard_map.100 = bf16[768,1024]{1,0:T(8,128)(2,1)} custom-call(bf16[384,1024]{1,0:T(8,128)(2,1)} %get-tuple-element.45.hgrad_ref.refs_0_, bf16[384,1024]{1,0:T(8,128)(2,1)} %copy-done.12, bf16[192,1024]{1,0:T(8,128)(2,1)} %collective-permute-done.12.refs_2_, bf16[192,1024]{1,0:T(8,128)(2,1)} %collective-permute-done.13.refs_3_, ...), custom_call_target="tpu_custom_call" | custom-call | flops 2415919104 | bytes 5505024 | tf_op jit(solution)/shard_map/pallas_call | solution.py:448
  282.1 3.8 %shard_map.99 = (bf16[128,3072]{1,0:T(8,128)(2,1)}, bf16[128,2]{1,0:T(8,128)(2,1)}) custom-call(s32[1]{0:T(128)} %bitcast.place_ref, s32[2,128]{1,0:T(2,128)} %bitcast.25, bf16[2,128]{1,0:T(2,128)(2,1)} %bitcast.27, bf16[512,2432]{1,0:T(8,128)(2,1)} %bitcast.16), custom_call_target="tpu_custom_call" | custom-call | flops 805306368 | bytes 3276800 | tf_op jit(solution)/shard_map/pallas_call | solution.py:395
  (70 shorter events, 16.7 us)
Async XLA Ops:
  2.8 12.5 %collective-permute-start.4 = (bf16[144,768]{1,0:T(8,128)(2,1)}, bf16[144,768]{1,0:T(8,128)(2,1)S(1)}, u32[]{:S(2)}, u32[]{:S(2)}) collective-permute-start(bf16[144,768]{1,0:T(8,128)(2,1)} %get-tuple-element.38), channel_id=1, source_target_pairs={{0,3},{1,0},{2,1},{3,2},{4,7},{5,4},{6,5},{7,6},{8,11},{9,8},{10,9... | collective-permute-start | bytes 663560 | tf_op jit(solution)/shard_map/ppermute | solution.py:464
  6.1 9.2 %collective-permute-start.5 = (bf16[144,768]{1,0:T(8,128)(2,1)}, bf16[144,768]{1,0:T(8,128)(2,1)S(1)}, u32[]{:S(2)}, u32[]{:S(2)}) collective-permute-start(bf16[144,768]{1,0:T(8,128)(2,1)} %get-tuple-element.39), channel_id=1, source_target_pairs={{0,2},{1,3},{2,0},{3,1},{4,6},{5,7},{6,4},{7,5},{8,10},{9,11},{10,... | collective-permute-start | bytes 663560 | tf_op jit(solution)/shard_map/ppermute | solution.py:464
  6.6 13.3 %collective-permute-start.6 = (bf16[144,768]{1,0:T(8,128)(2,1)}, bf16[144,768]{1,0:T(8,128)(2,1)S(1)}, u32[]{:S(2)}, u32[]{:S(2)}) collective-permute-start(bf16[144,768]{1,0:T(8,128)(2,1)} %get-tuple-element.40), channel_id=1, source_target_pairs={{0,1},{1,2},{2,3},{3,0},{4,5},{5,6},{6,7},{7,4},{8,9},{9,10},{10,1... | collective-permute-start | bytes 663560 | tf_op jit(solution)/shard_map/ppermute | solution.py:464
  24.4 70.5 %all-to-all-start.1 = ((bf16[64,8,2304]{2,1,0:T(8,128)(2,1)}), bf16[64,8,2304]{2,1,0:T(8,128)(2,1)S(1)}, u32[]{:S(2)}, u32[]{:S(2)}) async-start(bf16[64,8,2304]{2,1,0:T(8,128)(2,1)} %bitcast.14), calls=%async_computation.1 | async-start | bytes 4718592 | tf_op jit(solution)/shard_map/all_to_all | solution.py:483
  36.5 37.0 %collective-permute-start.1 = (bf16[768,1024]{1,0:T(8,128)(2,1)}, bf16[768,1024]{1,0:T(8,128)(2,1)S(1)}, u32[]{:S(2)}, u32[]{:S(2)}) collective-permute-start(bf16[768,1024]{1,0:T(8,128)(2,1)} %bitcast.19), channel_id=1, source_target_pairs={{0,1},{1,2},{2,3},{3,0},{4,5},{5,6},{6,7},{7,4},{8,9},{9,10},{10,1... | collective-permute-start | bytes 4718600 | tf_op jit(solution)/shard_map/ppermute | solution.py:464
  36.6 37.9 %collective-permute-start = (bf16[768,1024]{1,0:T(8,128)(2,1)}, bf16[768,1024]{1,0:T(8,128)(2,1)S(1)}, u32[]{:S(2)}, u32[]{:S(2)}) collective-permute-start(bf16[768,1024]{1,0:T(8,128)(2,1)} %bitcast.20), channel_id=1, source_target_pairs={{0,3},{1,0},{2,1},{3,2},{4,7},{5,4},{6,5},{7,6},{8,11},{9,8},{10,9... | collective-permute-start | bytes 4718600 | tf_op jit(solution)/shard_map/ppermute | solution.py:464
  74.5 19.2 %collective-permute-start.2 = (bf16[384,1024]{1,0:T(8,128)(2,1)}, bf16[384,1024]{1,0:T(8,128)(2,1)S(1)}, u32[]{:S(2)}, u32[]{:S(2)}) collective-permute-start(bf16[384,1024]{1,0:T(8,128)(2,1)} %slice.24), channel_id=1, source_target_pairs={{0,1},{1,2},{2,3},{3,0},{4,5},{5,6},{6,7},{7,4},{8,9},{9,10},{10,1... | collective-permute-start | bytes 2359304 | tf_op jit(solution)/shard_map/ppermute | solution.py:464
  76.6 18.2 %collective-permute-start.3 = (bf16[384,1024]{1,0:T(8,128)(2,1)}, bf16[384,1024]{1,0:T(8,128)(2,1)}, u32[]{:S(2)}, u32[]{:S(2)}) collective-permute-start(bf16[384,1024]{1,0:T(8,128)(2,1)} %slice.25), channel_id=1, source_target_pairs={{0,3},{1,0},{2,1},{3,2},{4,7},{5,4},{6,5},{7,6},{8,11},{9,8},{10,9... | collective-permute-start | bytes 2359304 | tf_op jit(solution)/shard_map/ppermute | solution.py:464
  93.7 22.6 %copy-start.5 = (bf16[384,1024]{1,0:T(8,128)(2,1)}, bf16[384,1024]{1,0:T(8,128)(2,1)S(1)}, u32[]{:S(2)}) copy-start(bf16[384,1024]{1,0:T(8,128)(2,1)S(1)} %collective-permute-done.2.up2a) | copy-start | bytes 2359300
  96.3 67.7 %all-to-all-start = ((bf16[64,8,2304]{2,1,0:T(8,128)(2,1)}), bf16[64,8,2304]{2,1,0:T(8,128)(2,1)S(1)}, u32[]{:S(2)}, u32[]{:S(2)}) async-start(bf16[64,8,2304]{2,1,0:T(8,128)(2,1)} %bitcast.13), calls=%async_computation | async-start | bytes 4718592 | tf_op jit(solution)/shard_map/all_to_all | solution.py:483
  116.3 36.7 %collective-permute-start.7 = (bf16[384,1024]{1,0:T(8,128)(2,1)}, bf16[384,1024]{1,0:T(8,128)(2,1)S(1)}, u32[]{:S(2)}, u32[]{:S(2)}) collective-permute-start(bf16[384,1024]{1,0:T(8,128)(2,1)} %get-tuple-element.42), channel_id=1, source_target_pairs={{0,3},{1,0},{2,1},{3,2},{4,7},{5,4},{6,5},{7,6},{8,11},{9,8},{10,9... | collective-permute-start | bytes 2359304 | tf_op jit(solution)/shard_map/ppermute | solution.py:464
  119.7 33.3 %collective-permute-start.8 = (bf16[384,1024]{1,0:T(8,128)(2,1)}, bf16[384,1024]{1,0:T(8,128)(2,1)S(1)}, u32[]{:S(2)}, u32[]{:S(2)}) collective-permute-start(bf16[384,1024]{1,0:T(8,128)(2,1)} %get-tuple-element.43), channel_id=1, source_target_pairs={{0,2},{1,3},{2,0},{3,1},{4,6},{5,7},{6,4},{7,5},{8,10},{9,11},{10,... | collective-permute-start | bytes 2359304 | tf_op jit(solution)/shard_map/ppermute | solution.py:464
  119.7 37.5 %collective-permute-start.9 = (bf16[384,1024]{1,0:T(8,128)(2,1)}, bf16[384,1024]{1,0:T(8,128)(2,1)}, u32[]{:S(2)}, u32[]{:S(2)}) collective-permute-start(bf16[384,1024]{1,0:T(8,128)(2,1)} %get-tuple-element.44), channel_id=1, source_target_pairs={{0,1},{1,2},{2,3},{3,0},{4,5},{5,6},{6,7},{7,4},{8,9},{9,10},{10,1... | collective-permute-start | bytes 2359304 | tf_op jit(solution)/shard_map/ppermute | solution.py:464
  153.0 11.1 %copy-start.6 = (bf16[384,1024]{1,0:T(8,128)(2,1)}, bf16[384,1024]{1,0:T(8,128)(2,1)S(1)}, u32[]{:S(2)}) copy-start(bf16[384,1024]{1,0:T(8,128)(2,1)S(1)} %collective-permute-done.7.b1) | copy-start | bytes 2359300
  185.5 10.9 %copy-start.15 = (bf16[384,1024]{1,0:T(8,128)(2,1)S(1)}, bf16[384,1024]{1,0:T(8,128)(2,1)}, u32[]{:S(2)}) copy-start(bf16[384,1024]{1,0:T(8,128)(2,1)} %get-tuple-element.45.hgrad_ref.refs_0_) | copy-start | bytes 2359300
  185.5 95.1 %all-to-all-start.2 = ((bf16[64,8,2432]{2,1,0:T(8,128)(2,1)}), bf16[64,8,2432]{2,1,0:T(8,128)(2,1)S(1)}, u32[]{:S(2)}, u32[]{:S(2)}) async-start(bf16[64,8,2432]{2,1,0:T(8,128)(2,1)} %bitcast.17), calls=%async_computation.2 | async-start | bytes 4980736 | tf_op jit(solution)/shard_map/all_to_all | solution.py:483
  192.8 21.2 %collective-permute-start.18 = (bf16[384,1024]{1,0:T(8,128)(2,1)}, bf16[384,1024]{1,0:T(8,128)(2,1)S(1)}, u32[]{:S(2)}, u32[]{:S(2)}) collective-permute-start(bf16[384,1024]{1,0:T(8,128)(2,1)} %get-tuple-element.53.refs_0_), channel_id=1, source_target_pairs={{0,1},{1,2},{2,3},{3,0},{4,5},{5,6},{6,7},{7,4},{8,9},{9,10},{10,1... | collective-permute-start | bytes 2359304 | tf_op jit(solution)/shard_map/ppermute | solution.py:464
  192.9 21.3 %collective-permute-start.17 = (bf16[384,1024]{1,0:T(8,128)(2,1)}, bf16[384,1024]{1,0:T(8,128)(2,1)S(1)}, u32[]{:S(2)}, u32[]{:S(2)}) collective-permute-start(bf16[384,1024]{1,0:T(8,128)(2,1)} %get-tuple-element.53.refs_0_), channel_id=1, source_target_pairs={{0,3},{1,0},{2,1},{3,2},{4,7},{5,4},{6,5},{7,6},{8,11},{9,8},{10,9... | collective-permute-start | bytes 2359304 | tf_op jit(solution)/shard_map/ppermute | solution.py:464
  196.4 34.5 %collective-permute-start.11 = (bf16[384,1024]{1,0:T(8,128)(2,1)S(1)}, bf16[384,1024]{1,0:T(8,128)(2,1)S(1)}, u32[]{:S(2)}, u32[]{:S(2)}) collective-permute-start(bf16[384,1024]{1,0:T(8,128)(2,1)S(1)} %copy-done.15), channel_id=1, source_target_pairs={{0,1},{1,2},{2,3},{3,0},{4,5},{5,6},{6,7},{7,4},{8,9},{9,10},{10,1... | collective-permute-start | bytes 2359304 | tf_op jit(solution)/shard_map/ppermute | solution.py:464
  196.4 34.6 %collective-permute-start.10 = (bf16[384,1024]{1,0:T(8,128)(2,1)S(1)}, bf16[384,1024]{1,0:T(8,128)(2,1)S(1)}, u32[]{:S(2)}, u32[]{:S(2)}) collective-permute-start(bf16[384,1024]{1,0:T(8,128)(2,1)S(1)} %copy-done.15), channel_id=1, source_target_pairs={{0,3},{1,0},{2,1},{3,2},{4,7},{5,4},{6,5},{7,6},{8,11},{9,8},{10,9... | collective-permute-start | bytes 2359304 | tf_op jit(solution)/shard_map/ppermute | solution.py:464
  214.0 18.6 %copy-start.13 = (bf16[384,1024]{1,0:T(8,128)(2,1)}, bf16[384,1024]{1,0:T(8,128)(2,1)S(1)}, u32[]{:S(2)}) copy-start(bf16[384,1024]{1,0:T(8,128)(2,1)S(1)} %collective-permute-done.18.refs_4_) | copy-start | bytes 2359300
  214.0 25.2 %collective-permute-start.19 = (bf16[192,1024]{1,0:T(8,128)(2,1)S(1)}, bf16[192,1024]{1,0:T(8,128)(2,1)S(1)}, u32[]{:S(2)}, u32[]{:S(2)}) collective-permute-start(bf16[192,1024]{1,0:T(8,128)(2,1)S(1)} %slice.28), channel_id=1, source_target_pairs={{0,1},{1,2},{2,3},{3,0},{4,5},{5,6},{6,7},{7,4},{8,9},{9,10},{10,1... | collective-permute-start | bytes 1179656 | tf_op jit(solution)/shard_map/ppermute | solution.py:464
  214.1 27.8 %copy-start.14 = (bf16[384,1024]{1,0:T(8,128)(2,1)}, bf16[384,1024]{1,0:T(8,128)(2,1)S(1)}, u32[]{:S(2)}) copy-start(bf16[384,1024]{1,0:T(8,128)(2,1)S(1)} %collective-permute-done.17.refs_1_) | copy-start | bytes 2359300
  214.2 25.1 %collective-permute-start.20 = (bf16[192,1024]{1,0:T(8,128)(2,1)S(1)}, bf16[192,1024]{1,0:T(8,128)(2,1)S(1)}, u32[]{:S(2)}, u32[]{:S(2)}) collective-permute-start(bf16[192,1024]{1,0:T(8,128)(2,1)S(1)} %slice.29), channel_id=1, source_target_pairs={{0,3},{1,0},{2,1},{3,2},{4,7},{5,4},{6,5},{7,6},{8,11},{9,8},{10,9... | collective-permute-start | bytes 1179656 | tf_op jit(solution)/shard_map/ppermute | solution.py:464
  216.9 46.6 %collective-permute-start.14 = (bf16[384,768]{1,0:T(8,128)(2,1)}, bf16[384,768]{1,0:T(8,128)(2,1)}, u32[]{:S(2)}, u32[]{:S(2)}) collective-permute-start(bf16[384,768]{1,0:T(8,128)(2,1)} %get-tuple-element.50), channel_id=1, source_target_pairs={{0,3},{1,0},{2,1},{3,2},{4,7},{5,4},{6,5},{7,6},{8,11},{9,8},{10,9... | collective-permute-start | bytes 1769480 | tf_op jit(solution)/shard_map/ppermute | solution.py:464
  230.8 11.1 %copy-start.11 = (bf16[384,1024]{1,0:T(8,128)(2,1)}, bf16[384,1024]{1,0:T(8,128)(2,1)S(1)}, u32[]{:S(2)}) copy-start(bf16[384,1024]{1,0:T(8,128)(2,1)S(1)} %collective-permute-done.11.refs_4_) | copy-start | bytes 2359300
  230.8 32.7 %collective-permute-start.15 = (bf16[384,768]{1,0:T(8,128)(2,1)}, bf16[384,768]{1,0:T(8,128)(2,1)}, u32[]{:S(2)}, u32[]{:S(2)}) collective-permute-start(bf16[384,768]{1,0:T(8,128)(2,1)} %get-tuple-element.51), channel_id=1, source_target_pairs={{0,2},{1,3},{2,0},{3,1},{4,6},{5,7},{6,4},{7,5},{8,10},{9,11},{10,... | collective-permute-start | bytes 1769480 | tf_op jit(solution)/shard_map/ppermute | solution.py:464
  231.0 11.0 %copy-start.12 = (bf16[384,1024]{1,0:T(8,128)(2,1)}, bf16[384,1024]{1,0:T(8,128)(2,1)S(1)}, u32[]{:S(2)}) copy-start(bf16[384,1024]{1,0:T(8,128)(2,1)S(1)} %collective-permute-done.10.refs_1_) | copy-start | bytes 2359300
  231.0 33.6 %collective-permute-start.16 = (bf16[384,768]{1,0:T(8,128)(2,1)}, bf16[384,768]{1,0:T(8,128)(2,1)S(1)}, u32[]{:S(2)}, u32[]{:S(2)}) collective-permute-start(bf16[384,768]{1,0:T(8,128)(2,1)} %get-tuple-element.52), channel_id=1, source_target_pairs={{0,1},{1,2},{2,3},{3,0},{4,5},{5,6},{6,7},{7,4},{8,9},{9,10},{10,1... | collective-permute-start | bytes 1769480 | tf_op jit(solution)/shard_map/ppermute | solution.py:464
  239.3 33.8 %collective-permute-start.12 = (bf16[192,1024]{1,0:T(8,128)(2,1)S(1)}, bf16[192,1024]{1,0:T(8,128)(2,1)}, u32[]{:S(2)}, u32[]{:S(2)}) collective-permute-start(bf16[192,1024]{1,0:T(8,128)(2,1)S(1)} %slice.26), channel_id=1, source_target_pairs={{0,1},{1,2},{2,3},{3,0},{4,5},{5,6},{6,7},{7,4},{8,9},{9,10},{10,1... | collective-permute-start | bytes 1179656 | tf_op jit(solution)/shard_map/ppermute | solution.py:464
  239.3 33.8 %collective-permute-start.13 = (bf16[192,1024]{1,0:T(8,128)(2,1)S(1)}, bf16[192,1024]{1,0:T(8,128)(2,1)}, u32[]{:S(2)}, u32[]{:S(2)}) collective-permute-start(bf16[192,1024]{1,0:T(8,128)(2,1)S(1)} %slice.27), channel_id=1, source_target_pairs={{0,3},{1,0},{2,1},{3,2},{4,7},{5,4},{6,5},{7,6},{8,11},{9,8},{10,9... | collective-permute-start | bytes 1179656 | tf_op jit(solution)/shard_map/ppermute | solution.py:464
  264.6 8.5 %copy-start.16 = (bf16[384,768]{1,0:T(8,128)(2,1)}, bf16[384,768]{1,0:T(8,128)(2,1)S(1)}, u32[]{:S(2)}) copy-start(bf16[384,768]{1,0:T(8,128)(2,1)S(1)} %collective-permute-done.16.refs_8_) | copy-start | bytes 1769476
  (11 other events, 24.8 us)
where the time goes:
time: 288 us; the launch traced here: 287 us
  waiting for transfers between devices  160 us (56%)
  starting transfers between devices  59.4 us (21%)
  Pallas kernels  56 us (19%)
  local copies, waits for them, and re-layouts  10.5 us (4%)
    ppermute x21, waiting for transfers between devices, shift(): lax.ppermute(values, 'cross', [(i, (i + by) % count) for i in range(count)])  154 us
    all_to_all x3, starting transfers between devices, exchange(): lax.all_to_all(blocks, 'expert', split_axis=0, concat_axis=0, tiled=True)  32 us
    ppermute x21, starting transfers between devices, shift(): lax.ppermute(values, 'cross', [(i, (i + by) % count) for i in range(count)])  27.5 us
    pallas_call x2, Pallas kernels, outer(): pl.pallas_call(functools.partial(outer_body, split_left), out_shape=jax.S...  15.3 us
    pallas_call x1, Pallas kernels, hidden_grads_of(): pl.pallas_call(hidden_body, out_shape=[jax.ShapeDtypeStruct((rows, block)...  10.3 us
    pallas_call x1, Pallas kernels, input_grads(): pl.pallas_call(input_body, out_shape=jax.ShapeDtypeStruct((experts * ROWS...  9.69 us
    unnamed x39, local copies, waits for them, and re-layouts  8.44 us
    pallas_call x1, Pallas kernels, project(): pl.pallas_call(project_body, out_shape=[jax.ShapeDtypeStruct((rows, block...  7.37 us
  transfers between devices with their start and end apart: 24, of which 14 were waited for; matrix products, arithmetic and copies ran while one was open for 1% of the time, Pallas kernels for 9%

commit v1 on v0

--- a/solution.py
+++ b/solution.py
@@ -252,59 +252,67 @@
     )(got, down)
 
 
-def hidden_body(
-    got_ref, up0, up1, up2a, up2b, up3, b0, b1, b2, b3,
-    x0, x1, x2, x3, hidden_ref, hgrad_ref, extra_ref,
+def unpack_rows_body(got_ref, x0, x1, x2, x3):
+    unpack(got_ref, (x0, x1, x2, x3))
+
+
+def unpack_rows(got):
+    rows_all, packed = got.shape
+    size = group_size(rows_all)
+    block = packed // 3
+    return pl.pallas_call(
+        unpack_rows_body,
+        grid=(rows_all // (size * ROWS),),
+        out_shape=[jax.ShapeDtypeStruct((rows_all // ROWS * CAP, block), BF16)] * 4,
+        in_specs=[pl.BlockSpec((size * ROWS, packed), lambda i: (i, 0))],
+        out_specs=[pl.BlockSpec((size * CAP, block), lambda i: (i, 0))] * 4,
+        compiler_params=VMEM,
+        cost_estimate=pl.CostEstimate(
+            flops=12 * rows_all * size * CAP * block,
+            bytes_accessed=4 * rows_all * packed,
+            transcendentals=0,
+        ),
+    )(got)
+
+
+def expert_body(
+    x0, x1, x2, x3, b0, b1, b2, b3, up0, up1, up2a, up2b, up3,
+    hidden_ref, hgrad_ref, ret_ref, w0, w1, w2, w3, p0, p1, p2, p3, sems,
 ):
-    unpack(got_ref, (x0, x1, x2, x3))
-    half = up2a.shape[0]
     rows, hidden_width = hidden_ref.shape
+    block = w0.shape[0]
+    half = block // 2
     step = min(256, hidden_width)
-    score = jnp.zeros((rows, 1), F32)
+    sources = (up0, up1, up2a, up2b, up3, b0, b1, b2, b3)
+    places = (w0, w1, w2.at[:half, :], w2.at[half:, :], w3, p0, p1, p2, p3)
+    copies = []
     for j in range(hidden_width // step):
         at = slice(j * step, (j + 1) * step)
-        pre_act = dot(x0[...], up0[:, at])
-        pre_act += dot(x1[...], up1[:, at])
-        pre_act += dot(x3[...], up3[:, at])
-        pre_act += dot(x2[:, :half], up2a[:, at])
-        pre_act += dot(x2[:, half:], up2b[:, at])
-        back = b0[:, at] + b1[:, at].astype(F32) + b2[:, at].astype(F32) + b3[:, at].astype(F32)
+        copies.append(
+            [
+                pltpu.make_async_copy(source.at[:, at], target.at[:, at], sems.at[p, j])
+                for p, (source, target) in enumerate(zip(sources, places))
+            ]
+        )
+        for copy in copies[-1]:
+            copy.start()
+    score = jnp.zeros((rows, 1), F32)
+    for j, group in enumerate(copies):
+        at = slice(j * step, (j + 1) * step)
+        for copy in group:
+            copy.wait()
+        pre_act = dot(x0[...], w0[:, at])
+        pre_act += dot(x1[...], w1[:, at])
+        pre_act += dot(x2[...], w2[:, at])
+        pre_act += dot(x3[...], w3[:, at])
+        back = p0[:, at] + p1[:, at].astype(F32) + p2[:, at].astype(F32) + p3[:, at].astype(F32)
         sigmoid_val = jax.nn.sigmoid(pre_act)
         hidden = (pre_act * sigmoid_val).astype(BF16)
         hidden_ref[:, at] = hidden
         slope = sigmoid_val * (1.0 + pre_act * (1.0 - sigmoid_val))
         hgrad_ref[:, at] = (back * slope).astype(BF16)
         score += jnp.sum(hidden.astype(F32) * back, axis=1, keepdims=True)
-    high = score.astype(BF16)
-    low = (score - high.astype(F32)).astype(BF16)
-    lane = iota((rows, 128), 1)
-    extra = jnp.where(lane == 0, high.astype(F32), jnp.where(lane == 1, low.astype(F32), 0.0))
-    extra_ref[...] = extra.astype(BF16)
-
-
-def hidden_grads_of(got, ups, backs):
-    rows_all, packed = got.shape
-    rows = rows_all // ROWS * CAP
-    block, hidden_width = packed // 3, ups[0].shape[1]
-    return pl.pallas_call(
-        hidden_body,
-        out_shape=[jax.ShapeDtypeStruct((rows, block), BF16)] * 4
-        + [jax.ShapeDtypeStruct((rows, hidden_width), BF16)] * 2
-        + [jax.ShapeDtypeStruct((rows, 128), BF16)],
-        in_specs=[pl.BlockSpec(memory_space=pltpu.VMEM)] * 10,
-        out_specs=[pl.BlockSpec(memory_space=pltpu.VMEM)] * 7,
-        compiler_params=VMEM,
-        cost_estimate=pl.CostEstimate(
-            flops=10 * rows * block * hidden_width,
-            bytes_accessed=24 * block * hidden_width,
-            transcendentals=rows * hidden_width,
-        ),
-    )(got, *ups, *backs)
-
-
-def input_body(hgrad_ref, extra_ref, up0, up1, up2a, up2b, up3, ret_ref):
-    rows = hgrad_ref.shape[0]
-    block = up0.shape[0]
+
     size = group_size(ret_ref.shape[0])
     main, rest = packers(size)
     groups = [
@@ -312,41 +320,47 @@
         for g in range(rows // (size * CAP))
     ]
     whole = hgrad_ref[...]
-    half_up = up2a.shape[0]
-    chunk = min(384, half_up)
+    chunk = min(256, block)
     for n in range(block // chunk):
         at = slice(n * chunk, (n + 1) * chunk)
-        if (n + 1) * chunk <= half_up:
-            opposite = up2a[at, :]
-        else:
-            opposite = up2b[n * chunk - half_up : (n + 1) * chunk - half_up, :]
-        last = dot(whole, up3[at, :], NT).astype(BF16)
-        for part, weight in enumerate((up0[at, :], up1[at, :], opposite)):
-            here = dot(whole, weight, NT).astype(BF16)
+        last = dot(whole, w3[at, :], NT).astype(BF16)
+        for part, weight in enumerate((w0, w1, w2)):
+            here = dot(whole, weight[at, :], NT).astype(BF16)
             start = part * block + n * chunk
             for source, target in groups:
                 ret_ref[target, start : start + chunk] = (
                     dot(main, here[source]) + dot(rest[part], last[source])
                 ).astype(BF16)
+    high = score.astype(BF16)
+    low = (score - high.astype(F32)).astype(BF16)
+    lane = iota((rows, 128), 1)
+    extra = jnp.where(lane == 0, high.astype(F32), jnp.where(lane == 1, low.astype(F32), 0.0))
+    extra = extra.astype(BF16)
     for source, target in groups:
-        ret_ref[target, 3 * block :] = dot(main, extra_ref[source, :]).astype(BF16)
-
-
-def input_grads(hgrad, extra, ups, experts):
-    rows, hidden_width = hgrad.shape
-    block = ups[0].shape[0]
-    return pl.pallas_call(
-        input_body,
-        out_shape=jax.ShapeDtypeStruct((experts * ROWS, 3 * block + 128), BF16),
-        in_specs=[pl.BlockSpec(memory_space=pltpu.VMEM)] * 7,
-        out_specs=pl.BlockSpec(memory_space=pltpu.VMEM),
-        compiler_params=VMEM,
-        cost_estimate=pl.CostEstimate(
-            flops=10 * rows * block * hidden_width,
-            bytes_accessed=16 * block * hidden_width,
-            transcendentals=0,
-        ),
-    )(hgrad, extra, *ups)
+        ret_ref[target, 3 * block :] = dot(main, extra[source]).astype(BF16)
+
+
+def expert(wholes, ups, backs, experts):
+    rows, block = wholes[0].shape
+    hidden_width = ups[0].shape[1]
+    vmem = pl.BlockSpec(memory_space=pltpu.VMEM)
+    return pl.pallas_call(
+        expert_body,
+        out_shape=[jax.ShapeDtypeStruct((rows, hidden_width), BF16)] * 2
+        + [jax.ShapeDtypeStruct((experts * ROWS, 3 * block + 128), BF16)],
+        in_specs=[vmem] * 4 + [pl.BlockSpec(memory_space=pl.ANY)] * 9,
+        out_specs=[vmem] * 3,
+        scratch_shapes=[pltpu.VMEM((block, hidden_width), BF16)] * 4
+        + [pltpu.VMEM((rows, hidden_width), F32)]
+        + [pltpu.VMEM((rows, hidden_width), BF16)] * 3
+        + [pltpu.SemaphoreType.DMA((9, hidden_width // min(256, hidden_width)))],
+        compiler_params=VMEM,
+        cost_estimate=pl.CostEstimate(
+            flops=20 * rows * block * hidden_width,
+            bytes_accessed=24 * block * hidden_width,
+            transcendentals=rows * hidden_width,
+        ),
+    )(*wholes, *backs, *ups)
 
 
 def combine_body(place_ref, ids_ref, weight_ref, ret_ref, dtok_ref, droute_ref):
@@ -409,54 +423,68 @@
     )(place, ids, weight, ret)
 
 
-def outer_body(split_left, *refs):
-    halves = refs[:5]
-    wholes = refs[5:9]
-    out_ref = refs[9]
-    half = halves[2].shape[0]
+def near_body(l0, l1, l3, r0, r1, r3, out_ref):
     step = min(256, out_ref.shape[0])
 
     def one(j, carry):
         at = pl.ds(pl.multiple_of(j * step, step), step)
-
-        def term(part, whole):
-            if split_left:
-                return dot(part[:, at], whole, TN)
-            return dot(whole[:, at], part[...], TN)
-
-        def of(ref):
-            return ref[...] if split_left else ref
-
-        total = term(halves[0], of(wholes[0]))
-        total += term(halves[1], of(wholes[1]))
-        total += term(halves[4], of(wholes[3]))
-        if split_left:
-            total += term(halves[2], wholes[2][:half, :])
-            total += term(halves[3], wholes[2][half:, :])
+        total = dot(l0[:, at], r0[...], TN)
+        total += dot(l1[:, at], r1[...], TN)
+        total += dot(l3[:, at], r3[...], TN)
+        out_ref[at, :] = total
+        return carry
+
+    lax.fori_loop(0, out_ref.shape[0] // step, one, 0)
+
+
+def outer_near(lefts, rights):
+    rows, shape = lefts[0].shape[0], (lefts[0].shape[1], rights[0].shape[1])
+    return pl.pallas_call(
+        near_body,
+        out_shape=jax.ShapeDtypeStruct(shape, F32),
+        in_specs=[pl.BlockSpec(memory_space=pltpu.VMEM)] * 6,
+        out_specs=pl.BlockSpec(memory_space=pltpu.VMEM),
+        compiler_params=VMEM,
+        cost_estimate=pl.CostEstimate(
+            flops=6 * rows * shape[0] * shape[1],
+            bytes_accessed=6 * rows * sum(shape) + 4 * shape[0] * shape[1],
+            transcendentals=0,
+        ),
+    )(*lefts, *rights)
+
+
+def last_body(left_in_halves, total_ref, whole, first, second, out_ref):
+    half = first.shape[0]
+    step = min(256, out_ref.shape[0])
+
+    def one(j, carry):
+        at = pl.ds(pl.multiple_of(j * step, step), step)
+        total = total_ref[at, :]
+        if left_in_halves:
+            total += dot(first[:, at], whole[:half, :], TN)
+            total += dot(second[:, at], whole[half:, :], TN)
         else:
-            total += dot(wholes[2][:half, at], halves[2][...], TN)
-            total += dot(wholes[2][half:, at], halves[3][...], TN)
+            total += dot(whole[:half, at], first[...], TN)
+            total += dot(whole[half:, at], second[...], TN)
         out_ref[at, :] = total.astype(BF16)
         return carry
 
     lax.fori_loop(0, out_ref.shape[0] // step, one, 0)
 
 
-def outer(split_left, halves, wholes):
-    split_width, whole_width = halves[0].shape[1], wholes[0].shape[1]
-    shape = (split_width, whole_width) if split_left else (whole_width, split_width)
-    return pl.pallas_call(
-        functools.partial(outer_body, split_left),
-        out_shape=jax.ShapeDtypeStruct(shape, BF16),
-        in_specs=[pl.BlockSpec(memory_space=pltpu.VMEM)] * 9,
+def outer_last(left_in_halves, total, whole, first, second):
+    return pl.pallas_call(
+        functools.partial(last_body, left_in_halves),
+        out_shape=jax.ShapeDtypeStruct(total.shape, BF16),
+        in_specs=[pl.BlockSpec(memory_space=pltpu.VMEM)] * 4,
         out_specs=pl.BlockSpec(memory_space=pltpu.VMEM),
         compiler_params=VMEM,
         cost_estimate=pl.CostEstimate(
-            flops=8 * wholes[0].shape[0] * split_width * whole_width,
-            bytes_accessed=4 * 2 * wholes[0].shape[0] * (split_width + whole_width),
-            transcendentals=0,
-        ),
-    )(*halves, *wholes)
+            flops=2 * whole.shape[0] * total.shape[0] * total.shape[1],
+            bytes_accessed=6 * total.size + 2 * whole.shape[0] * sum(total.shape),
+            transcendentals=0,
+        ),
+    )(total, whole, first, second)
 
 
 def shift(values, by):
@@ -492,21 +520,29 @@
     ids, weight = route_ids.T, route_weight.T
     cot_slices = transpose(slices(place, ids, weight, cotangent))
     got_grad = exchange(dispatch_grads(cot_slices, experts), experts)
-    ups = far(near(up_weight[0]))
+    ups_near = near(up_weight[0])
     sent_tokens = dispatch_tokens(place, ids, tokens, experts)
-    sent_tokens, ups = lax.optimization_barrier((sent_tokens, ups))
+    sent_tokens, ups_near = lax.optimization_barrier((sent_tokens, ups_near))
+    ups = far(ups_near)
     got_tokens = exchange(sent_tokens, experts)
-    *grads, b0, b1, b2, b3 = project(got_grad, down_weight[0])
+    g0, g1, g2, g3, b0, b1, b2, b3 = project(got_grad, down_weight[0])
     backs = transpose((b0, b1, b2, b3))
-    x0, x1, x2, x3, hidden, hidden_grad, extra = hidden_grads_of(got_tokens, ups, backs)
-    ret = input_grads(hidden_grad, extra, ups, experts)
+    got_tokens, backs, ups = lax.optimization_barrier((got_tokens, backs, ups))
+    wholes = unpack_rows(got_tokens)
+    t1, t3 = shift(wholes[3], -1), shift(wholes[1], 1)
+    hidden, hidden_grad, ret = expert(wholes, ups, backs, experts)
+    ret, t1, t3 = lax.optimization_barrier((ret, t1, t3))
     back = exchange(ret, experts)
-    hiddens = far(near(hidden))
-    token_slices = transpose((x0, x1, x2, x3))
-    hidden_grads = far(near(hidden_grad))
-    grad_down = outer(True, hiddens, grads)
-    grad_up = outer(False, hidden_grads, token_slices)
+    h0, h1, h2a, h2b, h3 = far(near(hidden))
+    d0, d1, d2a, d2b, d3 = far(near(hidden_grad))
+    t2 = shift(wholes[2], 2)
+    down_near = outer_near((h0, h1, h3), (g0, g1, g3))
+    up_near = outer_near((wholes[0], t1, t3), (d0, d1, d3))
+    grad_down = outer_last(True, down_near, g2, h2a, h2b)
+    back, grad_down, up_near = lax.optimization_barrier((back, grad_down, up_near))
     d_tokens, d_route = combine(place, ids, weight, back, count, width)
+    up_near, d_tokens, d_route = lax.optimization_barrier((up_near, d_tokens, d_route))
+    grad_up = outer_last(False, up_near, t2, d2a, d2b)
     return d_tokens, d_route, grad_up[None], grad_down[None]
 
 

time: 288 us -> 284 us (0.986); the launches traced: 287 us -> 279 us
  waiting for transfers between devices: 160 us -> 128 us
  Pallas kernels: 56 us -> 64.9 us
  starting transfers between devices: 59.4 us -> 67.3 us
  local copies, waits for them, and re-layouts: 10.5 us -> 17.9 us
    ppermute x21, waiting for transfers between devices: 154 us -> 110 us  [shift(): lax.ppermute(values, 'cross', [(i, (i + by) % count) for i in range(count)])]
    all_to_all x3, waiting for transfers between devices: 6.87 us -> 18 us  [exchange(): lax.all_to_all(blocks, 'expert', split_axis=0, concat_axis=0, tiled=True)]
    pallas_call x4 -> x6, Pallas kernels: 35.3 us -> 44.1 us  [the longest x1 17.1 us: expert(): pl.pallas_call(expert_body, out_shape=[jax.ShapeDtypeStruct((rows, hidden...]
    ppermute x21, starting transfers between devices: 27.5 us -> 36.2 us  [shift(): lax.ppermute(values, 'cross', [(i, (i + by) % count) for i in range(count)])]
    unnamed x39 -> x27, local copies, waits for them, and re-layouts: 8.44 us -> 11.5 us
  transfers between devices with their start and end apart: 24 -> 24, of which waited for: 14 -> 9; matrix products, arithmetic and copies ran while one was open for 1% -> 3% of each run, Pallas kernels for 9% -> 18%
where the time goes in v1:
time: 284 us; the launch traced here: 279 us
  waiting for transfers between devices  128 us (45%)
  starting transfers between devices  67.3 us (24%)
  Pallas kernels  64.9 us (23%)
  local copies, waits for them, and re-layouts  17.9 us (6%)
    ppermute x21, waiting for transfers between devices, shift(): lax.ppermute(values, 'cross', [(i, (i + by) % count) for i in range(count)])  110 us
    ppermute x21, starting transfers between devices, shift(): lax.ppermute(values, 'cross', [(i, (i + by) % count) for i in range(count)])  36.2 us
    all_to_all x3, starting transfers between devices, exchange(): lax.all_to_all(blocks, 'expert', split_axis=0, concat_axis=0, tiled=True)  31.1 us
    all_to_all x3, waiting for transfers between devices, exchange(): lax.all_to_all(blocks, 'expert', split_axis=0, concat_axis=0, tiled=True)  18 us
    pallas_call x1, Pallas kernels, expert(): pl.pallas_call(expert_body, out_shape=[jax.ShapeDtypeStruct((rows, hidden...  17.1 us
    pallas_call x2, Pallas kernels, outer_near(): pl.pallas_call(near_body, out_shape=jax.ShapeDtypeStruct(shape, F32), in_...  13.9 us
    unnamed x27, local copies, waits for them, and re-layouts  11.5 us
    pallas_call x2, Pallas kernels, outer_last(): pl.pallas_call(functools.partial(last_body, left_in_halves), out_shape=ja...  9.8 us
  transfers between devices with their start and end apart: 24, of which 9 were waited for; matrix products, arithmetic and copies ran while one was open for 3% of the time, Pallas kernels for 18%

profile of v1, /device:TPU:1, one launch (start us, length us, event | category | flops | bytes accessed | tf_op | source)
XLA Modules:
  0.0 279.3 jit_solution(4690824909565011067)
XLA Ops:
  0.6 2.1 shard_map.94
  2.8 3.3 %collective-permute-start.2 = (bf16[144,768]{1,0:T(8,128)(2,1)}, bf16[144,768]{1,0:T(8,128)(2,1)S(1)}, u32[]{:S(2)}, u32[]{:S(2)}) collective-permute-start(bf16[144,768]{1,0:T(8,128)(2,1)} %get-tuple-element.50), channel_id=1, source_target_pairs={{0,3},{1,0},{2,1},{3,2},{4,7},{5,4},{6,5},{7,6},{8,11},{9,8},{10,9... | collective-permute-start | bytes 663560 | tf_op jit(solution)/shard_map/ppermute | solution.py:492
  7.2 8.1 %collective-permute-done.2.s1 = bf16[144,768]{1,0:T(8,128)(2,1)S(1)} collective-permute-done((bf16[144,768]{1,0:T(8,128)(2,1)}, bf16[144,768]{1,0:T(8,128)(2,1)S(1)}, u32[]{:S(2)}, u32[]{:S(2)}) %collective-permute-start.2) | collective-permute-done | bytes 221216 | tf_op jit(solution)/shard_map/ppermute | solution.py:492
  15.3 4.6 %collective-permute-done.4.s3 = bf16[144,768]{1,0:T(8,128)(2,1)S(1)} collective-permute-done((bf16[144,768]{1,0:T(8,128)(2,1)}, bf16[144,768]{1,0:T(8,128)(2,1)S(1)}, u32[]{:S(2)}, u32[]{:S(2)}) %collective-permute-start.4) | collective-permute-done | bytes 221216 | tf_op jit(solution)/shard_map/ppermute | solution.py:492
  20.6 3.8 %shard_map.95 = bf16[512,2304]{1,0:T(8,128)(2,1)} custom-call(bf16[144,768]{1,0:T(8,128)(2,1)} %get-tuple-element.49.s0, bf16[144,768]{1,0:T(8,128)(2,1)} %copy-done.8, bf16[144,768]{1,0:T(8,128)(2,1)} %copy-done.9, bf16[144,768]{1,0:T(8,128)(2,1)} %copy-done.10), custom_call_target="tpu_custom_call" | custom-call | flops 679477248 | bytes 3244032 | tf_op jit(solution)/shard_map/pallas_call | solution.py:160
  24.3 12.1 %all-to-all-start.1 = ((bf16[64,8,2304]{2,1,0:T(8,128)(2,1)}), bf16[64,8,2304]{2,1,0:T(8,128)(2,1)S(1)}, u32[]{:S(2)}, u32[]{:S(2)}) async-start(bf16[64,8,2304]{2,1,0:T(8,128)(2,1)} %bitcast.14), calls=%async_computation.1 | async-start | bytes 4718592 | tf_op jit(solution)/shard_map/all_to_all | solution.py:511
  36.6 2.7 collective-permute-start
  39.3 3.6 %shard_map.93 = bf16[512,2304]{1,0:T(8,128)(2,1)} custom-call(s32[1]{0:T(128)} %bitcast.place_ref, s32[2,128]{1,0:T(2,128)} %bitcast.22, bf16[128,3072]{1,0:T(8,128)(2,1)} %values_ref.2), custom_call_target="tpu_custom_call" | custom-call | flops 603979776 | bytes 3145728 | tf_op jit(solution)/shard_map/pallas_call | solution.py:95
  42.9 30.8 %collective-permute-done.1.up3 = bf16[768,1024]{1,0:T(8,128)(2,1)} collective-permute-done((bf16[768,1024]{1,0:T(8,128)(2,1)}, bf16[768,1024]{1,0:T(8,128)(2,1)}, u32[]{:S(2)}, u32[]{:S(2)}) %collective-permute-start.1) | collective-permute-done | bytes 1572896 | tf_op jit(solution)/shard_map/ppermute | solution.py:492
  73.6 18.0 %all-to-all-done.1 = bf16[64,8,2304]{2,1,0:T(8,128)(2,1)S(1)} async-done(((bf16[64,8,2304]{2,1,0:T(8,128)(2,1)}), bf16[64,8,2304]{2,1,0:T(8,128)(2,1)S(1)}, u32[]{:S(2)}, u32[]{:S(2)}) %all-to-all-start.1) | async-done | bytes 2359328 | tf_op jit(solution)/shard_map/all_to_all | solution.py:511
  91.7 1.4 copy-done.2
  93.1 7.1 %all-to-all-start = ((bf16[64,8,2304]{2,1,0:T(8,128)(2,1)}), bf16[64,8,2304]{2,1,0:T(8,128)(2,1)S(1)}, u32[]{:S(2)}, u32[]{:S(2)}) async-start(bf16[64,8,2304]{2,1,0:T(8,128)(2,1)} %bitcast.13), calls=%async_computation | async-start | bytes 4718592 | tf_op jit(solution)/shard_map/all_to_all | solution.py:511
  101.5 2.1 slice.18
  103.5 2.7 collective-permute-start.9
  106.2 7.4 %shard_map.96 = (bf16[384,768]{1,0:T(8,128)(2,1)}, bf16[384,768]{1,0:T(8,128)(2,1)}, bf16[384,768]{1,0:T(8,128)(2,1)}, bf16[384,768]{1,0:T(8,128)(2,1)}, f32[384...) custom-call(bf16[512,2304]{1,0:T(8,128)(2,1)} %bitcast.18, ...), custom_call_target="tpu_custom_call" | custom-call | flops 3019898880 | bytes 8257536 | tf_op jit(solution)/shard_map/pallas_call | solution.py:239
  115.0 24.8 %collective-permute-done.8.up2a = bf16[384,1024]{1,0:T(8,128)(2,1)} collective-permute-done((bf16[384,1024]{1,0:T(8,128)(2,1)}, bf16[384,1024]{1,0:T(8,128)(2,1)}, u32[]{:S(2)}, u32[]{:S(2)}) %collective-permute-start.8) | collective-permute-done | bytes 786464 | tf_op jit(solution)/shard_map/ppermute | solution.py:492
  141.7 15.7 %collective-permute-done.7.b3 = bf16[384,1024]{1,0:T(8,128)(2,1)} collective-permute-done((bf16[384,1024]{1,0:T(8,128)(2,1)}, bf16[384,1024]{1,0:T(8,128)(2,1)}, u32[]{:S(2)}, u32[]{:S(2)}) %collective-permute-start.7) | collective-permute-done | bytes 786464 | tf_op jit(solution)/shard_map/ppermute | solution.py:492
  158.8 3.3 %shard_map.97 = (bf16[384,768]{1,0:T(8,128)(2,1)}, bf16[384,768]{1,0:T(8,128)(2,1)}, bf16[384,768]{1,0:T(8,128)(2,1)}, bf16[384,768]{1,0:T(8,128)(2,1)}) custom-call(bf16[512,2304]{1,0:T(8,128)(2,1)} %bitcast.17), custom_call_target="tpu_custom_call" | custom-call | flops 905969664 | bytes 4718592 | tf_op jit(solution)/shard_map/pallas_call | solution.py:263
  163.3 2.9 %collective-permute-start.10 = (bf16[384,768]{1,0:T(8,128)(2,1)}, bf16[384,768]{1,0:T(8,128)(2,1)}, u32[]{:S(2)}, u32[]{:S(2)}) collective-permute-start(bf16[384,768]{1,0:T(8,128)(2,1)} %get-tuple-element.64.x3), channel_id=1, source_target_pairs={{0,3},{1,0},{2,1},{3,2},{4,7},{5,4},{6,5},{7,6},{8,11},{9,8},{10,9... | collective-permute-start | bytes 1769480 | tf_op jit(solution)/shard_map/ppermute | solution.py:492
  166.2 17.1 %shard_map.98 = (bf16[384,1024]{1,0:T(8,128)(2,1)}, bf16[384,1024]{1,0:T(8,128)(2,1)}, bf16[512,2432]{1,0:T(8,128)(2,1)}) custom-call(bf16[384,768]{1,0:T(8,128)(2,1)} %get-tuple-element.61.x0.l0, bf16[384,768]{1,0:T(8,128)(2,1)} %get-tuple-element.62.x1, bf16[384,768]{1,0:T(8,128)(2,1)} %get-tuple-element.63.x2, bf16[384,768]{1,0:T(8,128)(2,1)} %get-tuple-element.64.x3, ...), custom_call_target="tpu_custom_call" | custom-call | flops 6039797760 | bytes 18874368 | tf_op jit(solution)/shard_map/pallas_call | solution.py:347
  183.4 11.8 %all-to-all-start.2 = ((bf16[64,8,2432]{2,1,0:T(8,128)(2,1)}), bf16[64,8,2432]{2,1,0:T(8,128)(2,1)S(1)}, u32[]{:S(2)}, u32[]{:S(2)}) async-start(bf16[64,8,2432]{2,1,0:T(8,128)(2,1)} %bitcast.15), calls=%async_computation.2 | async-start | bytes 4980736 | tf_op jit(solution)/shard_map/all_to_all | solution.py:511
  195.3 2.7 collective-permute-start.12
  198.0 2.7 collective-permute-start.16
  200.7 14.7 %collective-permute-done.13.l3 = bf16[384,1024]{1,0:T(8,128)(2,1)S(1)} collective-permute-done((bf16[384,1024]{1,0:T(8,128)(2,1)}, bf16[384,1024]{1,0:T(8,128)(2,1)S(1)}, u32[]{:S(2)}, u32[]{:S(2)}) %collective-permute-start.13) | collective-permute-done | bytes 786464 | tf_op jit(solution)/shard_map/ppermute | solution.py:492
  217.9 2.7 collective-permute-start.15
  220.6 11.7 %collective-permute-done.17.r3 = bf16[384,1024]{1,0:T(8,128)(2,1)S(1)} collective-permute-done((bf16[384,1024]{1,0:T(8,128)(2,1)}, bf16[384,1024]{1,0:T(8,128)(2,1)S(1)}, u32[]{:S(2)}, u32[]{:S(2)}) %collective-permute-start.17) | collective-permute-done | bytes 786464 | tf_op jit(solution)/shard_map/ppermute | solution.py:492
  235.6 12.7 %collective-permute-start.20 = (bf16[192,1024]{1,0:T(8,128)(2,1)}, bf16[192,1024]{1,0:T(8,128)(2,1)}, u32[]{:S(2)}, u32[]{:S(2)}) collective-permute-start(bf16[192,1024]{1,0:T(8,128)(2,1)} %slice.27), channel_id=1, source_target_pairs={{0,3},{1,0},{2,1},{3,2},{4,7},{5,4},{6,5},{7,6},{8,11},{9,8},{10,9... | collective-permute-start | bytes 1179656 | tf_op jit(solution)/shard_map/ppermute | solution.py:492
  248.2 6.8 %shard_map.101.total_ref = f32[768,1024]{1,0:T(8,128)} custom-call(bf16[384,768]{1,0:T(8,128)(2,1)} %get-tuple-element.61.x0.l0, bf16[384,768]{1,0:T(8,128)(2,1)} %collective-permute-done.10.l1, bf16[384,768]{1,0:T(8,128)(2,1)} %collective-permute-done.11.l3, bf16[384,1024]{1,0:T(8,128)(2,1)} %get-tuple-element.83.r0, bf16[384,1024]{1,0:T(8,128)(2,1)} %copy-done.6, ...), custom_call_target="tpu_custom_call" | custom-call | flops 1811939328 | bytes 7274496 | tf_op jit(solution)/shard_map/pallas_call | solution.py:442
  255.1 7.1 %shard_map.99.total_ref = f32[1024,768]{1,0:T(8,128)} custom-call(bf16[384,1024]{1,0:T(8,128)(2,1)} %get-tuple-element.76.l0, bf16[384,1024]{1,0:T(8,128)(2,1)} %copy-done.4, bf16[384,1024]{1,0:T(8,128)(2,1)} %copy-done.3, bf16[384,768]{1,0:T(8,128)(2,1)} %get-tuple-element.77.r0, bf16[384,768]{1,0:T(8,128)(2,1)} %get-tuple-element.78.r1, ...), custom_call_target="tpu_custom_call" | custom-call | flops 1811939328 | bytes 7274496 | tf_op jit(solution)/shard_map/pallas_call | solution.py:442
  262.9 5.0 %shard_map.100 = bf16[1024,768]{1,0:T(8,128)(2,1)} custom-call(f32[1024,768]{1,0:T(8,128)} %shard_map.99.total_ref, bf16[384,768]{1,0:T(8,128)(2,1)} %get-tuple-element.80.whole, bf16[192,1024]{1,0:T(8,128)(2,1)} %copy-done.7, bf16[192,1024]{1,0:T(8,128)(2,1)} %collective-permute-done.15.second), custom_call_target="tpu_custom_call" | custom-call | flops 603979776 | bytes 6094848 | tf_op jit(solution)/shard_map/pallas_call | solution.py:476
  269.4 3.8 %shard_map.102 = (bf16[128,3072]{1,0:T(8,128)(2,1)}, bf16[128,2]{1,0:T(8,128)(2,1)}) custom-call(s32[1]{0:T(128)} %bitcast.place_ref, s32[2,128]{1,0:T(2,128)} %bitcast.23, bf16[2,128]{1,0:T(2,128)(2,1)} %bitcast.25, bf16[512,2432]{1,0:T(8,128)(2,1)} %bitcast.16), custom_call_target="tpu_custom_call" | custom-call | flops 805306368 | bytes 3276800 | tf_op jit(solution)/shard_map/pallas_call | solution.py:409
  274.5 4.8 %shard_map.103 = bf16[768,1024]{1,0:T(8,128)(2,1)} custom-call(f32[768,1024]{1,0:T(8,128)} %shard_map.101.total_ref, bf16[384,768]{1,0:T(8,128)(2,1)} %collective-permute-done.18.whole, bf16[192,1024]{1,0:T(8,128)(2,1)} %collective-permute-done.19.first, bf16[192,1024]{1,0:T(8,128)(2,1)} %collective-permute-done.20.second), custom_call_target="tpu_custom_call" | custom-call | flops 603979776 | bytes 6094848 | tf_op jit(solution)/shard_map/pallas_call | solution.py:476
  (60 shorter events, 18.5 us)
Async XLA Ops:
  2.8 12.5 %collective-permute-start.2 = (bf16[144,768]{1,0:T(8,128)(2,1)}, bf16[144,768]{1,0:T(8,128)(2,1)S(1)}, u32[]{:S(2)}, u32[]{:S(2)}) collective-permute-start(bf16[144,768]{1,0:T(8,128)(2,1)} %get-tuple-element.50), channel_id=1, source_target_pairs={{0,3},{1,0},{2,1},{3,2},{4,7},{5,4},{6,5},{7,6},{8,11},{9,8},{10,9... | collective-permute-start | bytes 663560 | tf_op jit(solution)/shard_map/ppermute | solution.py:492
  6.1 9.2 %collective-permute-start.3 = (bf16[144,768]{1,0:T(8,128)(2,1)}, bf16[144,768]{1,0:T(8,128)(2,1)S(1)}, u32[]{:S(2)}, u32[]{:S(2)}) collective-permute-start(bf16[144,768]{1,0:T(8,128)(2,1)} %get-tuple-element.51), channel_id=1, source_target_pairs={{0,2},{1,3},{2,0},{3,1},{4,6},{5,7},{6,4},{7,5},{8,10},{9,11},{10,... | collective-permute-start | bytes 663560 | tf_op jit(solution)/shard_map/ppermute | solution.py:492
  6.6 13.3 %collective-permute-start.4 = (bf16[144,768]{1,0:T(8,128)(2,1)}, bf16[144,768]{1,0:T(8,128)(2,1)S(1)}, u32[]{:S(2)}, u32[]{:S(2)}) collective-permute-start(bf16[144,768]{1,0:T(8,128)(2,1)} %get-tuple-element.52), channel_id=1, source_target_pairs={{0,1},{1,2},{2,3},{3,0},{4,5},{5,6},{6,7},{7,4},{8,9},{9,10},{10,1... | collective-permute-start | bytes 663560 | tf_op jit(solution)/shard_map/ppermute | solution.py:492
  15.3 4.6 %copy-start.8 = (bf16[144,768]{1,0:T(8,128)(2,1)}, bf16[144,768]{1,0:T(8,128)(2,1)S(1)}, u32[]{:S(2)}) copy-start(bf16[144,768]{1,0:T(8,128)(2,1)S(1)} %collective-permute-done.2.s1) | copy-start | bytes 663556
  15.3 4.6 %copy-start.9 = (bf16[144,768]{1,0:T(8,128)(2,1)}, bf16[144,768]{1,0:T(8,128)(2,1)S(1)}, u32[]{:S(2)}) copy-start(bf16[144,768]{1,0:T(8,128)(2,1)S(1)} %collective-permute-done.3.s2) | copy-start | bytes 663556
  24.3 67.3 %all-to-all-start.1 = ((bf16[64,8,2304]{2,1,0:T(8,128)(2,1)}), bf16[64,8,2304]{2,1,0:T(8,128)(2,1)S(1)}, u32[]{:S(2)}, u32[]{:S(2)}) async-start(bf16[64,8,2304]{2,1,0:T(8,128)(2,1)} %bitcast.14), calls=%async_computation.1 | async-start | bytes 4718592 | tf_op jit(solution)/shard_map/all_to_all | solution.py:511
  36.5 37.1 %collective-permute-start.1 = (bf16[768,1024]{1,0:T(8,128)(2,1)}, bf16[768,1024]{1,0:T(8,128)(2,1)}, u32[]{:S(2)}, u32[]{:S(2)}) collective-permute-start(bf16[768,1024]{1,0:T(8,128)(2,1)} %bitcast.27), channel_id=1, source_target_pairs={{0,1},{1,2},{2,3},{3,0},{4,5},{5,6},{6,7},{7,4},{8,9},{9,10},{10,1... | collective-permute-start | bytes 4718600 | tf_op jit(solution)/shard_map/ppermute | solution.py:492
  36.6 37.0 %collective-permute-start = (bf16[768,1024]{1,0:T(8,128)(2,1)}, bf16[768,1024]{1,0:T(8,128)(2,1)}, u32[]{:S(2)}, u32[]{:S(2)}) collective-permute-start(bf16[768,1024]{1,0:T(8,128)(2,1)} %bitcast.28), channel_id=1, source_target_pairs={{0,3},{1,0},{2,1},{3,2},{4,7},{5,4},{6,5},{7,6},{8,11},{9,8},{10,9... | collective-permute-start | bytes 4718600 | tf_op jit(solution)/shard_map/ppermute | solution.py:492
  91.7 1.4 copy-start.2
  93.1 64.3 %all-to-all-start = ((bf16[64,8,2304]{2,1,0:T(8,128)(2,1)}), bf16[64,8,2304]{2,1,0:T(8,128)(2,1)S(1)}, u32[]{:S(2)}, u32[]{:S(2)}) async-start(bf16[64,8,2304]{2,1,0:T(8,128)(2,1)} %bitcast.13), calls=%async_computation | async-start | bytes 4718592 | tf_op jit(solution)/shard_map/all_to_all | solution.py:511
  103.5 36.4 %collective-permute-start.8 = (bf16[384,1024]{1,0:T(8,128)(2,1)}, bf16[384,1024]{1,0:T(8,128)(2,1)}, u32[]{:S(2)}, u32[]{:S(2)}) collective-permute-start(bf16[384,1024]{1,0:T(8,128)(2,1)} %slice.18), channel_id=1, source_target_pairs={{0,1},{1,2},{2,3},{3,0},{4,5},{5,6},{6,7},{7,4},{8,9},{9,10},{10,1... | collective-permute-start | bytes 2359304 | tf_op jit(solution)/shard_map/ppermute | solution.py:492
  103.5 36.4 %collective-permute-start.9 = (bf16[384,1024]{1,0:T(8,128)(2,1)S(1)}, bf16[384,1024]{1,0:T(8,128)(2,1)}, u32[]{:S(2)}, u32[]{:S(2)}) collective-permute-start(bf16[384,1024]{1,0:T(8,128)(2,1)S(1)} %slice.19), channel_id=1, source_target_pairs={{0,3},{1,0},{2,1},{3,2},{4,7},{5,4},{6,5},{7,6},{8,11},{9,8},{10,9... | collective-permute-start | bytes 2359304 | tf_op jit(solution)/shard_map/ppermute | solution.py:492
  113.6 26.4 %collective-permute-start.5 = (bf16[384,1024]{1,0:T(8,128)(2,1)}, bf16[384,1024]{1,0:T(8,128)(2,1)S(1)}, u32[]{:S(2)}, u32[]{:S(2)}) collective-permute-start(bf16[384,1024]{1,0:T(8,128)(2,1)} %get-tuple-element.54), channel_id=1, source_target_pairs={{0,3},{1,0},{2,1},{3,2},{4,7},{5,4},{6,5},{7,6},{8,11},{9,8},{10,9... | collective-permute-start | bytes 2359304 | tf_op jit(solution)/shard_map/ppermute | solution.py:492
  113.6 26.4 %collective-permute-start.6 = (bf16[384,1024]{1,0:T(8,128)(2,1)}, bf16[384,1024]{1,0:T(8,128)(2,1)S(1)}, u32[]{:S(2)}, u32[]{:S(2)}) collective-permute-start(bf16[384,1024]{1,0:T(8,128)(2,1)} %get-tuple-element.55), channel_id=1, source_target_pairs={{0,2},{1,3},{2,0},{3,1},{4,6},{5,7},{6,4},{7,5},{8,10},{9,11},{10,... | collective-permute-start | bytes 2359304 | tf_op jit(solution)/shard_map/ppermute | solution.py:492
  114.1 43.3 %collective-permute-start.7 = (bf16[384,1024]{1,0:T(8,128)(2,1)}, bf16[384,1024]{1,0:T(8,128)(2,1)}, u32[]{:S(2)}, u32[]{:S(2)}) collective-permute-start(bf16[384,1024]{1,0:T(8,128)(2,1)} %get-tuple-element.56), channel_id=1, source_target_pairs={{0,1},{1,2},{2,3},{3,0},{4,5},{5,6},{6,7},{7,4},{8,9},{9,10},{10,1... | collective-permute-start | bytes 2359304 | tf_op jit(solution)/shard_map/ppermute | solution.py:492
  140.0 0.9 copy-start.11
  157.4 1.4 copy-start.1
  162.1 21.2 %collective-permute-start.11 = (bf16[384,768]{1,0:T(8,128)(2,1)}, bf16[384,768]{1,0:T(8,128)(2,1)}, u32[]{:S(2)}, u32[]{:S(2)}) collective-permute-start(bf16[384,768]{1,0:T(8,128)(2,1)} %get-tuple-element.62.x1), channel_id=1, source_target_pairs={{0,1},{1,2},{2,3},{3,0},{4,5},{5,6},{6,7},{7,4},{8,9},{9,10},{10,1... | collective-permute-start | bytes 1769480 | tf_op jit(solution)/shard_map/ppermute | solution.py:492
  163.3 20.1 %collective-permute-start.10 = (bf16[384,768]{1,0:T(8,128)(2,1)}, bf16[384,768]{1,0:T(8,128)(2,1)}, u32[]{:S(2)}, u32[]{:S(2)}) collective-permute-start(bf16[384,768]{1,0:T(8,128)(2,1)} %get-tuple-element.64.x3), channel_id=1, source_target_pairs={{0,3},{1,0},{2,1},{3,2},{4,7},{5,4},{6,5},{7,6},{8,11},{9,8},{10,9... | collective-permute-start | bytes 1769480 | tf_op jit(solution)/shard_map/ppermute | solution.py:492
  183.4 84.5 %all-to-all-start.2 = ((bf16[64,8,2432]{2,1,0:T(8,128)(2,1)}), bf16[64,8,2432]{2,1,0:T(8,128)(2,1)S(1)}, u32[]{:S(2)}, u32[]{:S(2)}) async-start(bf16[64,8,2432]{2,1,0:T(8,128)(2,1)} %bitcast.15), calls=%async_computation.2 | async-start | bytes 4980736 | tf_op jit(solution)/shard_map/all_to_all | solution.py:511
  195.2 20.2 %collective-permute-start.13 = (bf16[384,1024]{1,0:T(8,128)(2,1)}, bf16[384,1024]{1,0:T(8,128)(2,1)S(1)}, u32[]{:S(2)}, u32[]{:S(2)}) collective-permute-start(bf16[384,1024]{1,0:T(8,128)(2,1)} %get-tuple-element.76.l0), channel_id=1, source_target_pairs={{0,1},{1,2},{2,3},{3,0},{4,5},{5,6},{6,7},{7,4},{8,9},{9,10},{10,1... | collective-permute-start | bytes 2359304 | tf_op jit(solution)/shard_map/ppermute | solution.py:492
  195.3 20.9 %collective-permute-start.12 = (bf16[384,1024]{1,0:T(8,128)(2,1)}, bf16[384,1024]{1,0:T(8,128)(2,1)S(1)}, u32[]{:S(2)}, u32[]{:S(2)}) collective-permute-start(bf16[384,1024]{1,0:T(8,128)(2,1)} %get-tuple-element.76.l0), channel_id=1, source_target_pairs={{0,3},{1,0},{2,1},{3,2},{4,7},{5,4},{6,5},{7,6},{8,11},{9,8},{10,9... | collective-permute-start | bytes 2359304 | tf_op jit(solution)/shard_map/ppermute | solution.py:492
  198.0 34.3 %collective-permute-start.17 = (bf16[384,1024]{1,0:T(8,128)(2,1)}, bf16[384,1024]{1,0:T(8,128)(2,1)S(1)}, u32[]{:S(2)}, u32[]{:S(2)}) collective-permute-start(bf16[384,1024]{1,0:T(8,128)(2,1)} %get-tuple-element.83.r0), channel_id=1, source_target_pairs={{0,1},{1,2},{2,3},{3,0},{4,5},{5,6},{6,7},{7,4},{8,9},{9,10},{10,1... | collective-permute-start | bytes 2359304 | tf_op jit(solution)/shard_map/ppermute | solution.py:492
  198.0 35.9 %collective-permute-start.16 = (bf16[384,1024]{1,0:T(8,128)(2,1)}, bf16[384,1024]{1,0:T(8,128)(2,1)S(1)}, u32[]{:S(2)}, u32[]{:S(2)}) collective-permute-start(bf16[384,1024]{1,0:T(8,128)(2,1)} %get-tuple-element.83.r0), channel_id=1, source_target_pairs={{0,3},{1,0},{2,1},{3,2},{4,7},{5,4},{6,5},{7,6},{8,11},{9,8},{10,9... | collective-permute-start | bytes 2359304 | tf_op jit(solution)/shard_map/ppermute | solution.py:492
  200.7 73.9 %collective-permute-start.18 = (bf16[384,768]{1,0:T(8,128)(2,1)}, bf16[384,768]{1,0:T(8,128)(2,1)}, u32[]{:S(2)}, u32[]{:S(2)}) collective-permute-start(bf16[384,768]{1,0:T(8,128)(2,1)} %get-tuple-element.63.x2), channel_id=1, source_target_pairs={{0,2},{1,3},{2,0},{3,1},{4,6},{5,7},{6,4},{7,5},{8,10},{9,11},{10,... | collective-permute-start | bytes 1769480 | tf_op jit(solution)/shard_map/ppermute | solution.py:492
  215.4 39.6 %copy-start.3 = (bf16[384,1024]{1,0:T(8,128)(2,1)}, bf16[384,1024]{1,0:T(8,128)(2,1)S(1)}, u32[]{:S(2)}) copy-start(bf16[384,1024]{1,0:T(8,128)(2,1)S(1)} %collective-permute-done.13.l3) | copy-start | bytes 2359300
  216.3 45.9 %collective-permute-start.14 = (bf16[192,1024]{1,0:T(8,128)(2,1)}, bf16[192,1024]{1,0:T(8,128)(2,1)S(1)}, u32[]{:S(2)}, u32[]{:S(2)}) collective-permute-start(bf16[192,1024]{1,0:T(8,128)(2,1)} %slice.24), channel_id=1, source_target_pairs={{0,1},{1,2},{2,3},{3,0},{4,5},{5,6},{6,7},{7,4},{8,9},{9,10},{10,1... | collective-permute-start | bytes 1179656 | tf_op jit(solution)/shard_map/ppermute | solution.py:492
  216.3 0.9 copy-start.4
  217.9 44.2 %collective-permute-start.15 = (bf16[192,1024]{1,0:T(8,128)(2,1)}, bf16[192,1024]{1,0:T(8,128)(2,1)}, u32[]{:S(2)}, u32[]{:S(2)}) collective-permute-start(bf16[192,1024]{1,0:T(8,128)(2,1)} %slice.25), channel_id=1, source_target_pairs={{0,3},{1,0},{2,1},{3,2},{4,7},{5,4},{6,5},{7,6},{8,11},{9,8},{10,9... | collective-permute-start | bytes 1179656 | tf_op jit(solution)/shard_map/ppermute | solution.py:492
  233.9 40.6 %collective-permute-start.19 = (bf16[192,1024]{1,0:T(8,128)(2,1)}, bf16[192,1024]{1,0:T(8,128)(2,1)}, u32[]{:S(2)}, u32[]{:S(2)}) collective-permute-start(bf16[192,1024]{1,0:T(8,128)(2,1)} %slice.26), channel_id=1, source_target_pairs={{0,1},{1,2},{2,3},{3,0},{4,5},{5,6},{6,7},{7,4},{8,9},{9,10},{10,1... | collective-permute-start | bytes 1179656 | tf_op jit(solution)/shard_map/ppermute | solution.py:492
  235.6 39.0 %collective-permute-start.20 = (bf16[192,1024]{1,0:T(8,128)(2,1)}, bf16[192,1024]{1,0:T(8,128)(2,1)}, u32[]{:S(2)}, u32[]{:S(2)}) collective-permute-start(bf16[192,1024]{1,0:T(8,128)(2,1)} %slice.27), channel_id=1, source_target_pairs={{0,3},{1,0},{2,1},{3,2},{4,7},{5,4},{6,5},{7,6},{8,11},{9,8},{10,9... | collective-permute-start | bytes 1179656 | tf_op jit(solution)/shard_map/ppermute | solution.py:492
  267.9 1.4 copy-start
  (5 other events, 4.1 us)

commit v2 on v1

--- a/solution.py
+++ b/solution.py
@@ -11,7 +11,12 @@
 ROWS = 8
 F32 = jnp.float32
 BF16 = jnp.bfloat16
-VMEM = pltpu.CompilerParams(vmem_limit_bytes=60 * 1024 * 1024)
+
+
+def vmem(mebibytes):
+    return pltpu.CompilerParams(vmem_limit_bytes=mebibytes * 1024 * 1024)
+
+
 NT = (((1,), (1,)), ((), ()))
 TN = (((0,), (0,)), ((), ()))
 
@@ -91,13 +96,13 @@
     count, width = values.shape
     rows_all = experts * ROWS
     packed = 3 * width // 4
-    vmem = pl.BlockSpec(memory_space=pltpu.VMEM)
+    spec = pl.BlockSpec(memory_space=pltpu.VMEM)
     return pl.pallas_call(
         token_body,
         out_shape=jax.ShapeDtypeStruct((rows_all, packed), BF16),
-        in_specs=[pl.BlockSpec(memory_space=pltpu.SMEM), vmem, vmem],
-        out_specs=vmem,
-        compiler_params=VMEM,
+        in_specs=[pl.BlockSpec(memory_space=pltpu.SMEM), spec, spec],
+        out_specs=spec,
+        compiler_params=vmem(60),
         cost_estimate=pl.CostEstimate(
             flops=4 * rows_all * count * packed,
             bytes_accessed=2 * (count * width + rows_all * packed),
@@ -125,13 +130,13 @@
 
 def slices(place, ids, weight, values):
     count, width = values.shape
-    vmem = pl.BlockSpec(memory_space=pltpu.VMEM)
+    spec = pl.BlockSpec(memory_space=pltpu.VMEM)
     return pl.pallas_call(
         slice_body,
         out_shape=[jax.ShapeDtypeStruct((count + NOTES, width // 4), BF16)] * 4,
-        in_specs=[pl.BlockSpec(memory_space=pltpu.SMEM), vmem, vmem, vmem],
-        out_specs=[vmem] * 4,
-        compiler_params=VMEM,
+        in_specs=[pl.BlockSpec(memory_space=pltpu.SMEM), spec, spec, spec],
+        out_specs=[spec] * 4,
+        compiler_params=vmem(60),
         cost_estimate=pl.CostEstimate(
             flops=0, bytes_accessed=4 * count * width, transcendentals=0
         ),
@@ -156,13 +161,13 @@
 def dispatch_grads(parts, experts):
     count, block = parts[0].shape
     rows_all = experts * ROWS
-    vmem = pl.BlockSpec(memory_space=pltpu.VMEM)
+    spec = pl.BlockSpec(memory_space=pltpu.VMEM)
     return pl.pallas_call(
         grad_body,
         out_shape=jax.ShapeDtypeStruct((rows_all, 3 * block), BF16),
-        in_specs=[vmem] * 4,
-        out_specs=vmem,
-        compiler_params=VMEM,
+        in_specs=[spec] * 4,
+        out_specs=spec,
+        compiler_params=vmem(60),
         cost_estimate=pl.CostEstimate(
             flops=12 * rows_all * count * block,
             bytes_accessed=2 * (4 * count + 3 * rows_all) * block,
@@ -243,7 +248,7 @@
         + [jax.ShapeDtypeStruct((rows, hidden_width), BF16)] * 3,
         in_specs=[pl.BlockSpec(memory_space=pltpu.VMEM)] * 2,
         out_specs=[pl.BlockSpec(memory_space=pltpu.VMEM)] * 8,
-        compiler_params=VMEM,
+        compiler_params=vmem(60),
         cost_estimate=pl.CostEstimate(
             flops=10 * rows * block * hidden_width,
             bytes_accessed=12 * rows * (block + hidden_width),
@@ -266,7 +271,7 @@
         out_shape=[jax.ShapeDtypeStruct((rows_all // ROWS * CAP, block), BF16)] * 4,
         in_specs=[pl.BlockSpec((size * ROWS, packed), lambda i: (i, 0))],
         out_specs=[pl.BlockSpec((size * CAP, block), lambda i: (i, 0))] * 4,
-        compiler_params=VMEM,
+        compiler_params=vmem(12),
         cost_estimate=pl.CostEstimate(
             flops=12 * rows_all * size * CAP * block,
             bytes_accessed=4 * rows_all * packed,
@@ -276,30 +281,36 @@
 
 
 def expert_body(
-    x0, x1, x2, x3, b0, b1, b2, b3, up0, up1, up2a, up2b, up3,
-    hidden_ref, hgrad_ref, ret_ref, w0, w1, w2, w3, p0, p1, p2, p3, sems,
+    x0, x1, x2, x3, up0, up1, up2a, up2b, up3, b0, b1, b2, b3,
+    hidden_out, hgrad_out, ret_out,
+    w0, w1, w2, w3, p0, p1, p2, p3, hidden_ref, hgrad_ref, ret_ref, in_sems, row_sems, ret_sems,
 ):
     rows, hidden_width = hidden_ref.shape
     block = w0.shape[0]
     half = block // 2
     step = min(256, hidden_width)
+    steps = hidden_width // step
     sources = (up0, up1, up2a, up2b, up3, b0, b1, b2, b3)
     places = (w0, w1, w2.at[:half, :], w2.at[half:, :], w3, p0, p1, p2, p3)
-    copies = []
-    for j in range(hidden_width // step):
+
+    def fetch(j):
         at = slice(j * step, (j + 1) * step)
-        copies.append(
-            [
-                pltpu.make_async_copy(source.at[:, at], target.at[:, at], sems.at[p, j])
-                for p, (source, target) in enumerate(zip(sources, places))
-            ]
-        )
-        for copy in copies[-1]:
+        group = [
+            pltpu.make_async_copy(source.at[:, at], place.at[:, at], in_sems.at[p, j])
+            for p, (source, place) in enumerate(zip(sources, places))
+        ]
+        for copy in group:
             copy.start()
+        return group
+
+    fetched = [fetch(0)]
+    leaving = []
     score = jnp.zeros((rows, 1), F32)
-    for j, group in enumerate(copies):
+    for j in range(steps):
         at = slice(j * step, (j + 1) * step)
-        for copy in group:
+        if j + 1 < steps:
+            fetched.append(fetch(j + 1))
+        for copy in fetched[j]:
             copy.wait()
         pre_act = dot(x0[...], w0[:, at])
         pre_act += dot(x1[...], w1[:, at])
@@ -312,6 +323,9 @@
         slope = sigmoid_val * (1.0 + pre_act * (1.0 - sigmoid_val))
         hgrad_ref[:, at] = (back * slope).astype(BF16)
         score += jnp.sum(hidden.astype(F32) * back, axis=1, keepdims=True)
+        for k, (ref, out) in enumerate(((hidden_ref, hidden_out), (hgrad_ref, hgrad_out))):
+            leaving.append(pltpu.make_async_copy(ref.at[:, at], out.at[:, at], row_sems.at[k, j]))
+            leaving[-1].start()
 
     size = group_size(ret_ref.shape[0])
     main, rest = packers(size)
@@ -319,6 +333,22 @@
         (slice(g * size * CAP, (g + 1) * size * CAP), slice(g * size * ROWS, (g + 1) * size * ROWS))
         for g in range(rows // (size * CAP))
     ]
+    high = score.astype(BF16)
+    low = (score - high.astype(F32)).astype(BF16)
+    lane = iota((rows, 128), 1)
+    extra = jnp.where(lane == 0, high.astype(F32), jnp.where(lane == 1, low.astype(F32), 0.0))
+    extra = extra.astype(BF16)
+    for source, target in groups:
+        ret_ref[target, 3 * block :] = dot(main, extra[source]).astype(BF16)
+
+    def leave(start, width, at):
+        copy = pltpu.make_async_copy(
+            ret_ref.at[:, start : start + width], ret_out.at[:, start : start + width], ret_sems.at[at]
+        )
+        copy.start()
+        leaving.append(copy)
+
+    leave(3 * block, 128, 0)
     whole = hgrad_ref[...]
     chunk = min(256, block)
     for n in range(block // chunk):
@@ -331,36 +361,40 @@
                 ret_ref[target, start : start + chunk] = (
                     dot(main, here[source]) + dot(rest[part], last[source])
                 ).astype(BF16)
-    high = score.astype(BF16)
-    low = (score - high.astype(F32)).astype(BF16)
-    lane = iota((rows, 128), 1)
-    extra = jnp.where(lane == 0, high.astype(F32), jnp.where(lane == 1, low.astype(F32), 0.0))
-    extra = extra.astype(BF16)
-    for source, target in groups:
-        ret_ref[target, 3 * block :] = dot(main, extra[source]).astype(BF16)
+            leave(start, chunk, 1 + 3 * n + part)
+    for copy in leaving:
+        copy.wait()
 
 
 def expert(wholes, ups, backs, experts):
     rows, block = wholes[0].shape
     hidden_width = ups[0].shape[1]
-    vmem = pl.BlockSpec(memory_space=pltpu.VMEM)
+    packed = (experts * ROWS, 3 * block + 128)
+    steps, chunks = hidden_width // min(256, hidden_width), block // min(256, block)
+    spec = pl.BlockSpec(memory_space=pltpu.VMEM)
+    anywhere = pl.BlockSpec(memory_space=pl.ANY)
     return pl.pallas_call(
         expert_body,
         out_shape=[jax.ShapeDtypeStruct((rows, hidden_width), BF16)] * 2
-        + [jax.ShapeDtypeStruct((experts * ROWS, 3 * block + 128), BF16)],
-        in_specs=[vmem] * 4 + [pl.BlockSpec(memory_space=pl.ANY)] * 9,
-        out_specs=[vmem] * 3,
+        + [jax.ShapeDtypeStruct(packed, BF16)],
+        in_specs=[spec] * 4 + [anywhere] * 9,
+        out_specs=[anywhere] * 3,
         scratch_shapes=[pltpu.VMEM((block, hidden_width), BF16)] * 4
         + [pltpu.VMEM((rows, hidden_width), F32)]
-        + [pltpu.VMEM((rows, hidden_width), BF16)] * 3
-        + [pltpu.SemaphoreType.DMA((9, hidden_width // min(256, hidden_width)))],
-        compiler_params=VMEM,
+        + [pltpu.VMEM((rows, hidden_width), BF16)] * 5
+        + [pltpu.VMEM(packed, BF16)]
+        + [
+            pltpu.SemaphoreType.DMA((9, steps)),
+            pltpu.SemaphoreType.DMA((2, steps)),
+            pltpu.SemaphoreType.DMA((1 + 3 * chunks,)),
+        ],
+        compiler_params=vmem(60),
         cost_estimate=pl.CostEstimate(
             flops=20 * rows * block * hidden_width,
             bytes_accessed=24 * block * hidden_width,
             transcendentals=rows * hidden_width,
         ),
-    )(*wholes, *backs, *ups)
+    )(*wholes, *ups, *backs)
 
 
 def combine_body(place_ref, ids_ref, weight_ref, ret_ref, dtok_ref, droute_ref):
@@ -405,16 +439,16 @@
 
 
 def combine(place, ids, weight, ret, count, width):
-    vmem = pl.BlockSpec(memory_space=pltpu.VMEM)
+    spec = pl.BlockSpec(memory_space=pltpu.VMEM)
     return pl.pallas_call(
         combine_body,
         out_shape=[
             jax.ShapeDtypeStruct((count, width), BF16),
             jax.ShapeDtypeStruct((count, 2), BF16),
         ],
-        in_specs=[pl.BlockSpec(memory_space=pltpu.SMEM), vmem, vmem, vmem],
-        out_specs=[vmem, vmem],
-        compiler_params=VMEM,
+        in_specs=[pl.BlockSpec(memory_space=pltpu.SMEM), spec, spec, spec],
+        out_specs=[spec, spec],
+        compiler_params=vmem(20),
         cost_estimate=pl.CostEstimate(
             flops=4 * ret.shape[0] * count * width,
             bytes_accessed=2 * (count * width + ret.size),
@@ -444,7 +478,7 @@
         out_shape=jax.ShapeDtypeStruct(shape, F32),
         in_specs=[pl.BlockSpec(memory_space=pltpu.VMEM)] * 6,
         out_specs=pl.BlockSpec(memory_space=pltpu.VMEM),
-        compiler_params=VMEM,
+        compiler_params=vmem(16),
         cost_estimate=pl.CostEstimate(
             flops=6 * rows * shape[0] * shape[1],
             bytes_accessed=6 * rows * sum(shape) + 4 * shape[0] * shape[1],
@@ -478,7 +512,7 @@
         out_shape=jax.ShapeDtypeStruct(total.shape, BF16),
         in_specs=[pl.BlockSpec(memory_space=pltpu.VMEM)] * 4,
         out_specs=pl.BlockSpec(memory_space=pltpu.VMEM),
-        compiler_params=VMEM,
+        compiler_params=vmem(16),
         cost_estimate=pl.CostEstimate(
             flops=2 * whole.shape[0] * total.shape[0] * total.shape[1],
             bytes_accessed=6 * total.size + 2 * whole.shape[0] * sum(total.shape),
@@ -534,9 +568,10 @@
     ret, t1, t3 = lax.optimization_barrier((ret, t1, t3))
     back = exchange(ret, experts)
     h0, h1, h2a, h2b, h3 = far(near(hidden))
-    d0, d1, d2a, d2b, d3 = far(near(hidden_grad))
+    down_near = outer_near((h0, h1, h3), (g0, g1, g3))
     t2 = shift(wholes[2], 2)
-    down_near = outer_near((h0, h1, h3), (g0, g1, g3))
+    grads_near, down_near = lax.optimization_barrier((near(hidden_grad), down_near))
+    d0, d1, d2a, d2b, d3 = far(grads_near)
     up_near = outer_near((wholes[0], t1, t3), (d0, d1, d3))
     grad_down = outer_last(True, down_near, g2, h2a, h2b)
     back, grad_down, up_near = lax.optimization_barrier((back, grad_down, up_near))

time: 284 us -> 267 us (0.940); the launches traced: 279 us -> 265 us
  Pallas kernels: 64.9 us -> 51.5 us
  local copies, waits for them, and re-layouts: 17.9 us -> 14.1 us
    pallas_call x2, Pallas kernels: 13.9 us -> 6.27 us  [outer_near(): pl.pallas_call(near_body, out_shape=jax.ShapeDtypeStruct(shape, F32), in_...]
    pallas_call x2, Pallas kernels: 9.8 us -> 6.49 us  [outer_last(): pl.pallas_call(functools.partial(last_body, left_in_halves), out_shape=ja...]
    unnamed x27 -> x51, local copies, waits for them, and re-layouts: 11.5 us -> 9.25 us
  transfers between devices with their start and end apart: 24 -> 24, of which waited for: 9 -> 10; matrix products, arithmetic and copies ran while one was open for 3% -> 2% of each run, Pallas kernels for 18% -> 15%
where the time goes in v2:
time: 267 us; the launch traced here: 265 us
  waiting for transfers between devices  130 us (49%)
  starting transfers between devices  69.1 us (26%)
  Pallas kernels  51.5 us (19%)
  local copies, waits for them, and re-layouts  14.1 us (5%)
    ppermute x21, waiting for transfers between devices, shift(): lax.ppermute(values, 'cross', [(i, (i + by) % count) for i in range(count)])  112 us
    ppermute x21, starting transfers between devices, shift(): lax.ppermute(values, 'cross', [(i, (i + by) % count) for i in range(count)])  37.5 us
    all_to_all x3, starting transfers between devices, exchange(): lax.all_to_all(blocks, 'expert', split_axis=0, concat_axis=0, tiled=True)  31.6 us
    all_to_all x3, waiting for transfers between devices, exchange(): lax.all_to_all(blocks, 'expert', split_axis=0, concat_axis=0, tiled=True)  18 us
    pallas_call x1, Pallas kernels, expert(): pl.pallas_call(expert_body, out_shape=[jax.ShapeDtypeStruct((rows, hidden...  16.8 us
    unnamed x51, local copies, waits for them, and re-layouts  9.25 us
    pallas_call x1, Pallas kernels, project(): pl.pallas_call(project_body, out_shape=[jax.ShapeDtypeStruct((rows, block...  7.29 us
    pallas_call x2, Pallas kernels, outer_last(): pl.pallas_call(functools.partial(last_body, left_in_halves), out_shape=ja...  6.49 us
  transfers between devices with their start and end apart: 24, of which 10 were waited for; matrix products, arithmetic and copies ran while one was open for 2% of the time, Pallas kernels for 15%

profile of v2, /device:TPU:1, one launch (start us, length us, event | category | flops | bytes accessed | tf_op | source)
XLA Modules:
  0.0 265.2 jit_solution(1136288475719384557)
XLA Ops:
  0.6 2.1 shard_map.94
  2.8 3.3 %collective-permute-start.2 = (bf16[144,768]{1,0:T(8,128)(2,1)}, bf16[144,768]{1,0:T(8,128)(2,1)S(1)}, u32[]{:S(2)}, u32[]{:S(2)}) collective-permute-start(bf16[144,768]{1,0:T(8,128)(2,1)} %get-tuple-element.54), channel_id=1, source_target_pairs={{0,3},{1,0},{2,1},{3,2},{4,7},{5,4},{6,5},{7,6},{8,11},{9,8},{10,9... | collective-permute-start | bytes 663560 | tf_op jit(solution)/shard_map/ppermute | solution.py:526
  7.2 8.1 %collective-permute-done.2.s1 = bf16[144,768]{1,0:T(8,128)(2,1)S(1)} collective-permute-done((bf16[144,768]{1,0:T(8,128)(2,1)}, bf16[144,768]{1,0:T(8,128)(2,1)S(1)}, u32[]{:S(2)}, u32[]{:S(2)}) %collective-permute-start.2) | collective-permute-done | bytes 221216 | tf_op jit(solution)/shard_map/ppermute | solution.py:526
  15.3 4.6 %collective-permute-done.4.s3 = bf16[144,768]{1,0:T(8,128)(2,1)S(1)} collective-permute-done((bf16[144,768]{1,0:T(8,128)(2,1)}, bf16[144,768]{1,0:T(8,128)(2,1)S(1)}, u32[]{:S(2)}, u32[]{:S(2)}) %collective-permute-start.4) | collective-permute-done | bytes 221216 | tf_op jit(solution)/shard_map/ppermute | solution.py:526
  20.6 3.7 %shard_map.95 = bf16[512,2304]{1,0:T(8,128)(2,1)} custom-call(bf16[144,768]{1,0:T(8,128)(2,1)} %get-tuple-element.53.s0, bf16[144,768]{1,0:T(8,128)(2,1)} %copy-done.20, bf16[144,768]{1,0:T(8,128)(2,1)} %copy-done.21, bf16[144,768]{1,0:T(8,128)(2,1)} %copy-done.22), custom_call_target="tpu_custom_call" | custom-call | flops 679477248 | bytes 3244032 | tf_op jit(solution)/shard_map/pallas_call | solution.py:165
  24.3 12.1 %all-to-all-start.1 = ((bf16[64,8,2304]{2,1,0:T(8,128)(2,1)}), bf16[64,8,2304]{2,1,0:T(8,128)(2,1)S(1)}, u32[]{:S(2)}, u32[]{:S(2)}) async-start(bf16[64,8,2304]{2,1,0:T(8,128)(2,1)} %bitcast.20), calls=%async_computation.1 | async-start | bytes 4718592 | tf_op jit(solution)/shard_map/all_to_all | solution.py:545
  36.6 2.7 %collective-permute-start = (bf16[768,1024]{1,0:T(8,128)(2,1)}, bf16[768,1024]{1,0:T(8,128)(2,1)}, u32[]{:S(2)}, u32[]{:S(2)}) collective-permute-start(bf16[768,1024]{1,0:T(8,128)(2,1)} %bitcast.27), channel_id=1, source_target_pairs={{0,3},{1,0},{2,1},{3,2},{4,7},{5,4},{6,5},{7,6},{8,11},{9,8},{10,9... | collective-permute-start | bytes 4718600 | tf_op jit(solution)/shard_map/ppermute | solution.py:526
  39.2 3.7 %shard_map.93 = bf16[512,2304]{1,0:T(8,128)(2,1)} custom-call(s32[1]{0:T(128)} %bitcast.place_ref, s32[2,128]{1,0:T(2,128)} %bitcast.15, bf16[128,3072]{1,0:T(8,128)(2,1)} %values_ref.2), custom_call_target="tpu_custom_call" | custom-call | flops 603979776 | bytes 3145728 | tf_op jit(solution)/shard_map/pallas_call | solution.py:100
  42.9 30.7 %collective-permute-done.1.up3 = bf16[768,1024]{1,0:T(8,128)(2,1)} collective-permute-done((bf16[768,1024]{1,0:T(8,128)(2,1)}, bf16[768,1024]{1,0:T(8,128)(2,1)}, u32[]{:S(2)}, u32[]{:S(2)}) %collective-permute-start.1) | collective-permute-done | bytes 1572896 | tf_op jit(solution)/shard_map/ppermute | solution.py:526
  73.6 18.0 %all-to-all-done.1 = bf16[64,8,2304]{2,1,0:T(8,128)(2,1)S(1)} async-done(((bf16[64,8,2304]{2,1,0:T(8,128)(2,1)}), bf16[64,8,2304]{2,1,0:T(8,128)(2,1)S(1)}, u32[]{:S(2)}, u32[]{:S(2)}) %all-to-all-start.1) | async-done | bytes 2359328 | tf_op jit(solution)/shard_map/all_to_all | solution.py:545
  91.6 1.5 copy-done.19
  93.1 7.1 %all-to-all-start = ((bf16[64,8,2304]{2,1,0:T(8,128)(2,1)}), bf16[64,8,2304]{2,1,0:T(8,128)(2,1)S(1)}, u32[]{:S(2)}, u32[]{:S(2)}) async-start(bf16[64,8,2304]{2,1,0:T(8,128)(2,1)} %bitcast.19), calls=%async_computation | async-start | bytes 4718592 | tf_op jit(solution)/shard_map/all_to_all | solution.py:545
  101.4 2.1 slice.18
  103.5 2.7 %collective-permute-start.9 = (bf16[384,1024]{1,0:T(8,128)(2,1)S(1)}, bf16[384,1024]{1,0:T(8,128)(2,1)}, u32[]{:S(2)}, u32[]{:S(2)}) collective-permute-start(bf16[384,1024]{1,0:T(8,128)(2,1)S(1)} %slice.19), channel_id=1, source_target_pairs={{0,3},{1,0},{2,1},{3,2},{4,7},{5,4},{6,5},{7,6},{8,11},{9,8},{10,9... | collective-permute-start | bytes 2359304 | tf_op jit(solution)/shard_map/ppermute | solution.py:526
  106.2 7.3 %shard_map.96 = (bf16[384,768]{1,0:T(8,128)(2,1)}, bf16[384,768]{1,0:T(8,128)(2,1)}, bf16[384,768]{1,0:T(8,128)(2,1)}, bf16[384,768]{1,0:T(8,128)(2,1)}, f32[384...) custom-call(bf16[512,2304]{1,0:T(8,128)(2,1)} %bitcast.22, ...), custom_call_target="tpu_custom_call" | custom-call | flops 3019898880 | bytes 8257536 | tf_op jit(solution)/shard_map/pallas_call | solution.py:244
  114.9 24.9 %collective-permute-done.8.up2a = bf16[384,1024]{1,0:T(8,128)(2,1)} collective-permute-done((bf16[384,1024]{1,0:T(8,128)(2,1)}, bf16[384,1024]{1,0:T(8,128)(2,1)}, u32[]{:S(2)}, u32[]{:S(2)}) %collective-permute-start.8) | collective-permute-done | bytes 786464 | tf_op jit(solution)/shard_map/ppermute | solution.py:526
  141.7 15.7 %collective-permute-done.7.b3 = bf16[384,1024]{1,0:T(8,128)(2,1)} collective-permute-done((bf16[384,1024]{1,0:T(8,128)(2,1)}, bf16[384,1024]{1,0:T(8,128)(2,1)}, u32[]{:S(2)}, u32[]{:S(2)}) %collective-permute-start.7) | collective-permute-done | bytes 786464 | tf_op jit(solution)/shard_map/ppermute | solution.py:526
  161.6 2.7 %collective-permute-start.10 = (bf16[384,768]{1,0:T(8,128)(2,1)S(1)}, bf16[384,768]{1,0:T(8,128)(2,1)S(1)}, u32[]{:S(2)}, u32[]{:S(2)}) collective-permute-start(bf16[384,768]{1,0:T(8,128)(2,1)S(1)} %get-tuple-element.68.x3), channel_id=1, source_target_pairs={{0,3},{1,0},{2,1},{3,2},{4,7},{5,4},{6,5},{7,6},{8,11},{9,8},{10,9... | collective-permute-start | bytes 1769480 | tf_op jit(solution)/shard_map/ppermute | solution.py:526
  164.3 16.8 %shard_map.98 = (bf16[384,1024]{1,0:T(8,128)(2,1)}, bf16[384,1024]{1,0:T(8,128)(2,1)}, bf16[512,2432]{1,0:T(8,128)(2,1)}) custom-call(bf16[384,768]{1,0:T(8,128)(2,1)} %copy-done.7, bf16[384,768]{1,0:T(8,128)(2,1)} %copy-done.18, bf16[384,768]{1,0:T(8,128)(2,1)} %copy-done.16, bf16[384,768]{1,0:T(8,128)(2,1)} %copy-done.17, bf16[768,1024]{1,0:T(8,128)(2,1)} %bitcast.28, ...), custom_call_target="tpu_custom_call" | custom-call | flops 6039797760 | bytes 18874368 | tf_op jit(solution)/shard_map/pallas_call | solution.py:376
  182.8 12.3 %all-to-all-start.2 = ((bf16[64,8,2432]{2,1,0:T(8,128)(2,1)}), bf16[64,8,2432]{2,1,0:T(8,128)(2,1)}, u32[]{:S(2)}, u32[]{:S(2)}) async-start(bf16[64,8,2432]{2,1,0:T(8,128)(2,1)} %bitcast.21), calls=%async_computation.2 | async-start | bytes 4980736 | tf_op jit(solution)/shard_map/all_to_all | solution.py:545
  195.2 2.7 %collective-permute-start.14 = (bf16[384,1024]{1,0:T(8,128)(2,1)S(1)}, bf16[384,1024]{1,0:T(8,128)(2,1)S(1)}, u32[]{:S(2)}, u32[]{:S(2)}) collective-permute-start(bf16[384,1024]{1,0:T(8,128)(2,1)S(1)} %copy-done.2), channel_id=1, source_target_pairs={{0,3},{1,0},{2,1},{3,2},{4,7},{5,4},{6,5},{7,6},{8,11},{9,8},{10,9... | collective-permute-start | bytes 2359304 | tf_op jit(solution)/shard_map/ppermute | solution.py:526
  197.9 2.7 %collective-permute-start.12 = (bf16[384,1024]{1,0:T(8,128)(2,1)S(1)}, bf16[384,1024]{1,0:T(8,128)(2,1)S(1)}, u32[]{:S(2)}, u32[]{:S(2)}) collective-permute-start(bf16[384,1024]{1,0:T(8,128)(2,1)S(1)} %copy-done), channel_id=1, source_target_pairs={{0,3},{1,0},{2,1},{3,2},{4,7},{5,4},{6,5},{7,6},{8,11},{9,8},{10,9... | collective-permute-start | bytes 2359304 | tf_op jit(solution)/shard_map/ppermute | solution.py:526
  200.6 14.5 %collective-permute-done.15.l3 = bf16[384,1024]{1,0:T(8,128)(2,1)S(1)} collective-permute-done((bf16[384,1024]{1,0:T(8,128)(2,1)S(1)}, bf16[384,1024]{1,0:T(8,128)(2,1)S(1)}, u32[]{:S(2)}, u32[]{:S(2)}) %collective-permute-start.15) | collective-permute-done | bytes 786464 | tf_op jit(solution)/shard_map/ppermute | solution.py:526
  215.3 2.7 %collective-permute-start.17 = (bf16[192,1024]{1,0:T(8,128)(2,1)S(1)}, bf16[192,1024]{1,0:T(8,128)(2,1)S(1)}, u32[]{:S(2)}, u32[]{:S(2)}) collective-permute-start(bf16[192,1024]{1,0:T(8,128)(2,1)S(1)} %slice.25), channel_id=1, source_target_pairs={{0,3},{1,0},{2,1},{3,2},{4,7},{5,4},{6,5},{7,6},{8,11},{9,8},{10,9... | collective-permute-start | bytes 1179656 | tf_op jit(solution)/shard_map/ppermute | solution.py:526
  218.0 3.3 %shard_map.99.total_ref = f32[1024,768]{1,0:T(8,128)S(1)} custom-call(bf16[384,1024]{1,0:T(8,128)(2,1)S(1)} %copy-done.2, bf16[384,1024]{1,0:T(8,128)(2,1)S(1)} %collective-permute-done.14.l1, bf16[384,1024]{1,0:T(8,128)(2,1)S(1)} %collective-permute-done.15.l3, bf16[384,768]{1,0:T(8,128)(2,1)S(1)} %copy-done.4, bf16[384,768]{1,0:T(8,128)(2,1)S(1)} %copy-done.5, ...), custom_call_target="tpu_custom_call" | custom-call | flops 1811939328 | bytes 7274496 | tf_op jit(solution)/shard_map/pallas_call | solution.py:476
  221.3 10.7 %collective-permute-done.13.r3 = bf16[384,1024]{1,0:T(8,128)(2,1)S(1)} collective-permute-done((bf16[384,1024]{1,0:T(8,128)(2,1)S(1)}, bf16[384,1024]{1,0:T(8,128)(2,1)S(1)}, u32[]{:S(2)}, u32[]{:S(2)}) %collective-permute-start.13) | collective-permute-done | bytes 786464 | tf_op jit(solution)/shard_map/ppermute | solution.py:526
  233.5 14.0 %collective-permute-start.20 = (bf16[192,1024]{1,0:T(8,128)(2,1)}, bf16[192,1024]{1,0:T(8,128)(2,1)}, u32[]{:S(2)}, u32[]{:S(2)}) collective-permute-start(bf16[192,1024]{1,0:T(8,128)(2,1)} %slice.23), channel_id=1, source_target_pairs={{0,3},{1,0},{2,1},{3,2},{4,7},{5,4},{6,5},{7,6},{8,11},{9,8},{10,9... | collective-permute-start | bytes 1179656 | tf_op jit(solution)/shard_map/ppermute | solution.py:526
  247.5 3.0 %shard_map.101.total_ref = f32[768,1024]{1,0:T(8,128)S(1)} custom-call(bf16[384,768]{1,0:T(8,128)(2,1)S(1)} %copy-done.8, bf16[384,768]{1,0:T(8,128)(2,1)S(1)} %copy-done.12, bf16[384,768]{1,0:T(8,128)(2,1)S(1)} %copy-done.10, bf16[384,1024]{1,0:T(8,128)(2,1)S(1)} %copy-done.1, bf16[384,1024]{1,0:T(8,128)(2,1)S(1)} %collective-permute-done.12.r1, ...), custom_call_target="tpu_custom_call" | custom-call | flops 1811939328 | bytes 7274496 | tf_op jit(solution)/shard_map/pallas_call | solution.py:476
  250.6 2.4 collective-permute-done.16.first
  252.9 2.8 %shard_map.100 = bf16[1024,768]{1,0:T(8,128)(2,1)} custom-call(f32[1024,768]{1,0:T(8,128)S(1)} %shard_map.99.total_ref, bf16[384,768]{1,0:T(8,128)(2,1)S(1)} %copy-done.3, bf16[192,1024]{1,0:T(8,128)(2,1)S(1)} %collective-permute-done.16.first, bf16[192,1024]{1,0:T(8,128)(2,1)S(1)} %collective-permute-done.17.second), custom_call_target="tpu_custom_call" | custom-call | flops 603979776 | bytes 6094848 | tf_op jit(solution)/shard_map/pallas_call | solution.py:510
  255.7 3.8 %shard_map.102 = (bf16[128,3072]{1,0:T(8,128)(2,1)}, bf16[128,2]{1,0:T(8,128)(2,1)S(1)}) custom-call(s32[1]{0:T(128)} %bitcast.place_ref, s32[2,128]{1,0:T(2,128)S(1)} %bitcast.16, bf16[2,128]{1,0:T(2,128)(2,1)S(1)} %bitcast.18, bf16[512,2432]{1,0:T(8,128)(2,1)} %bitcast.10.ret_ref), custom_call_target="tpu_custom_call" | custom-call | flops 805306368 | bytes 3276800 | tf_op jit(solution)/shard_map/pallas_call | solution.py:443
  261.5 3.7 %shard_map.103 = bf16[768,1024]{1,0:T(8,128)(2,1)} custom-call(f32[768,1024]{1,0:T(8,128)S(1)} %shard_map.101.total_ref, bf16[384,768]{1,0:T(8,128)(2,1)} %collective-permute-done.18.whole, bf16[192,1024]{1,0:T(8,128)(2,1)S(1)} %collective-permute-done.19.first, bf16[192,1024]{1,0:T(8,128)(2,1)} %collective-permute-done.20.second), custom_call_target="tpu_custom_call" | custom-call | flops 603979776 | bytes 6094848 | tf_op jit(solution)/shard_map/pallas_call | solution.py:510
  (84 shorter events, 16.0 us)
Async XLA Ops:
  2.8 12.5 %collective-permute-start.2 = (bf16[144,768]{1,0:T(8,128)(2,1)}, bf16[144,768]{1,0:T(8,128)(2,1)S(1)}, u32[]{:S(2)}, u32[]{:S(2)}) collective-permute-start(bf16[144,768]{1,0:T(8,128)(2,1)} %get-tuple-element.54), channel_id=1, source_target_pairs={{0,3},{1,0},{2,1},{3,2},{4,7},{5,4},{6,5},{7,6},{8,11},{9,8},{10,9... | collective-permute-start | bytes 663560 | tf_op jit(solution)/shard_map/ppermute | solution.py:526
  6.1 9.2 %collective-permute-start.3 = (bf16[144,768]{1,0:T(8,128)(2,1)}, bf16[144,768]{1,0:T(8,128)(2,1)S(1)}, u32[]{:S(2)}, u32[]{:S(2)}) collective-permute-start(bf16[144,768]{1,0:T(8,128)(2,1)} %get-tuple-element.55), channel_id=1, source_target_pairs={{0,2},{1,3},{2,0},{3,1},{4,6},{5,7},{6,4},{7,5},{8,10},{9,11},{10,... | collective-permute-start | bytes 663560 | tf_op jit(solution)/shard_map/ppermute | solution.py:526
  6.6 13.3 %collective-permute-start.4 = (bf16[144,768]{1,0:T(8,128)(2,1)}, bf16[144,768]{1,0:T(8,128)(2,1)S(1)}, u32[]{:S(2)}, u32[]{:S(2)}) collective-permute-start(bf16[144,768]{1,0:T(8,128)(2,1)} %get-tuple-element.56), channel_id=1, source_target_pairs={{0,1},{1,2},{2,3},{3,0},{4,5},{5,6},{6,7},{7,4},{8,9},{9,10},{10,1... | collective-permute-start | bytes 663560 | tf_op jit(solution)/shard_map/ppermute | solution.py:526
  24.3 67.3 %all-to-all-start.1 = ((bf16[64,8,2304]{2,1,0:T(8,128)(2,1)}), bf16[64,8,2304]{2,1,0:T(8,128)(2,1)S(1)}, u32[]{:S(2)}, u32[]{:S(2)}) async-start(bf16[64,8,2304]{2,1,0:T(8,128)(2,1)} %bitcast.20), calls=%async_computation.1 | async-start | bytes 4718592 | tf_op jit(solution)/shard_map/all_to_all | solution.py:545
  36.5 37.1 %collective-permute-start.1 = (bf16[768,1024]{1,0:T(8,128)(2,1)}, bf16[768,1024]{1,0:T(8,128)(2,1)}, u32[]{:S(2)}, u32[]{:S(2)}) collective-permute-start(bf16[768,1024]{1,0:T(8,128)(2,1)} %bitcast.26), channel_id=1, source_target_pairs={{0,1},{1,2},{2,3},{3,0},{4,5},{5,6},{6,7},{7,4},{8,9},{9,10},{10,1... | collective-permute-start | bytes 4718600 | tf_op jit(solution)/shard_map/ppermute | solution.py:526
  36.6 37.0 %collective-permute-start = (bf16[768,1024]{1,0:T(8,128)(2,1)}, bf16[768,1024]{1,0:T(8,128)(2,1)}, u32[]{:S(2)}, u32[]{:S(2)}) collective-permute-start(bf16[768,1024]{1,0:T(8,128)(2,1)} %bitcast.27), channel_id=1, source_target_pairs={{0,3},{1,0},{2,1},{3,2},{4,7},{5,4},{6,5},{7,6},{8,11},{9,8},{10,9... | collective-permute-start | bytes 4718600 | tf_op jit(solution)/shard_map/ppermute | solution.py:526
  93.1 64.3 %all-to-all-start = ((bf16[64,8,2304]{2,1,0:T(8,128)(2,1)}), bf16[64,8,2304]{2,1,0:T(8,128)(2,1)S(1)}, u32[]{:S(2)}, u32[]{:S(2)}) async-start(bf16[64,8,2304]{2,1,0:T(8,128)(2,1)} %bitcast.19), calls=%async_computation | async-start | bytes 4718592 | tf_op jit(solution)/shard_map/all_to_all | solution.py:545
  103.5 36.4 %collective-permute-start.8 = (bf16[384,1024]{1,0:T(8,128)(2,1)}, bf16[384,1024]{1,0:T(8,128)(2,1)}, u32[]{:S(2)}, u32[]{:S(2)}) collective-permute-start(bf16[384,1024]{1,0:T(8,128)(2,1)} %slice.18), channel_id=1, source_target_pairs={{0,1},{1,2},{2,3},{3,0},{4,5},{5,6},{6,7},{7,4},{8,9},{9,10},{10,1... | collective-permute-start | bytes 2359304 | tf_op jit(solution)/shard_map/ppermute | solution.py:526
  103.5 36.4 %collective-permute-start.9 = (bf16[384,1024]{1,0:T(8,128)(2,1)S(1)}, bf16[384,1024]{1,0:T(8,128)(2,1)}, u32[]{:S(2)}, u32[]{:S(2)}) collective-permute-start(bf16[384,1024]{1,0:T(8,128)(2,1)S(1)} %slice.19), channel_id=1, source_target_pairs={{0,3},{1,0},{2,1},{3,2},{4,7},{5,4},{6,5},{7,6},{8,11},{9,8},{10,9... | collective-permute-start | bytes 2359304 | tf_op jit(solution)/shard_map/ppermute | solution.py:526
  113.5 26.5 %collective-permute-start.5 = (bf16[384,1024]{1,0:T(8,128)(2,1)}, bf16[384,1024]{1,0:T(8,128)(2,1)S(1)}, u32[]{:S(2)}, u32[]{:S(2)}) collective-permute-start(bf16[384,1024]{1,0:T(8,128)(2,1)} %get-tuple-element.58), channel_id=1, source_target_pairs={{0,3},{1,0},{2,1},{3,2},{4,7},{5,4},{6,5},{7,6},{8,11},{9,8},{10,9... | collective-permute-start | bytes 2359304 | tf_op jit(solution)/shard_map/ppermute | solution.py:526
  113.5 26.5 %collective-permute-start.6 = (bf16[384,1024]{1,0:T(8,128)(2,1)}, bf16[384,1024]{1,0:T(8,128)(2,1)S(1)}, u32[]{:S(2)}, u32[]{:S(2)}) collective-permute-start(bf16[384,1024]{1,0:T(8,128)(2,1)} %get-tuple-element.59), channel_id=1, source_target_pairs={{0,2},{1,3},{2,0},{3,1},{4,6},{5,7},{6,4},{7,5},{8,10},{9,11},{10,... | collective-permute-start | bytes 2359304 | tf_op jit(solution)/shard_map/ppermute | solution.py:526
  114.1 43.3 %collective-permute-start.7 = (bf16[384,1024]{1,0:T(8,128)(2,1)}, bf16[384,1024]{1,0:T(8,128)(2,1)}, u32[]{:S(2)}, u32[]{:S(2)}) collective-permute-start(bf16[384,1024]{1,0:T(8,128)(2,1)} %get-tuple-element.60), channel_id=1, source_target_pairs={{0,1},{1,2},{2,3},{3,0},{4,5},{5,6},{6,7},{7,4},{8,9},{9,10},{10,1... | collective-permute-start | bytes 2359304 | tf_op jit(solution)/shard_map/ppermute | solution.py:526
  160.4 20.8 %collective-permute-start.11 = (bf16[384,768]{1,0:T(8,128)(2,1)S(1)}, bf16[384,768]{1,0:T(8,128)(2,1)S(1)}, u32[]{:S(2)}, u32[]{:S(2)}) collective-permute-start(bf16[384,768]{1,0:T(8,128)(2,1)S(1)} %get-tuple-element.66.x1), channel_id=1, source_target_pairs={{0,1},{1,2},{2,3},{3,0},{4,5},{5,6},{6,7},{7,4},{8,9},{9,10},{10,1... | collective-permute-start | bytes 1769480 | tf_op jit(solution)/shard_map/ppermute | solution.py:526
  161.6 20.4 %collective-permute-start.10 = (bf16[384,768]{1,0:T(8,128)(2,1)S(1)}, bf16[384,768]{1,0:T(8,128)(2,1)S(1)}, u32[]{:S(2)}, u32[]{:S(2)}) collective-permute-start(bf16[384,768]{1,0:T(8,128)(2,1)S(1)} %get-tuple-element.68.x3), channel_id=1, source_target_pairs={{0,3},{1,0},{2,1},{3,2},{4,7},{5,4},{6,5},{7,6},{8,11},{9,8},{10,9... | collective-permute-start | bytes 1769480 | tf_op jit(solution)/shard_map/ppermute | solution.py:526
  182.8 35.2 %copy-start.4 = (bf16[384,768]{1,0:T(8,128)(2,1)S(1)}, bf16[384,768]{1,0:T(8,128)(2,1)}, u32[]{:S(2)}) copy-start(bf16[384,768]{1,0:T(8,128)(2,1)} %get-tuple-element.82.r0) | copy-start | bytes 1769476
  182.8 35.2 %copy-start.5 = (bf16[384,768]{1,0:T(8,128)(2,1)S(1)}, bf16[384,768]{1,0:T(8,128)(2,1)}, u32[]{:S(2)}) copy-start(bf16[384,768]{1,0:T(8,128)(2,1)} %get-tuple-element.83.r1) | copy-start | bytes 1769476
  182.8 35.2 %copy-start.6 = (bf16[384,768]{1,0:T(8,128)(2,1)S(1)}, bf16[384,768]{1,0:T(8,128)(2,1)}, u32[]{:S(2)}) copy-start(bf16[384,768]{1,0:T(8,128)(2,1)} %get-tuple-element.84.r3) | copy-start | bytes 1769476
  182.8 72.9 %all-to-all-start.2 = ((bf16[64,8,2432]{2,1,0:T(8,128)(2,1)}), bf16[64,8,2432]{2,1,0:T(8,128)(2,1)}, u32[]{:S(2)}, u32[]{:S(2)}) async-start(bf16[64,8,2432]{2,1,0:T(8,128)(2,1)} %bitcast.21), calls=%async_computation.2 | async-start | bytes 4980736 | tf_op jit(solution)/shard_map/all_to_all | solution.py:545
  195.1 20.0 %collective-permute-start.15 = (bf16[384,1024]{1,0:T(8,128)(2,1)S(1)}, bf16[384,1024]{1,0:T(8,128)(2,1)S(1)}, u32[]{:S(2)}, u32[]{:S(2)}) collective-permute-start(bf16[384,1024]{1,0:T(8,128)(2,1)S(1)} %copy-done.2), channel_id=1, source_target_pairs={{0,1},{1,2},{2,3},{3,0},{4,5},{5,6},{6,7},{7,4},{8,9},{9,10},{10,1... | collective-permute-start | bytes 2359304 | tf_op jit(solution)/shard_map/ppermute | solution.py:526
  195.2 20.0 %collective-permute-start.14 = (bf16[384,1024]{1,0:T(8,128)(2,1)S(1)}, bf16[384,1024]{1,0:T(8,128)(2,1)S(1)}, u32[]{:S(2)}, u32[]{:S(2)}) collective-permute-start(bf16[384,1024]{1,0:T(8,128)(2,1)S(1)} %copy-done.2), channel_id=1, source_target_pairs={{0,3},{1,0},{2,1},{3,2},{4,7},{5,4},{6,5},{7,6},{8,11},{9,8},{10,9... | collective-permute-start | bytes 2359304 | tf_op jit(solution)/shard_map/ppermute | solution.py:526
  197.9 34.1 %collective-permute-start.13 = (bf16[384,1024]{1,0:T(8,128)(2,1)S(1)}, bf16[384,1024]{1,0:T(8,128)(2,1)S(1)}, u32[]{:S(2)}, u32[]{:S(2)}) collective-permute-start(bf16[384,1024]{1,0:T(8,128)(2,1)S(1)} %copy-done), channel_id=1, source_target_pairs={{0,1},{1,2},{2,3},{3,0},{4,5},{5,6},{6,7},{7,4},{8,9},{9,10},{10,1... | collective-permute-start | bytes 2359304 | tf_op jit(solution)/shard_map/ppermute | solution.py:526
  197.9 34.1 %collective-permute-start.12 = (bf16[384,1024]{1,0:T(8,128)(2,1)S(1)}, bf16[384,1024]{1,0:T(8,128)(2,1)S(1)}, u32[]{:S(2)}, u32[]{:S(2)}) collective-permute-start(bf16[384,1024]{1,0:T(8,128)(2,1)S(1)} %copy-done), channel_id=1, source_target_pairs={{0,3},{1,0},{2,1},{3,2},{4,7},{5,4},{6,5},{7,6},{8,11},{9,8},{10,9... | collective-permute-start | bytes 2359304 | tf_op jit(solution)/shard_map/ppermute | solution.py:526
  200.6 60.9 %collective-permute-start.18 = (bf16[384,768]{1,0:T(8,128)(2,1)}, bf16[384,768]{1,0:T(8,128)(2,1)}, u32[]{:S(2)}, u32[]{:S(2)}) collective-permute-start(bf16[384,768]{1,0:T(8,128)(2,1)} %copy-done.16), channel_id=1, source_target_pairs={{0,2},{1,3},{2,0},{3,1},{4,6},{5,7},{6,4},{7,5},{8,10},{9,11},{10,... | collective-permute-start | bytes 1769480 | tf_op jit(solution)/shard_map/ppermute | solution.py:526
  215.1 37.8 %collective-permute-start.16 = (bf16[192,1024]{1,0:T(8,128)(2,1)S(1)}, bf16[192,1024]{1,0:T(8,128)(2,1)S(1)}, u32[]{:S(2)}, u32[]{:S(2)}) collective-permute-start(bf16[192,1024]{1,0:T(8,128)(2,1)S(1)} %slice.24), channel_id=1, source_target_pairs={{0,1},{1,2},{2,3},{3,0},{4,5},{5,6},{6,7},{7,4},{8,9},{9,10},{10,1... | collective-permute-start | bytes 1179656 | tf_op jit(solution)/shard_map/ppermute | solution.py:526
  215.3 37.6 %collective-permute-start.17 = (bf16[192,1024]{1,0:T(8,128)(2,1)S(1)}, bf16[192,1024]{1,0:T(8,128)(2,1)S(1)}, u32[]{:S(2)}, u32[]{:S(2)}) collective-permute-start(bf16[192,1024]{1,0:T(8,128)(2,1)S(1)} %slice.25), channel_id=1, source_target_pairs={{0,3},{1,0},{2,1},{3,2},{4,7},{5,4},{6,5},{7,6},{8,11},{9,8},{10,9... | collective-permute-start | bytes 1179656 | tf_op jit(solution)/shard_map/ppermute | solution.py:526
  218.0 29.5 %copy-start.1 = (bf16[384,1024]{1,0:T(8,128)(2,1)S(1)}, bf16[384,1024]{1,0:T(8,128)(2,1)}, u32[]{:S(2)}) copy-start(bf16[384,1024]{1,0:T(8,128)(2,1)} %get-tuple-element.89.r0) | copy-start | bytes 2359300
  218.0 29.5 %copy-start.8 = (bf16[384,768]{1,0:T(8,128)(2,1)S(1)}, bf16[384,768]{1,0:T(8,128)(2,1)}, u32[]{:S(2)}) copy-start(bf16[384,768]{1,0:T(8,128)(2,1)} %copy-done.7) | copy-start | bytes 1769476
  218.0 29.5 %copy-start.10 = (bf16[384,768]{1,0:T(8,128)(2,1)S(1)}, bf16[384,768]{1,0:T(8,128)(2,1)}, u32[]{:S(2)}) copy-start(bf16[384,768]{1,0:T(8,128)(2,1)} %copy-done.9) | copy-start | bytes 1769476
  218.0 29.5 %copy-start.12 = (bf16[384,768]{1,0:T(8,128)(2,1)S(1)}, bf16[384,768]{1,0:T(8,128)(2,1)}, u32[]{:S(2)}) copy-start(bf16[384,768]{1,0:T(8,128)(2,1)} %copy-done.11) | copy-start | bytes 1769476
  233.5 19.4 %copy-start.3 = (bf16[384,768]{1,0:T(8,128)(2,1)S(1)}, bf16[384,768]{1,0:T(8,128)(2,1)}, u32[]{:S(2)}) copy-start(bf16[384,768]{1,0:T(8,128)(2,1)} %get-tuple-element.86.whole) | copy-start | bytes 1769476
  233.5 28.0 %collective-permute-start.19 = (bf16[192,1024]{1,0:T(8,128)(2,1)}, bf16[192,1024]{1,0:T(8,128)(2,1)S(1)}, u32[]{:S(2)}, u32[]{:S(2)}) collective-permute-start(bf16[192,1024]{1,0:T(8,128)(2,1)} %slice.22), channel_id=1, source_target_pairs={{0,1},{1,2},{2,3},{3,0},{4,5},{5,6},{6,7},{7,4},{8,9},{9,10},{10,1... | collective-permute-start | bytes 1179656 | tf_op jit(solution)/shard_map/ppermute | solution.py:526
  233.5 28.0 %collective-permute-start.20 = (bf16[192,1024]{1,0:T(8,128)(2,1)}, bf16[192,1024]{1,0:T(8,128)(2,1)}, u32[]{:S(2)}, u32[]{:S(2)}) collective-permute-start(bf16[192,1024]{1,0:T(8,128)(2,1)} %slice.23), channel_id=1, source_target_pairs={{0,3},{1,0},{2,1},{3,2},{4,7},{5,4},{6,5},{7,6},{8,11},{9,8},{10,9... | collective-permute-start | bytes 1179656 | tf_op jit(solution)/shard_map/ppermute | solution.py:526
  (17 other events, 57.9 us)

commit v3 on v2

--- a/solution.py
+++ b/solution.py
@@ -136,7 +136,7 @@
         out_shape=[jax.ShapeDtypeStruct((count + NOTES, width // 4), BF16)] * 4,
         in_specs=[pl.BlockSpec(memory_space=pltpu.SMEM), spec, spec, spec],
         out_specs=[spec] * 4,
-        compiler_params=vmem(60),
+        compiler_params=vmem(12),
         cost_estimate=pl.CostEstimate(
             flops=0, bytes_accessed=4 * count * width, transcendentals=0
         ),
@@ -167,7 +167,7 @@
         out_shape=jax.ShapeDtypeStruct((rows_all, 3 * block), BF16),
         in_specs=[spec] * 4,
         out_specs=spec,
-        compiler_params=vmem(60),
+        compiler_params=vmem(16),
         cost_estimate=pl.CostEstimate(
             flops=12 * rows_all * count * block,
             bytes_accessed=2 * (4 * count + 3 * rows_all) * block,
@@ -288,7 +288,7 @@
     rows, hidden_width = hidden_ref.shape
     block = w0.shape[0]
     half = block // 2
-    step = min(256, hidden_width)
+    step = min(512, hidden_width)
     steps = hidden_width // step
     sources = (up0, up1, up2a, up2b, up3, b0, b1, b2, b3)
     places = (w0, w1, w2.at[:half, :], w2.at[half:, :], w3, p0, p1, p2, p3)
@@ -350,7 +350,7 @@
 
     leave(3 * block, 128, 0)
     whole = hgrad_ref[...]
-    chunk = min(256, block)
+    chunk = min(768, block)
     for n in range(block // chunk):
         at = slice(n * chunk, (n + 1) * chunk)
         last = dot(whole, w3[at, :], NT).astype(BF16)
@@ -370,7 +370,7 @@
     rows, block = wholes[0].shape
     hidden_width = ups[0].shape[1]
     packed = (experts * ROWS, 3 * block + 128)
-    steps, chunks = hidden_width // min(256, hidden_width), block // min(256, block)
+    steps, chunks = hidden_width // min(512, hidden_width), block // min(768, block)
     spec = pl.BlockSpec(memory_space=pltpu.VMEM)
     anywhere = pl.BlockSpec(memory_space=pl.ANY)
     return pl.pallas_call(
@@ -429,13 +429,11 @@
         last += dot(pick, got)
     put(3, last)
     extra = ret_ref[:, 3 * block :]
-    lane = iota((count, 2), 1)
-    out = jnp.zeros((count, 2), F32)
     for k in range(2):
         pair = dot(hits[k], extra)
-        value = (pair[:, 0:1] + pair[:, 1:2]) / col(weight_ref[k : k + 1, :].astype(F32))
-        out = jnp.where(lane == k, value, out)
-    droute_ref[...] = out.astype(BF16)
+        score = pair[:, 0:1] + pair[:, 1:2]
+        row = jnp.sum(jnp.where(eye, score, 0.0), axis=0, keepdims=True)
+        droute_ref[k : k + 1, :] = (row / weight_ref[k : k + 1, :].astype(F32)).astype(BF16)
 
 
 def combine(place, ids, weight, ret, count, width):
@@ -444,7 +442,7 @@
         combine_body,
         out_shape=[
             jax.ShapeDtypeStruct((count, width), BF16),
-            jax.ShapeDtypeStruct((count, 2), BF16),
+            jax.ShapeDtypeStruct((2, count), BF16),
         ],
         in_specs=[pl.BlockSpec(memory_space=pltpu.SMEM), spec, spec, spec],
         out_specs=[spec, spec],
@@ -569,8 +567,10 @@
     back = exchange(ret, experts)
     h0, h1, h2a, h2b, h3 = far(near(hidden))
     down_near = outer_near((h0, h1, h3), (g0, g1, g3))
-    t2 = shift(wholes[2], 2)
-    grads_near, down_near = lax.optimization_barrier((near(hidden_grad), down_near))
+    grads_near, down_near, far_tokens = lax.optimization_barrier(
+        (near(hidden_grad), down_near, wholes[2])
+    )
+    t2 = shift(far_tokens, 2)
     d0, d1, d2a, d2b, d3 = far(grads_near)
     up_near = outer_near((wholes[0], t1, t3), (d0, d1, d3))
     grad_down = outer_last(True, down_near, g2, h2a, h2b)
@@ -578,7 +578,7 @@
     d_tokens, d_route = combine(place, ids, weight, back, count, width)
     up_near, d_tokens, d_route = lax.optimization_barrier((up_near, d_tokens, d_route))
     grad_up = outer_last(False, up_near, t2, d2a, d2b)
-    return d_tokens, d_route, grad_up[None], grad_down[None]
+    return d_tokens, d_route.T, grad_up[None], grad_down[None]
 
 
 def solution(mesh):

time: 267 us -> 264 us (0.989)
  waiting for transfers between devices: 130 us -> 145 us
  starting transfers between devices: 69.1 us -> 59.4 us
  Pallas kernels: 51.5 us -> 44.7 us
    ppermute x21, waiting for transfers between devices: 112 us -> 127 us  [shift(): lax.ppermute(values, 'cross', [(i, (i + by) % count) for i in range(count)])]
    ppermute x21, starting transfers between devices: 37.5 us -> 27.8 us  [shift(): lax.ppermute(values, 'cross', [(i, (i + by) % count) for i in range(count)])]
    pallas_call x1, Pallas kernels: 16.8 us -> 12.7 us  [expert(): pl.pallas_call(expert_body, out_shape=[jax.ShapeDtypeStruct((rows, hidden...]
    unnamed x51 -> x46, local copies, waits for them, and re-layouts: 9.25 us -> 8.24 us
  transfers between devices with their start and end apart: 24 -> 24, of which waited for: 10 -> 11; matrix products, arithmetic and copies ran while one was open for 2% -> 2% of each run, Pallas kernels for 15% -> 14%
where the time goes in v3:
time: 264 us; the launch traced here: 263 us
  waiting for transfers between devices  145 us (55%)
  starting transfers between devices  59.4 us (22%)
  Pallas kernels  44.7 us (17%)
  local copies, waits for them, and re-layouts  13.1 us (5%)
    ppermute x21, waiting for transfers between devices, shift(): lax.ppermute(values, 'cross', [(i, (i + by) % count) for i in range(count)])  127 us
    all_to_all x3, starting transfers between devices, exchange(): lax.all_to_all(blocks, 'expert', split_axis=0, concat_axis=0, tiled=True)  31.6 us
    ppermute x21, starting transfers between devices, shift(): lax.ppermute(values, 'cross', [(i, (i + by) % count) for i in range(count)])  27.8 us
    all_to_all x3, waiting for transfers between devices, exchange(): lax.all_to_all(blocks, 'expert', split_axis=0, concat_axis=0, tiled=True)  18 us
    pallas_call x1, Pallas kernels, expert(): pl.pallas_call(expert_body, out_shape=[jax.ShapeDtypeStruct((rows, hidden...  12.7 us
    unnamed x46, local copies, waits for them, and re-layouts  8.24 us
    pallas_call x1, Pallas kernels, project(): pl.pallas_call(project_body, out_shape=[jax.ShapeDtypeStruct((rows, block...  7.31 us
    pallas_call x2, Pallas kernels, outer_last(): pl.pallas_call(functools.partial(last_body, left_in_halves), out_shape=ja...  6.49 us
  transfers between devices with their start and end apart: 24, of which 11 were waited for; matrix products, arithmetic and copies ran while one was open for 2% of the time, Pallas kernels for 14%

profile of v3, /device:TPU:1, one launch (start us, length us, event | category | flops | bytes accessed | tf_op | source)
XLA Modules:
  0.0 263.5 jit_solution(4154990929551349309)
XLA Ops:
  3.2 3.4 %collective-permute-start.2 = (bf16[144,768]{1,0:T(8,128)(2,1)S(1)}, bf16[144,768]{1,0:T(8,128)(2,1)S(1)}, u32[]{:S(2)}, u32[]{:S(2)}) collective-permute-start(bf16[144,768]{1,0:T(8,128)(2,1)S(1)} %get-tuple-element.55), channel_id=1, source_target_pairs={{0,3},{1,0},{2,1},{3,2},{4,7},{5,4},{6,5},{7,6},{8,11},{9,8},{10,9... | collective-permute-start | bytes 663560 | tf_op jit(solution)/shard_map/ppermute | solution.py:524
  7.7 7.8 %collective-permute-done.2.s1 = bf16[144,768]{1,0:T(8,128)(2,1)S(1)} collective-permute-done((bf16[144,768]{1,0:T(8,128)(2,1)S(1)}, bf16[144,768]{1,0:T(8,128)(2,1)S(1)}, u32[]{:S(2)}, u32[]{:S(2)}) %collective-permute-start.2) | collective-permute-done | bytes 221216 | tf_op jit(solution)/shard_map/ppermute | solution.py:524
  15.4 4.7 %collective-permute-done.4.s3 = bf16[144,768]{1,0:T(8,128)(2,1)S(1)} collective-permute-done((bf16[144,768]{1,0:T(8,128)(2,1)S(1)}, bf16[144,768]{1,0:T(8,128)(2,1)S(1)}, u32[]{:S(2)}, u32[]{:S(2)}) %collective-permute-start.4) | collective-permute-done | bytes 221216 | tf_op jit(solution)/shard_map/ppermute | solution.py:524
  20.1 2.5 shard_map.95
  22.7 12.1 %all-to-all-start.1 = ((bf16[64,8,2304]{2,1,0:T(8,128)(2,1)}), bf16[64,8,2304]{2,1,0:T(8,128)(2,1)S(1)}, u32[]{:S(2)}, u32[]{:S(2)}) async-start(bf16[64,8,2304]{2,1,0:T(8,128)(2,1)} %bitcast.6), calls=%async_computation.1 | async-start | bytes 4718592 | tf_op jit(solution)/shard_map/all_to_all | solution.py:543
  34.9 2.7 %collective-permute-start = (bf16[768,1024]{1,0:T(8,128)(2,1)}, bf16[768,1024]{1,0:T(8,128)(2,1)}, u32[]{:S(2)}, u32[]{:S(2)}) collective-permute-start(bf16[768,1024]{1,0:T(8,128)(2,1)} %bitcast.27), channel_id=1, source_target_pairs={{0,3},{1,0},{2,1},{3,2},{4,7},{5,4},{6,5},{7,6},{8,11},{9,8},{10,9... | collective-permute-start | bytes 4718600 | tf_op jit(solution)/shard_map/ppermute | solution.py:524
  37.6 3.7 %shard_map.93 = bf16[512,2304]{1,0:T(8,128)(2,1)} custom-call(s32[1]{0:T(128)} %bitcast.place_ref, s32[2,128]{1,0:T(2,128)} %bitcast.15, bf16[128,3072]{1,0:T(8,128)(2,1)} %values_ref.2), custom_call_target="tpu_custom_call" | custom-call | flops 603979776 | bytes 3145728 | tf_op jit(solution)/shard_map/pallas_call | solution.py:100
  41.3 30.7 %collective-permute-done.1.up3 = bf16[768,1024]{1,0:T(8,128)(2,1)} collective-permute-done((bf16[768,1024]{1,0:T(8,128)(2,1)}, bf16[768,1024]{1,0:T(8,128)(2,1)}, u32[]{:S(2)}, u32[]{:S(2)}) %collective-permute-start.1) | collective-permute-done | bytes 1572896 | tf_op jit(solution)/shard_map/ppermute | solution.py:524
  72.0 18.0 %all-to-all-done.1 = bf16[64,8,2304]{2,1,0:T(8,128)(2,1)S(1)} async-done(((bf16[64,8,2304]{2,1,0:T(8,128)(2,1)}), bf16[64,8,2304]{2,1,0:T(8,128)(2,1)S(1)}, u32[]{:S(2)}, u32[]{:S(2)}) %all-to-all-start.1) | async-done | bytes 2359328 | tf_op jit(solution)/shard_map/all_to_all | solution.py:543
  91.5 7.1 %all-to-all-start = ((bf16[64,8,2304]{2,1,0:T(8,128)(2,1)}), bf16[64,8,2304]{2,1,0:T(8,128)(2,1)S(1)}, u32[]{:S(2)}, u32[]{:S(2)}) async-start(bf16[64,8,2304]{2,1,0:T(8,128)(2,1)} %bitcast.20), calls=%async_computation | async-start | bytes 4718592 | tf_op jit(solution)/shard_map/all_to_all | solution.py:543
  99.8 2.1 slice.18
  101.9 2.7 %collective-permute-start.9 = (bf16[384,1024]{1,0:T(8,128)(2,1)S(1)}, bf16[384,1024]{1,0:T(8,128)(2,1)}, u32[]{:S(2)}, u32[]{:S(2)}) collective-permute-start(bf16[384,1024]{1,0:T(8,128)(2,1)S(1)} %slice.19), channel_id=1, source_target_pairs={{0,3},{1,0},{2,1},{3,2},{4,7},{5,4},{6,5},{7,6},{8,11},{9,8},{10,9... | collective-permute-start | bytes 2359304 | tf_op jit(solution)/shard_map/ppermute | solution.py:524
  104.6 7.3 %shard_map.96 = (bf16[384,768]{1,0:T(8,128)(2,1)}, bf16[384,768]{1,0:T(8,128)(2,1)}, bf16[384,768]{1,0:T(8,128)(2,1)}, bf16[384,768]{1,0:T(8,128)(2,1)}, f32[384...) custom-call(bf16[512,2304]{1,0:T(8,128)(2,1)} %bitcast.22, ...), custom_call_target="tpu_custom_call" | custom-call | flops 3019898880 | bytes 8257536 | tf_op jit(solution)/shard_map/pallas_call | solution.py:244
  113.3 24.9 %collective-permute-done.8.up2a = bf16[384,1024]{1,0:T(8,128)(2,1)} collective-permute-done((bf16[384,1024]{1,0:T(8,128)(2,1)}, bf16[384,1024]{1,0:T(8,128)(2,1)}, u32[]{:S(2)}, u32[]{:S(2)}) %collective-permute-start.8) | collective-permute-done | bytes 786464 | tf_op jit(solution)/shard_map/ppermute | solution.py:524
  140.1 15.7 %collective-permute-done.7.b3 = bf16[384,1024]{1,0:T(8,128)(2,1)} collective-permute-done((bf16[384,1024]{1,0:T(8,128)(2,1)}, bf16[384,1024]{1,0:T(8,128)(2,1)}, u32[]{:S(2)}, u32[]{:S(2)}) %collective-permute-start.7) | collective-permute-done | bytes 786464 | tf_op jit(solution)/shard_map/ppermute | solution.py:524
  155.8 1.9 shard_map.97
  159.7 2.7 %collective-permute-start.10 = (bf16[384,768]{1,0:T(8,128)(2,1)S(1)}, bf16[384,768]{1,0:T(8,128)(2,1)S(1)}, u32[]{:S(2)}, u32[]{:S(2)}) collective-permute-start(bf16[384,768]{1,0:T(8,128)(2,1)S(1)} %get-tuple-element.69.x3), channel_id=1, source_target_pairs={{0,3},{1,0},{2,1},{3,2},{4,7},{5,4},{6,5},{7,6},{8,11},{9,8},{10,9... | collective-permute-start | bytes 1769480 | tf_op jit(solution)/shard_map/ppermute | solution.py:524
  162.4 12.7 %shard_map.98 = (bf16[384,1024]{1,0:T(8,128)(2,1)}, bf16[384,1024]{1,0:T(8,128)(2,1)}, bf16[512,2432]{1,0:T(8,128)(2,1)}) custom-call(bf16[384,768]{1,0:T(8,128)(2,1)} %copy-done.8, bf16[384,768]{1,0:T(8,128)(2,1)} %copy-done.19, bf16[384,768]{1,0:T(8,128)(2,1)} %get-tuple-element.100.x2, bf16[384,768]{1,0:T(8,128)(2,1)} %copy-done.18, ...), custom_call_target="tpu_custom_call" | custom-call | flops 6039797760 | bytes 18874368 | tf_op jit(solution)/shard_map/pallas_call | solution.py:376
  176.8 12.3 %all-to-all-start.2 = ((bf16[64,8,2432]{2,1,0:T(8,128)(2,1)}), bf16[64,8,2432]{2,1,0:T(8,128)(2,1)}, u32[]{:S(2)}, u32[]{:S(2)}) async-start(bf16[64,8,2432]{2,1,0:T(8,128)(2,1)} %bitcast.21), calls=%async_computation.2 | async-start | bytes 4980736 | tf_op jit(solution)/shard_map/all_to_all | solution.py:543
  189.2 2.7 %collective-permute-start.14 = (bf16[384,1024]{1,0:T(8,128)(2,1)S(1)}, bf16[384,1024]{1,0:T(8,128)(2,1)S(1)}, u32[]{:S(2)}, u32[]{:S(2)}) collective-permute-start(bf16[384,1024]{1,0:T(8,128)(2,1)S(1)} %copy-done.2), channel_id=1, source_target_pairs={{0,3},{1,0},{2,1},{3,2},{4,7},{5,4},{6,5},{7,6},{8,11},{9,8},{10,9... | collective-permute-start | bytes 2359304 | tf_op jit(solution)/shard_map/ppermute | solution.py:524
  191.9 2.7 %collective-permute-start.12 = (bf16[384,1024]{1,0:T(8,128)(2,1)S(1)}, bf16[384,1024]{1,0:T(8,128)(2,1)S(1)}, u32[]{:S(2)}, u32[]{:S(2)}) collective-permute-start(bf16[384,1024]{1,0:T(8,128)(2,1)S(1)} %copy-done), channel_id=1, source_target_pairs={{0,3},{1,0},{2,1},{3,2},{4,7},{5,4},{6,5},{7,6},{8,11},{9,8},{10,9... | collective-permute-start | bytes 2359304 | tf_op jit(solution)/shard_map/ppermute | solution.py:524
  194.5 14.5 %collective-permute-done.15.l3 = bf16[384,1024]{1,0:T(8,128)(2,1)S(1)} collective-permute-done((bf16[384,1024]{1,0:T(8,128)(2,1)S(1)}, bf16[384,1024]{1,0:T(8,128)(2,1)S(1)}, u32[]{:S(2)}, u32[]{:S(2)}) %collective-permute-start.15) | collective-permute-done | bytes 786464 | tf_op jit(solution)/shard_map/ppermute | solution.py:524
  209.1 3.2 %shard_map.99.total_ref = f32[1024,768]{1,0:T(8,128)S(1)} custom-call(bf16[384,1024]{1,0:T(8,128)(2,1)S(1)} %copy-done.2, bf16[384,1024]{1,0:T(8,128)(2,1)S(1)} %collective-permute-done.14.l1, bf16[384,1024]{1,0:T(8,128)(2,1)S(1)} %collective-permute-done.15.l3, bf16[384,768]{1,0:T(8,128)(2,1)S(1)} %copy-done.5, bf16[384,768]{1,0:T(8,128)(2,1)S(1)} %copy-done.6, ...), custom_call_target="tpu_custom_call" | custom-call | flops 1811939328 | bytes 7274496 | tf_op jit(solution)/shard_map/pallas_call | solution.py:474
  212.4 13.5 %collective-permute-done.13.r3 = bf16[384,1024]{1,0:T(8,128)(2,1)S(1)} collective-permute-done((bf16[384,1024]{1,0:T(8,128)(2,1)S(1)}, bf16[384,1024]{1,0:T(8,128)(2,1)S(1)}, u32[]{:S(2)}, u32[]{:S(2)}) %collective-permute-start.13) | collective-permute-done | bytes 786464 | tf_op jit(solution)/shard_map/ppermute | solution.py:524
  227.3 1.7 collective-permute-start.16
  232.4 2.3 collective-permute-start.20
  234.7 3.0 %shard_map.101.total_ref = f32[768,1024]{1,0:T(8,128)S(1)} custom-call(bf16[384,768]{1,0:T(8,128)(2,1)S(1)} %copy-done.9, bf16[384,768]{1,0:T(8,128)(2,1)S(1)} %copy-done.13, bf16[384,768]{1,0:T(8,128)(2,1)S(1)} %copy-done.11, bf16[384,1024]{1,0:T(8,128)(2,1)S(1)} %copy-done.1, bf16[384,1024]{1,0:T(8,128)(2,1)S(1)} %collective-permute-done.12.r1, ...), custom_call_target="tpu_custom_call" | custom-call | flops 1811939328 | bytes 7274496 | tf_op jit(solution)/shard_map/pallas_call | solution.py:474
  237.7 13.6 %collective-permute-done.16.first = bf16[192,1024]{1,0:T(8,128)(2,1)S(1)} collective-permute-done((bf16[192,1024]{1,0:T(8,128)(2,1)S(1)}, bf16[192,1024]{1,0:T(8,128)(2,1)S(1)}, u32[]{:S(2)}, u32[]{:S(2)}) %collective-permute-start.16) | collective-permute-done | bytes 393248 | tf_op jit(solution)/shard_map/ppermute | solution.py:524
  251.3 2.8 %shard_map.100 = bf16[1024,768]{1,0:T(8,128)(2,1)} custom-call(f32[1024,768]{1,0:T(8,128)S(1)} %shard_map.99.total_ref, bf16[384,768]{1,0:T(8,128)(2,1)S(1)} %copy-done.4, bf16[192,1024]{1,0:T(8,128)(2,1)S(1)} %collective-permute-done.16.first, bf16[192,1024]{1,0:T(8,128)(2,1)S(1)} %collective-permute-done.17.second), custom_call_target="tpu_custom_call" | custom-call | flops 603979776 | bytes 6094848 | tf_op jit(solution)/shard_map/pallas_call | solution.py:508
  254.1 3.8 %shard_map.102 = (bf16[128,3072]{1,0:T(8,128)(2,1)}, bf16[2,128]{1,0:T(2,128)(2,1)}) custom-call(s32[1]{0:T(128)} %bitcast.place_ref, s32[2,128]{1,0:T(2,128)S(1)} %bitcast.17, bf16[2,128]{1,0:T(2,128)(2,1)S(1)} %bitcast.19, bf16[512,2432]{1,0:T(8,128)(2,1)} %bitcast.10.ret_ref), custom_call_target="tpu_custom_call" | custom-call | flops 805306368 | bytes 3276800 | tf_op jit(solution)/shard_map/pallas_call | solution.py:441
  258.0 1.8 collective-permute-done.19.first
  259.8 3.7 %shard_map.103 = bf16[768,1024]{1,0:T(8,128)(2,1)} custom-call(f32[768,1024]{1,0:T(8,128)S(1)} %shard_map.101.total_ref, bf16[384,768]{1,0:T(8,128)(2,1)} %collective-permute-done.18.whole, bf16[192,1024]{1,0:T(8,128)(2,1)S(1)} %collective-permute-done.19.first, bf16[192,1024]{1,0:T(8,128)(2,1)} %collective-permute-done.20.second), custom_call_target="tpu_custom_call" | custom-call | flops 603979776 | bytes 6094848 | tf_op jit(solution)/shard_map/pallas_call | solution.py:508
  (79 shorter events, 18.3 us)
Async XLA Ops:
  3.2 12.3 %collective-permute-start.2 = (bf16[144,768]{1,0:T(8,128)(2,1)S(1)}, bf16[144,768]{1,0:T(8,128)(2,1)S(1)}, u32[]{:S(2)}, u32[]{:S(2)}) collective-permute-start(bf16[144,768]{1,0:T(8,128)(2,1)S(1)} %get-tuple-element.55), channel_id=1, source_target_pairs={{0,3},{1,0},{2,1},{3,2},{4,7},{5,4},{6,5},{7,6},{8,11},{9,8},{10,9... | collective-permute-start | bytes 663560 | tf_op jit(solution)/shard_map/ppermute | solution.py:524
  6.6 8.9 %collective-permute-start.3 = (bf16[144,768]{1,0:T(8,128)(2,1)S(1)}, bf16[144,768]{1,0:T(8,128)(2,1)S(1)}, u32[]{:S(2)}, u32[]{:S(2)}) collective-permute-start(bf16[144,768]{1,0:T(8,128)(2,1)S(1)} %get-tuple-element.56), channel_id=1, source_target_pairs={{0,2},{1,3},{2,0},{3,1},{4,6},{5,7},{6,4},{7,5},{8,10},{9,11},{10,... | collective-permute-start | bytes 663560 | tf_op jit(solution)/shard_map/ppermute | solution.py:524
  7.1 13.1 %collective-permute-start.4 = (bf16[144,768]{1,0:T(8,128)(2,1)S(1)}, bf16[144,768]{1,0:T(8,128)(2,1)S(1)}, u32[]{:S(2)}, u32[]{:S(2)}) collective-permute-start(bf16[144,768]{1,0:T(8,128)(2,1)S(1)} %get-tuple-element.57), channel_id=1, source_target_pairs={{0,1},{1,2},{2,3},{3,0},{4,5},{5,6},{6,7},{7,4},{8,9},{9,10},{10,1... | collective-permute-start | bytes 663560 | tf_op jit(solution)/shard_map/ppermute | solution.py:524
  22.7 67.3 %all-to-all-start.1 = ((bf16[64,8,2304]{2,1,0:T(8,128)(2,1)}), bf16[64,8,2304]{2,1,0:T(8,128)(2,1)S(1)}, u32[]{:S(2)}, u32[]{:S(2)}) async-start(bf16[64,8,2304]{2,1,0:T(8,128)(2,1)} %bitcast.6), calls=%async_computation.1 | async-start | bytes 4718592 | tf_op jit(solution)/shard_map/all_to_all | solution.py:543
  34.8 37.1 %collective-permute-start.1 = (bf16[768,1024]{1,0:T(8,128)(2,1)}, bf16[768,1024]{1,0:T(8,128)(2,1)}, u32[]{:S(2)}, u32[]{:S(2)}) collective-permute-start(bf16[768,1024]{1,0:T(8,128)(2,1)} %bitcast.26), channel_id=1, source_target_pairs={{0,1},{1,2},{2,3},{3,0},{4,5},{5,6},{6,7},{7,4},{8,9},{9,10},{10,1... | collective-permute-start | bytes 4718600 | tf_op jit(solution)/shard_map/ppermute | solution.py:524
  34.9 37.0 %collective-permute-start = (bf16[768,1024]{1,0:T(8,128)(2,1)}, bf16[768,1024]{1,0:T(8,128)(2,1)}, u32[]{:S(2)}, u32[]{:S(2)}) collective-permute-start(bf16[768,1024]{1,0:T(8,128)(2,1)} %bitcast.27), channel_id=1, source_target_pairs={{0,3},{1,0},{2,1},{3,2},{4,7},{5,4},{6,5},{7,6},{8,11},{9,8},{10,9... | collective-permute-start | bytes 4718600 | tf_op jit(solution)/shard_map/ppermute | solution.py:524
  91.5 64.3 %all-to-all-start = ((bf16[64,8,2304]{2,1,0:T(8,128)(2,1)}), bf16[64,8,2304]{2,1,0:T(8,128)(2,1)S(1)}, u32[]{:S(2)}, u32[]{:S(2)}) async-start(bf16[64,8,2304]{2,1,0:T(8,128)(2,1)} %bitcast.20), calls=%async_computation | async-start | bytes 4718592 | tf_op jit(solution)/shard_map/all_to_all | solution.py:543
  101.9 36.4 %collective-permute-start.8 = (bf16[384,1024]{1,0:T(8,128)(2,1)}, bf16[384,1024]{1,0:T(8,128)(2,1)}, u32[]{:S(2)}, u32[]{:S(2)}) collective-permute-start(bf16[384,1024]{1,0:T(8,128)(2,1)} %slice.18), channel_id=1, source_target_pairs={{0,1},{1,2},{2,3},{3,0},{4,5},{5,6},{6,7},{7,4},{8,9},{9,10},{10,1... | collective-permute-start | bytes 2359304 | tf_op jit(solution)/shard_map/ppermute | solution.py:524
  101.9 36.4 %collective-permute-start.9 = (bf16[384,1024]{1,0:T(8,128)(2,1)S(1)}, bf16[384,1024]{1,0:T(8,128)(2,1)}, u32[]{:S(2)}, u32[]{:S(2)}) collective-permute-start(bf16[384,1024]{1,0:T(8,128)(2,1)S(1)} %slice.19), channel_id=1, source_target_pairs={{0,3},{1,0},{2,1},{3,2},{4,7},{5,4},{6,5},{7,6},{8,11},{9,8},{10,9... | collective-permute-start | bytes 2359304 | tf_op jit(solution)/shard_map/ppermute | solution.py:524
  111.9 26.5 %collective-permute-start.5 = (bf16[384,1024]{1,0:T(8,128)(2,1)}, bf16[384,1024]{1,0:T(8,128)(2,1)S(1)}, u32[]{:S(2)}, u32[]{:S(2)}) collective-permute-start(bf16[384,1024]{1,0:T(8,128)(2,1)} %get-tuple-element.59), channel_id=1, source_target_pairs={{0,3},{1,0},{2,1},{3,2},{4,7},{5,4},{6,5},{7,6},{8,11},{9,8},{10,9... | collective-permute-start | bytes 2359304 | tf_op jit(solution)/shard_map/ppermute | solution.py:524
  111.9 26.5 %collective-permute-start.6 = (bf16[384,1024]{1,0:T(8,128)(2,1)}, bf16[384,1024]{1,0:T(8,128)(2,1)S(1)}, u32[]{:S(2)}, u32[]{:S(2)}) collective-permute-start(bf16[384,1024]{1,0:T(8,128)(2,1)} %get-tuple-element.60), channel_id=1, source_target_pairs={{0,2},{1,3},{2,0},{3,1},{4,6},{5,7},{6,4},{7,5},{8,10},{9,11},{10,... | collective-permute-start | bytes 2359304 | tf_op jit(solution)/shard_map/ppermute | solution.py:524
  112.4 43.3 %collective-permute-start.7 = (bf16[384,1024]{1,0:T(8,128)(2,1)}, bf16[384,1024]{1,0:T(8,128)(2,1)}, u32[]{:S(2)}, u32[]{:S(2)}) collective-permute-start(bf16[384,1024]{1,0:T(8,128)(2,1)} %get-tuple-element.61), channel_id=1, source_target_pairs={{0,1},{1,2},{2,3},{3,0},{4,5},{5,6},{6,7},{7,4},{8,9},{9,10},{10,1... | collective-permute-start | bytes 2359304 | tf_op jit(solution)/shard_map/ppermute | solution.py:524
  158.5 16.6 %collective-permute-start.11 = (bf16[384,768]{1,0:T(8,128)(2,1)S(1)}, bf16[384,768]{1,0:T(8,128)(2,1)S(1)}, u32[]{:S(2)}, u32[]{:S(2)}) collective-permute-start(bf16[384,768]{1,0:T(8,128)(2,1)S(1)} %get-tuple-element.67.x1), channel_id=1, source_target_pairs={{0,1},{1,2},{2,3},{3,0},{4,5},{5,6},{6,7},{7,4},{8,9},{9,10},{10,1... | collective-permute-start | bytes 1769480 | tf_op jit(solution)/shard_map/ppermute | solution.py:524
  159.7 16.3 %collective-permute-start.10 = (bf16[384,768]{1,0:T(8,128)(2,1)S(1)}, bf16[384,768]{1,0:T(8,128)(2,1)S(1)}, u32[]{:S(2)}, u32[]{:S(2)}) collective-permute-start(bf16[384,768]{1,0:T(8,128)(2,1)S(1)} %get-tuple-element.69.x3), channel_id=1, source_target_pairs={{0,3},{1,0},{2,1},{3,2},{4,7},{5,4},{6,5},{7,6},{8,11},{9,8},{10,9... | collective-permute-start | bytes 1769480 | tf_op jit(solution)/shard_map/ppermute | solution.py:524
  176.8 32.3 %copy-start.5 = (bf16[384,768]{1,0:T(8,128)(2,1)S(1)}, bf16[384,768]{1,0:T(8,128)(2,1)}, u32[]{:S(2)}) copy-start(bf16[384,768]{1,0:T(8,128)(2,1)} %get-tuple-element.83.r0) | copy-start | bytes 1769476
  176.8 32.3 %copy-start.6 = (bf16[384,768]{1,0:T(8,128)(2,1)S(1)}, bf16[384,768]{1,0:T(8,128)(2,1)}, u32[]{:S(2)}) copy-start(bf16[384,768]{1,0:T(8,128)(2,1)} %get-tuple-element.84.r1) | copy-start | bytes 1769476
  176.8 32.3 %copy-start.7 = (bf16[384,768]{1,0:T(8,128)(2,1)S(1)}, bf16[384,768]{1,0:T(8,128)(2,1)}, u32[]{:S(2)}) copy-start(bf16[384,768]{1,0:T(8,128)(2,1)} %get-tuple-element.85.r3) | copy-start | bytes 1769476
  176.8 77.3 %all-to-all-start.2 = ((bf16[64,8,2432]{2,1,0:T(8,128)(2,1)}), bf16[64,8,2432]{2,1,0:T(8,128)(2,1)}, u32[]{:S(2)}, u32[]{:S(2)}) async-start(bf16[64,8,2432]{2,1,0:T(8,128)(2,1)} %bitcast.21), calls=%async_computation.2 | async-start | bytes 4980736 | tf_op jit(solution)/shard_map/all_to_all | solution.py:543
  189.1 20.0 %collective-permute-start.15 = (bf16[384,1024]{1,0:T(8,128)(2,1)S(1)}, bf16[384,1024]{1,0:T(8,128)(2,1)S(1)}, u32[]{:S(2)}, u32[]{:S(2)}) collective-permute-start(bf16[384,1024]{1,0:T(8,128)(2,1)S(1)} %copy-done.2), channel_id=1, source_target_pairs={{0,1},{1,2},{2,3},{3,0},{4,5},{5,6},{6,7},{7,4},{8,9},{9,10},{10,1... | collective-permute-start | bytes 2359304 | tf_op jit(solution)/shard_map/ppermute | solution.py:524
  189.2 19.9 %collective-permute-start.14 = (bf16[384,1024]{1,0:T(8,128)(2,1)S(1)}, bf16[384,1024]{1,0:T(8,128)(2,1)S(1)}, u32[]{:S(2)}, u32[]{:S(2)}) collective-permute-start(bf16[384,1024]{1,0:T(8,128)(2,1)S(1)} %copy-done.2), channel_id=1, source_target_pairs={{0,3},{1,0},{2,1},{3,2},{4,7},{5,4},{6,5},{7,6},{8,11},{9,8},{10,9... | collective-permute-start | bytes 2359304 | tf_op jit(solution)/shard_map/ppermute | solution.py:524
  191.8 34.1 %collective-permute-start.13 = (bf16[384,1024]{1,0:T(8,128)(2,1)S(1)}, bf16[384,1024]{1,0:T(8,128)(2,1)S(1)}, u32[]{:S(2)}, u32[]{:S(2)}) collective-permute-start(bf16[384,1024]{1,0:T(8,128)(2,1)S(1)} %copy-done), channel_id=1, source_target_pairs={{0,1},{1,2},{2,3},{3,0},{4,5},{5,6},{6,7},{7,4},{8,9},{9,10},{10,1... | collective-permute-start | bytes 2359304 | tf_op jit(solution)/shard_map/ppermute | solution.py:524
  191.9 34.1 %collective-permute-start.12 = (bf16[384,1024]{1,0:T(8,128)(2,1)S(1)}, bf16[384,1024]{1,0:T(8,128)(2,1)S(1)}, u32[]{:S(2)}, u32[]{:S(2)}) collective-permute-start(bf16[384,1024]{1,0:T(8,128)(2,1)S(1)} %copy-done), channel_id=1, source_target_pairs={{0,3},{1,0},{2,1},{3,2},{4,7},{5,4},{6,5},{7,6},{8,11},{9,8},{10,9... | collective-permute-start | bytes 2359304 | tf_op jit(solution)/shard_map/ppermute | solution.py:524
  212.3 22.3 %copy-start.1 = (bf16[384,1024]{1,0:T(8,128)(2,1)S(1)}, bf16[384,1024]{1,0:T(8,128)(2,1)}, u32[]{:S(2)}) copy-start(bf16[384,1024]{1,0:T(8,128)(2,1)} %get-tuple-element.90.r0) | copy-start | bytes 2359300
  212.4 22.3 %copy-start.9 = (bf16[384,768]{1,0:T(8,128)(2,1)S(1)}, bf16[384,768]{1,0:T(8,128)(2,1)}, u32[]{:S(2)}) copy-start(bf16[384,768]{1,0:T(8,128)(2,1)} %copy-done.8) | copy-start | bytes 1769476
  212.4 22.3 %copy-start.11 = (bf16[384,768]{1,0:T(8,128)(2,1)S(1)}, bf16[384,768]{1,0:T(8,128)(2,1)}, u32[]{:S(2)}) copy-start(bf16[384,768]{1,0:T(8,128)(2,1)} %copy-done.10) | copy-start | bytes 1769476
  212.4 22.3 %copy-start.13 = (bf16[384,768]{1,0:T(8,128)(2,1)S(1)}, bf16[384,768]{1,0:T(8,128)(2,1)}, u32[]{:S(2)}) copy-start(bf16[384,768]{1,0:T(8,128)(2,1)} %copy-done.12) | copy-start | bytes 1769476
  225.9 33.8 %collective-permute-start.18 = (bf16[384,768]{1,0:T(8,128)(2,1)}, bf16[384,768]{1,0:T(8,128)(2,1)}, u32[]{:S(2)}, u32[]{:S(2)}) collective-permute-start(bf16[384,768]{1,0:T(8,128)(2,1)} %get-tuple-element.100.x2), channel_id=1, source_target_pairs={{0,2},{1,3},{2,0},{3,1},{4,6},{5,7},{6,4},{7,5},{8,10},{9,11},{10,... | collective-permute-start | bytes 1769480 | tf_op jit(solution)/shard_map/ppermute | solution.py:524
  227.3 24.0 %collective-permute-start.16 = (bf16[192,1024]{1,0:T(8,128)(2,1)S(1)}, bf16[192,1024]{1,0:T(8,128)(2,1)S(1)}, u32[]{:S(2)}, u32[]{:S(2)}) collective-permute-start(bf16[192,1024]{1,0:T(8,128)(2,1)S(1)} %slice.24), channel_id=1, source_target_pairs={{0,1},{1,2},{2,3},{3,0},{4,5},{5,6},{6,7},{7,4},{8,9},{9,10},{10,1... | collective-permute-start | bytes 1179656 | tf_op jit(solution)/shard_map/ppermute | solution.py:524
  229.0 22.3 %collective-permute-start.17 = (bf16[192,1024]{1,0:T(8,128)(2,1)S(1)}, bf16[192,1024]{1,0:T(8,128)(2,1)S(1)}, u32[]{:S(2)}, u32[]{:S(2)}) collective-permute-start(bf16[192,1024]{1,0:T(8,128)(2,1)S(1)} %slice.25), channel_id=1, source_target_pairs={{0,3},{1,0},{2,1},{3,2},{4,7},{5,4},{6,5},{7,6},{8,11},{9,8},{10,9... | collective-permute-start | bytes 1179656 | tf_op jit(solution)/shard_map/ppermute | solution.py:524
  232.0 19.4 %copy-start.4 = (bf16[384,768]{1,0:T(8,128)(2,1)S(1)}, bf16[384,768]{1,0:T(8,128)(2,1)}, u32[]{:S(2)}) copy-start(bf16[384,768]{1,0:T(8,128)(2,1)} %get-tuple-element.87.whole) | copy-start | bytes 1769476
  232.0 27.8 %collective-permute-start.19 = (bf16[192,1024]{1,0:T(8,128)(2,1)}, bf16[192,1024]{1,0:T(8,128)(2,1)S(1)}, u32[]{:S(2)}, u32[]{:S(2)}) collective-permute-start(bf16[192,1024]{1,0:T(8,128)(2,1)} %slice.22), channel_id=1, source_target_pairs={{0,1},{1,2},{2,3},{3,0},{4,5},{5,6},{6,7},{7,4},{8,9},{9,10},{10,1... | collective-permute-start | bytes 1179656 | tf_op jit(solution)/shard_map/ppermute | solution.py:524
  232.4 27.4 %collective-permute-start.20 = (bf16[192,1024]{1,0:T(8,128)(2,1)}, bf16[192,1024]{1,0:T(8,128)(2,1)}, u32[]{:S(2)}, u32[]{:S(2)}) collective-permute-start(bf16[192,1024]{1,0:T(8,128)(2,1)} %slice.23), channel_id=1, source_target_pairs={{0,3},{1,0},{2,1},{3,2},{4,7},{5,4},{6,5},{7,6},{8,11},{9,8},{10,9... | collective-permute-start | bytes 1179656 | tf_op jit(solution)/shard_map/ppermute | solution.py:524
  (15 other events, 49.0 us)

commit v4 on v3

--- a/solution.py
+++ b/solution.py
@@ -388,7 +388,7 @@
             pltpu.SemaphoreType.DMA((2, steps)),
             pltpu.SemaphoreType.DMA((1 + 3 * chunks,)),
         ],
-        compiler_params=vmem(60),
+        compiler_params=vmem(63),
         cost_estimate=pl.CostEstimate(
             flops=20 * rows * block * hidden_width,
             bytes_accessed=24 * block * hidden_width,
@@ -565,12 +565,11 @@
     hidden, hidden_grad, ret = expert(wholes, ups, backs, experts)
     ret, t1, t3 = lax.optimization_barrier((ret, t1, t3))
     back = exchange(ret, experts)
-    h0, h1, h2a, h2b, h3 = far(near(hidden))
+    hidden_near, far_tokens = lax.optimization_barrier((near(hidden), wholes[2]))
+    h0, h1, h2a, h2b, h3 = far(hidden_near)
+    t2 = shift(far_tokens, 2)
     down_near = outer_near((h0, h1, h3), (g0, g1, g3))
-    grads_near, down_near, far_tokens = lax.optimization_barrier(
-        (near(hidden_grad), down_near, wholes[2])
-    )
-    t2 = shift(far_tokens, 2)
+    grads_near, down_near = lax.optimization_barrier((near(hidden_grad), down_near))
     d0, d1, d2a, d2b, d3 = far(grads_near)
     up_near = outer_near((wholes[0], t1, t3), (d0, d1, d3))
     grad_down = outer_last(True, down_near, g2, h2a, h2b)

time: 264 us -> 260 us (0.985)
  waiting for transfers between devices: 145 us -> 129 us
  starting transfers between devices: 59.4 us -> 70.3 us
    ppermute x21, waiting for transfers between devices: 127 us -> 111 us  [shift(): lax.ppermute(values, 'cross', [(i, (i + by) % count) for i in range(count)])]
    ppermute x21, starting transfers between devices: 27.8 us -> 38.7 us  [shift(): lax.ppermute(values, 'cross', [(i, (i + by) % count) for i in range(count)])]
    unnamed x46 -> x40, local copies, waits for them, and re-layouts: 8.24 us -> 8.22 us
  transfers between devices with their start and end apart: 24 -> 24, of which waited for: 11 -> 11; matrix products, arithmetic and copies ran while one was open for 2% -> 2% of each run, Pallas kernels for 14% -> 15%
where the time goes in v4:
time: 260 us; the launch traced here: 259 us
  waiting for transfers between devices  129 us (50%)
  starting transfers between devices  70.3 us (27%)
  Pallas kernels  46.1 us (18%)
  local copies, waits for them, and re-layouts  13.1 us (5%)
    ppermute x21, waiting for transfers between devices, shift(): lax.ppermute(values, 'cross', [(i, (i + by) % count) for i in range(count)])  111 us
    ppermute x21, starting transfers between devices, shift(): lax.ppermute(values, 'cross', [(i, (i + by) % count) for i in range(count)])  38.7 us
    all_to_all x3, starting transfers between devices, exchange(): lax.all_to_all(blocks, 'expert', split_axis=0, concat_axis=0, tiled=True)  31.6 us
    all_to_all x3, waiting for transfers between devices, exchange(): lax.all_to_all(blocks, 'expert', split_axis=0, concat_axis=0, tiled=True)  18 us
    pallas_call x1, Pallas kernels, expert(): pl.pallas_call(expert_body, out_shape=[jax.ShapeDtypeStruct((rows, hidden...  12.8 us
    unnamed x40, local copies, waits for them, and re-layouts  8.22 us
    pallas_call x1, Pallas kernels, project(): pl.pallas_call(project_body, out_shape=[jax.ShapeDtypeStruct((rows, block...  7.34 us
    pallas_call x2, Pallas kernels, outer_near(): pl.pallas_call(near_body, out_shape=jax.ShapeDtypeStruct(shape, F32), in_...  7.33 us
  transfers between devices with their start and end apart: 24, of which 11 were waited for; matrix products, arithmetic and copies ran while one was open for 2% of the time, Pallas kernels for 15%

profile of v4, /device:TPU:1, one launch (start us, length us, event | category | flops | bytes accessed | tf_op | source)
XLA Modules:
  0.0 259.2 jit_solution(3941186397116824274)
XLA Ops:
  3.2 3.4 %collective-permute-start.2 = (bf16[144,768]{1,0:T(8,128)(2,1)S(1)}, bf16[144,768]{1,0:T(8,128)(2,1)S(1)}, u32[]{:S(2)}, u32[]{:S(2)}) collective-permute-start(bf16[144,768]{1,0:T(8,128)(2,1)S(1)} %get-tuple-element.58), channel_id=1, source_target_pairs={{0,3},{1,0},{2,1},{3,2},{4,7},{5,4},{6,5},{7,6},{8,11},{9,8},{10,9... | collective-permute-start | bytes 663560 | tf_op jit(solution)/shard_map/ppermute | solution.py:524
  7.7 7.8 %collective-permute-done.2.s1 = bf16[144,768]{1,0:T(8,128)(2,1)S(1)} collective-permute-done((bf16[144,768]{1,0:T(8,128)(2,1)S(1)}, bf16[144,768]{1,0:T(8,128)(2,1)S(1)}, u32[]{:S(2)}, u32[]{:S(2)}) %collective-permute-start.2) | collective-permute-done | bytes 221216 | tf_op jit(solution)/shard_map/ppermute | solution.py:524
  15.4 4.7 %collective-permute-done.4.s3 = bf16[144,768]{1,0:T(8,128)(2,1)S(1)} collective-permute-done((bf16[144,768]{1,0:T(8,128)(2,1)S(1)}, bf16[144,768]{1,0:T(8,128)(2,1)S(1)}, u32[]{:S(2)}, u32[]{:S(2)}) %collective-permute-start.4) | collective-permute-done | bytes 221216 | tf_op jit(solution)/shard_map/ppermute | solution.py:524
  20.1 2.5 shard_map.95
  22.6 12.1 %all-to-all-start.1 = ((bf16[64,8,2304]{2,1,0:T(8,128)(2,1)}), bf16[64,8,2304]{2,1,0:T(8,128)(2,1)S(1)}, u32[]{:S(2)}, u32[]{:S(2)}) async-start(bf16[64,8,2304]{2,1,0:T(8,128)(2,1)} %bitcast.6), calls=%async_computation.1 | async-start | bytes 4718592 | tf_op jit(solution)/shard_map/all_to_all | solution.py:543
  34.9 2.7 %collective-permute-start = (bf16[768,1024]{1,0:T(8,128)(2,1)}, bf16[768,1024]{1,0:T(8,128)(2,1)}, u32[]{:S(2)}, u32[]{:S(2)}) collective-permute-start(bf16[768,1024]{1,0:T(8,128)(2,1)} %bitcast.27), channel_id=1, source_target_pairs={{0,3},{1,0},{2,1},{3,2},{4,7},{5,4},{6,5},{7,6},{8,11},{9,8},{10,9... | collective-permute-start | bytes 4718600 | tf_op jit(solution)/shard_map/ppermute | solution.py:524
  37.5 3.7 %shard_map.93 = bf16[512,2304]{1,0:T(8,128)(2,1)} custom-call(s32[1]{0:T(128)} %bitcast.place_ref, s32[2,128]{1,0:T(2,128)} %bitcast.15, bf16[128,3072]{1,0:T(8,128)(2,1)} %values_ref.2), custom_call_target="tpu_custom_call" | custom-call | flops 603979776 | bytes 3145728 | tf_op jit(solution)/shard_map/pallas_call | solution.py:100
  41.2 30.7 %collective-permute-done.1.up3 = bf16[768,1024]{1,0:T(8,128)(2,1)} collective-permute-done((bf16[768,1024]{1,0:T(8,128)(2,1)}, bf16[768,1024]{1,0:T(8,128)(2,1)}, u32[]{:S(2)}, u32[]{:S(2)}) %collective-permute-start.1) | collective-permute-done | bytes 1572896 | tf_op jit(solution)/shard_map/ppermute | solution.py:524
  71.9 18.0 %all-to-all-done.1 = bf16[64,8,2304]{2,1,0:T(8,128)(2,1)S(1)} async-done(((bf16[64,8,2304]{2,1,0:T(8,128)(2,1)}), bf16[64,8,2304]{2,1,0:T(8,128)(2,1)S(1)}, u32[]{:S(2)}, u32[]{:S(2)}) %all-to-all-start.1) | async-done | bytes 2359328 | tf_op jit(solution)/shard_map/all_to_all | solution.py:543
  90.0 1.5 copy-done.17
  91.4 7.1 %all-to-all-start = ((bf16[64,8,2304]{2,1,0:T(8,128)(2,1)}), bf16[64,8,2304]{2,1,0:T(8,128)(2,1)S(1)}, u32[]{:S(2)}, u32[]{:S(2)}) async-start(bf16[64,8,2304]{2,1,0:T(8,128)(2,1)} %bitcast.20), calls=%async_computation | async-start | bytes 4718592 | tf_op jit(solution)/shard_map/all_to_all | solution.py:543
  99.8 2.1 slice.18
  101.8 2.7 %collective-permute-start.9 = (bf16[384,1024]{1,0:T(8,128)(2,1)S(1)}, bf16[384,1024]{1,0:T(8,128)(2,1)}, u32[]{:S(2)}, u32[]{:S(2)}) collective-permute-start(bf16[384,1024]{1,0:T(8,128)(2,1)S(1)} %slice.19), channel_id=1, source_target_pairs={{0,3},{1,0},{2,1},{3,2},{4,7},{5,4},{6,5},{7,6},{8,11},{9,8},{10,9... | collective-permute-start | bytes 2359304 | tf_op jit(solution)/shard_map/ppermute | solution.py:524
  104.5 7.3 %shard_map.96 = (bf16[384,768]{1,0:T(8,128)(2,1)}, bf16[384,768]{1,0:T(8,128)(2,1)}, bf16[384,768]{1,0:T(8,128)(2,1)}, bf16[384,768]{1,0:T(8,128)(2,1)}, f32[384...) custom-call(bf16[512,2304]{1,0:T(8,128)(2,1)} %bitcast.22, ...), custom_call_target="tpu_custom_call" | custom-call | flops 3019898880 | bytes 8257536 | tf_op jit(solution)/shard_map/pallas_call | solution.py:244
  113.3 24.9 %collective-permute-done.8.up2a = bf16[384,1024]{1,0:T(8,128)(2,1)} collective-permute-done((bf16[384,1024]{1,0:T(8,128)(2,1)}, bf16[384,1024]{1,0:T(8,128)(2,1)}, u32[]{:S(2)}, u32[]{:S(2)}) %collective-permute-start.8) | collective-permute-done | bytes 786464 | tf_op jit(solution)/shard_map/ppermute | solution.py:524
  140.0 15.7 %collective-permute-done.7.b3 = bf16[384,1024]{1,0:T(8,128)(2,1)} collective-permute-done((bf16[384,1024]{1,0:T(8,128)(2,1)}, bf16[384,1024]{1,0:T(8,128)(2,1)}, u32[]{:S(2)}, u32[]{:S(2)}) %collective-permute-start.7) | collective-permute-done | bytes 786464 | tf_op jit(solution)/shard_map/ppermute | solution.py:524
  155.7 2.0 shard_map.97
  160.6 2.7 %collective-permute-start.10 = (bf16[384,768]{1,0:T(8,128)(2,1)}, bf16[384,768]{1,0:T(8,128)(2,1)}, u32[]{:S(2)}, u32[]{:S(2)}) collective-permute-start(bf16[384,768]{1,0:T(8,128)(2,1)} %get-tuple-element.72.x3), channel_id=1, source_target_pairs={{0,3},{1,0},{2,1},{3,2},{4,7},{5,4},{6,5},{7,6},{8,11},{9,8},{10,9... | collective-permute-start | bytes 1769480 | tf_op jit(solution)/shard_map/ppermute | solution.py:524
  163.3 12.8 %shard_map.98 = (bf16[384,1024]{1,0:T(8,128)(2,1)}, bf16[384,1024]{1,0:T(8,128)(2,1)}, bf16[512,2432]{1,0:T(8,128)(2,1)}) custom-call(bf16[384,768]{1,0:T(8,128)(2,1)} %copy-done.8, bf16[384,768]{1,0:T(8,128)(2,1)} %get-tuple-element.70.x1, bf16[384,768]{1,0:T(8,128)(2,1)} %copy-done.16, bf16[384,768]{1,0:T(8,128)(2,1)} %get-tuple-element.72.x3, ...), custom_call_target="tpu_custom_call" | custom-call | flops 6039797760 | bytes 18874368 | tf_op jit(solution)/shard_map/pallas_call | solution.py:376
  177.0 12.3 %all-to-all-start.2 = ((bf16[64,8,2432]{2,1,0:T(8,128)(2,1)}), bf16[64,8,2432]{2,1,0:T(8,128)(2,1)}, u32[]{:S(2)}, u32[]{:S(2)}) async-start(bf16[64,8,2432]{2,1,0:T(8,128)(2,1)} %bitcast.21), calls=%async_computation.2 | async-start | bytes 4980736 | tf_op jit(solution)/shard_map/all_to_all | solution.py:543
  189.4 2.7 %collective-permute-start.14 = (bf16[384,1024]{1,0:T(8,128)(2,1)S(1)}, bf16[384,1024]{1,0:T(8,128)(2,1)S(1)}, u32[]{:S(2)}, u32[]{:S(2)}) collective-permute-start(bf16[384,1024]{1,0:T(8,128)(2,1)S(1)} %copy-done.2), channel_id=1, source_target_pairs={{0,3},{1,0},{2,1},{3,2},{4,7},{5,4},{6,5},{7,6},{8,11},{9,8},{10,9... | collective-permute-start | bytes 2359304 | tf_op jit(solution)/shard_map/ppermute | solution.py:524
  192.0 2.7 %collective-permute-start.12 = (bf16[384,1024]{1,0:T(8,128)(2,1)S(1)}, bf16[384,1024]{1,0:T(8,128)(2,1)S(1)}, u32[]{:S(2)}, u32[]{:S(2)}) collective-permute-start(bf16[384,1024]{1,0:T(8,128)(2,1)S(1)} %copy-done), channel_id=1, source_target_pairs={{0,3},{1,0},{2,1},{3,2},{4,7},{5,4},{6,5},{7,6},{8,11},{9,8},{10,9... | collective-permute-start | bytes 2359304 | tf_op jit(solution)/shard_map/ppermute | solution.py:524
  194.7 14.5 %collective-permute-done.15.l3 = bf16[384,1024]{1,0:T(8,128)(2,1)S(1)} collective-permute-done((bf16[384,1024]{1,0:T(8,128)(2,1)S(1)}, bf16[384,1024]{1,0:T(8,128)(2,1)S(1)}, u32[]{:S(2)}, u32[]{:S(2)}) %collective-permute-start.15) | collective-permute-done | bytes 786464 | tf_op jit(solution)/shard_map/ppermute | solution.py:524
  210.8 1.6 collective-permute-start.16
  213.5 3.3 %shard_map.99.total_ref = f32[1024,768]{1,0:T(8,128)S(1)} custom-call(bf16[384,1024]{1,0:T(8,128)(2,1)S(1)} %copy-done.2, bf16[384,1024]{1,0:T(8,128)(2,1)S(1)} %collective-permute-done.14.l1, bf16[384,1024]{1,0:T(8,128)(2,1)S(1)} %collective-permute-done.15.l3, bf16[384,768]{1,0:T(8,128)(2,1)S(1)} %copy-done.5, bf16[384,768]{1,0:T(8,128)(2,1)S(1)} %copy-done.6, ...), custom_call_target="tpu_custom_call" | custom-call | flops 1811939328 | bytes 7274496 | tf_op jit(solution)/shard_map/pallas_call | solution.py:474
  216.8 9.3 %collective-permute-done.13.r3 = bf16[384,1024]{1,0:T(8,128)(2,1)S(1)} collective-permute-done((bf16[384,1024]{1,0:T(8,128)(2,1)S(1)}, bf16[384,1024]{1,0:T(8,128)(2,1)S(1)}, u32[]{:S(2)}, u32[]{:S(2)}) %collective-permute-start.13) | collective-permute-done | bytes 786464 | tf_op jit(solution)/shard_map/ppermute | solution.py:524
  227.7 13.8 %collective-permute-start.20 = (bf16[192,1024]{1,0:T(8,128)(2,1)}, bf16[192,1024]{1,0:T(8,128)(2,1)}, u32[]{:S(2)}, u32[]{:S(2)}) collective-permute-start(bf16[192,1024]{1,0:T(8,128)(2,1)} %slice.23), channel_id=1, source_target_pairs={{0,3},{1,0},{2,1},{3,2},{4,7},{5,4},{6,5},{7,6},{8,11},{9,8},{10,9... | collective-permute-start | bytes 1179656 | tf_op jit(solution)/shard_map/ppermute | solution.py:524
  241.5 4.1 %shard_map.101.total_ref = f32[768,1024]{1,0:T(8,128)S(1)} custom-call(bf16[384,768]{1,0:T(8,128)(2,1)S(1)} %copy-done.9, bf16[384,768]{1,0:T(8,128)(2,1)} %collective-permute-done.10.l1, bf16[384,768]{1,0:T(8,128)(2,1)S(1)} %copy-done.11, bf16[384,1024]{1,0:T(8,128)(2,1)S(1)} %copy-done.1, bf16[384,1024]{1,0:T(8,128)(2,1)S(1)} %collective-permute-done.12.r1, ...), custom_call_target="tpu_custom_call" | custom-call | flops 1811939328 | bytes 7274496 | tf_op jit(solution)/shard_map/pallas_call | solution.py:474
  247.1 2.8 %shard_map.100 = bf16[1024,768]{1,0:T(8,128)(2,1)} custom-call(f32[1024,768]{1,0:T(8,128)S(1)} %shard_map.99.total_ref, bf16[384,768]{1,0:T(8,128)(2,1)S(1)} %copy-done.4, bf16[192,1024]{1,0:T(8,128)(2,1)S(1)} %collective-permute-done.16.first, bf16[192,1024]{1,0:T(8,128)(2,1)S(1)} %collective-permute-done.17.second), custom_call_target="tpu_custom_call" | custom-call | flops 603979776 | bytes 6094848 | tf_op jit(solution)/shard_map/pallas_call | solution.py:508
  249.9 3.8 %shard_map.102 = (bf16[128,3072]{1,0:T(8,128)(2,1)}, bf16[2,128]{1,0:T(2,128)(2,1)}) custom-call(s32[1]{0:T(128)} %bitcast.place_ref, s32[2,128]{1,0:T(2,128)S(1)} %bitcast.17, bf16[2,128]{1,0:T(2,128)(2,1)S(1)} %bitcast.19, bf16[512,2432]{1,0:T(8,128)(2,1)} %bitcast.10.ret_ref), custom_call_target="tpu_custom_call" | custom-call | flops 805306368 | bytes 3276800 | tf_op jit(solution)/shard_map/pallas_call | solution.py:441
  253.7 1.8 collective-permute-done.19.first
  255.5 3.7 %shard_map.103 = bf16[768,1024]{1,0:T(8,128)(2,1)} custom-call(f32[768,1024]{1,0:T(8,128)S(1)} %shard_map.101.total_ref, bf16[384,768]{1,0:T(8,128)(2,1)} %collective-permute-done.18.whole, bf16[192,1024]{1,0:T(8,128)(2,1)S(1)} %collective-permute-done.19.first, bf16[192,1024]{1,0:T(8,128)(2,1)} %collective-permute-done.20.second), custom_call_target="tpu_custom_call" | custom-call | flops 603979776 | bytes 6094848 | tf_op jit(solution)/shard_map/pallas_call | solution.py:508
  (73 shorter events, 17.8 us)
Async XLA Ops:
  3.2 12.3 %collective-permute-start.2 = (bf16[144,768]{1,0:T(8,128)(2,1)S(1)}, bf16[144,768]{1,0:T(8,128)(2,1)S(1)}, u32[]{:S(2)}, u32[]{:S(2)}) collective-permute-start(bf16[144,768]{1,0:T(8,128)(2,1)S(1)} %get-tuple-element.58), channel_id=1, source_target_pairs={{0,3},{1,0},{2,1},{3,2},{4,7},{5,4},{6,5},{7,6},{8,11},{9,8},{10,9... | collective-permute-start | bytes 663560 | tf_op jit(solution)/shard_map/ppermute | solution.py:524
  6.6 8.9 %collective-permute-start.3 = (bf16[144,768]{1,0:T(8,128)(2,1)S(1)}, bf16[144,768]{1,0:T(8,128)(2,1)S(1)}, u32[]{:S(2)}, u32[]{:S(2)}) collective-permute-start(bf16[144,768]{1,0:T(8,128)(2,1)S(1)} %get-tuple-element.59), channel_id=1, source_target_pairs={{0,2},{1,3},{2,0},{3,1},{4,6},{5,7},{6,4},{7,5},{8,10},{9,11},{10,... | collective-permute-start | bytes 663560 | tf_op jit(solution)/shard_map/ppermute | solution.py:524
  7.1 13.1 %collective-permute-start.4 = (bf16[144,768]{1,0:T(8,128)(2,1)S(1)}, bf16[144,768]{1,0:T(8,128)(2,1)S(1)}, u32[]{:S(2)}, u32[]{:S(2)}) collective-permute-start(bf16[144,768]{1,0:T(8,128)(2,1)S(1)} %get-tuple-element.60), channel_id=1, source_target_pairs={{0,1},{1,2},{2,3},{3,0},{4,5},{5,6},{6,7},{7,4},{8,9},{9,10},{10,1... | collective-permute-start | bytes 663560 | tf_op jit(solution)/shard_map/ppermute | solution.py:524
  22.6 67.3 %all-to-all-start.1 = ((bf16[64,8,2304]{2,1,0:T(8,128)(2,1)}), bf16[64,8,2304]{2,1,0:T(8,128)(2,1)S(1)}, u32[]{:S(2)}, u32[]{:S(2)}) async-start(bf16[64,8,2304]{2,1,0:T(8,128)(2,1)} %bitcast.6), calls=%async_computation.1 | async-start | bytes 4718592 | tf_op jit(solution)/shard_map/all_to_all | solution.py:543
  34.8 37.1 %collective-permute-start.1 = (bf16[768,1024]{1,0:T(8,128)(2,1)}, bf16[768,1024]{1,0:T(8,128)(2,1)}, u32[]{:S(2)}, u32[]{:S(2)}) collective-permute-start(bf16[768,1024]{1,0:T(8,128)(2,1)} %bitcast.26), channel_id=1, source_target_pairs={{0,1},{1,2},{2,3},{3,0},{4,5},{5,6},{6,7},{7,4},{8,9},{9,10},{10,1... | collective-permute-start | bytes 4718600 | tf_op jit(solution)/shard_map/ppermute | solution.py:524
  34.9 37.0 %collective-permute-start = (bf16[768,1024]{1,0:T(8,128)(2,1)}, bf16[768,1024]{1,0:T(8,128)(2,1)}, u32[]{:S(2)}, u32[]{:S(2)}) collective-permute-start(bf16[768,1024]{1,0:T(8,128)(2,1)} %bitcast.27), channel_id=1, source_target_pairs={{0,3},{1,0},{2,1},{3,2},{4,7},{5,4},{6,5},{7,6},{8,11},{9,8},{10,9... | collective-permute-start | bytes 4718600 | tf_op jit(solution)/shard_map/ppermute | solution.py:524
  91.4 64.3 %all-to-all-start = ((bf16[64,8,2304]{2,1,0:T(8,128)(2,1)}), bf16[64,8,2304]{2,1,0:T(8,128)(2,1)S(1)}, u32[]{:S(2)}, u32[]{:S(2)}) async-start(bf16[64,8,2304]{2,1,0:T(8,128)(2,1)} %bitcast.20), calls=%async_computation | async-start | bytes 4718592 | tf_op jit(solution)/shard_map/all_to_all | solution.py:543
  101.8 36.4 %collective-permute-start.8 = (bf16[384,1024]{1,0:T(8,128)(2,1)}, bf16[384,1024]{1,0:T(8,128)(2,1)}, u32[]{:S(2)}, u32[]{:S(2)}) collective-permute-start(bf16[384,1024]{1,0:T(8,128)(2,1)} %slice.18), channel_id=1, source_target_pairs={{0,1},{1,2},{2,3},{3,0},{4,5},{5,6},{6,7},{7,4},{8,9},{9,10},{10,1... | collective-permute-start | bytes 2359304 | tf_op jit(solution)/shard_map/ppermute | solution.py:524
  101.8 36.4 %collective-permute-start.9 = (bf16[384,1024]{1,0:T(8,128)(2,1)S(1)}, bf16[384,1024]{1,0:T(8,128)(2,1)}, u32[]{:S(2)}, u32[]{:S(2)}) collective-permute-start(bf16[384,1024]{1,0:T(8,128)(2,1)S(1)} %slice.19), channel_id=1, source_target_pairs={{0,3},{1,0},{2,1},{3,2},{4,7},{5,4},{6,5},{7,6},{8,11},{9,8},{10,9... | collective-permute-start | bytes 2359304 | tf_op jit(solution)/shard_map/ppermute | solution.py:524
  111.8 26.4 %collective-permute-start.5 = (bf16[384,1024]{1,0:T(8,128)(2,1)}, bf16[384,1024]{1,0:T(8,128)(2,1)S(1)}, u32[]{:S(2)}, u32[]{:S(2)}) collective-permute-start(bf16[384,1024]{1,0:T(8,128)(2,1)} %get-tuple-element.62), channel_id=1, source_target_pairs={{0,3},{1,0},{2,1},{3,2},{4,7},{5,4},{6,5},{7,6},{8,11},{9,8},{10,9... | collective-permute-start | bytes 2359304 | tf_op jit(solution)/shard_map/ppermute | solution.py:524
  111.9 26.4 %collective-permute-start.6 = (bf16[384,1024]{1,0:T(8,128)(2,1)}, bf16[384,1024]{1,0:T(8,128)(2,1)S(1)}, u32[]{:S(2)}, u32[]{:S(2)}) collective-permute-start(bf16[384,1024]{1,0:T(8,128)(2,1)} %get-tuple-element.63), channel_id=1, source_target_pairs={{0,2},{1,3},{2,0},{3,1},{4,6},{5,7},{6,4},{7,5},{8,10},{9,11},{10,... | collective-permute-start | bytes 2359304 | tf_op jit(solution)/shard_map/ppermute | solution.py:524
  112.4 43.3 %collective-permute-start.7 = (bf16[384,1024]{1,0:T(8,128)(2,1)}, bf16[384,1024]{1,0:T(8,128)(2,1)}, u32[]{:S(2)}, u32[]{:S(2)}) collective-permute-start(bf16[384,1024]{1,0:T(8,128)(2,1)} %get-tuple-element.64), channel_id=1, source_target_pairs={{0,1},{1,2},{2,3},{3,0},{4,5},{5,6},{6,7},{7,4},{8,9},{9,10},{10,1... | collective-permute-start | bytes 2359304 | tf_op jit(solution)/shard_map/ppermute | solution.py:524
  159.4 16.7 %collective-permute-start.11 = (bf16[384,768]{1,0:T(8,128)(2,1)}, bf16[384,768]{1,0:T(8,128)(2,1)S(1)}, u32[]{:S(2)}, u32[]{:S(2)}) collective-permute-start(bf16[384,768]{1,0:T(8,128)(2,1)} %get-tuple-element.70.x1), channel_id=1, source_target_pairs={{0,1},{1,2},{2,3},{3,0},{4,5},{5,6},{6,7},{7,4},{8,9},{9,10},{10,1... | collective-permute-start | bytes 1769480 | tf_op jit(solution)/shard_map/ppermute | solution.py:524
  160.6 16.3 %collective-permute-start.10 = (bf16[384,768]{1,0:T(8,128)(2,1)}, bf16[384,768]{1,0:T(8,128)(2,1)}, u32[]{:S(2)}, u32[]{:S(2)}) collective-permute-start(bf16[384,768]{1,0:T(8,128)(2,1)} %get-tuple-element.72.x3), channel_id=1, source_target_pairs={{0,3},{1,0},{2,1},{3,2},{4,7},{5,4},{6,5},{7,6},{8,11},{9,8},{10,9... | collective-permute-start | bytes 1769480 | tf_op jit(solution)/shard_map/ppermute | solution.py:524
  176.9 15.1 %copy-start = (bf16[384,1024]{1,0:T(8,128)(2,1)S(1)}, bf16[384,1024]{1,0:T(8,128)(2,1)}, u32[]{:S(2)}) copy-start(bf16[384,1024]{1,0:T(8,128)(2,1)} %get-tuple-element.96.r0) | copy-start | bytes 2359300
  177.0 36.6 %copy-start.5 = (bf16[384,768]{1,0:T(8,128)(2,1)S(1)}, bf16[384,768]{1,0:T(8,128)(2,1)}, u32[]{:S(2)}) copy-start(bf16[384,768]{1,0:T(8,128)(2,1)} %get-tuple-element.89.r0) | copy-start | bytes 1769476
  177.0 36.6 %copy-start.6 = (bf16[384,768]{1,0:T(8,128)(2,1)S(1)}, bf16[384,768]{1,0:T(8,128)(2,1)}, u32[]{:S(2)}) copy-start(bf16[384,768]{1,0:T(8,128)(2,1)} %get-tuple-element.90.r1) | copy-start | bytes 1769476
  177.0 36.6 %copy-start.7 = (bf16[384,768]{1,0:T(8,128)(2,1)S(1)}, bf16[384,768]{1,0:T(8,128)(2,1)}, u32[]{:S(2)}) copy-start(bf16[384,768]{1,0:T(8,128)(2,1)} %get-tuple-element.91.r3) | copy-start | bytes 1769476
  177.0 72.9 %all-to-all-start.2 = ((bf16[64,8,2432]{2,1,0:T(8,128)(2,1)}), bf16[64,8,2432]{2,1,0:T(8,128)(2,1)}, u32[]{:S(2)}, u32[]{:S(2)}) async-start(bf16[64,8,2432]{2,1,0:T(8,128)(2,1)} %bitcast.21), calls=%async_computation.2 | async-start | bytes 4980736 | tf_op jit(solution)/shard_map/all_to_all | solution.py:543
  189.3 20.0 %collective-permute-start.15 = (bf16[384,1024]{1,0:T(8,128)(2,1)S(1)}, bf16[384,1024]{1,0:T(8,128)(2,1)S(1)}, u32[]{:S(2)}, u32[]{:S(2)}) collective-permute-start(bf16[384,1024]{1,0:T(8,128)(2,1)S(1)} %copy-done.2), channel_id=1, source_target_pairs={{0,1},{1,2},{2,3},{3,0},{4,5},{5,6},{6,7},{7,4},{8,9},{9,10},{10,1... | collective-permute-start | bytes 2359304 | tf_op jit(solution)/shard_map/ppermute | solution.py:524
  189.4 19.9 %collective-permute-start.14 = (bf16[384,1024]{1,0:T(8,128)(2,1)S(1)}, bf16[384,1024]{1,0:T(8,128)(2,1)S(1)}, u32[]{:S(2)}, u32[]{:S(2)}) collective-permute-start(bf16[384,1024]{1,0:T(8,128)(2,1)S(1)} %copy-done.2), channel_id=1, source_target_pairs={{0,3},{1,0},{2,1},{3,2},{4,7},{5,4},{6,5},{7,6},{8,11},{9,8},{10,9... | collective-permute-start | bytes 2359304 | tf_op jit(solution)/shard_map/ppermute | solution.py:524
  192.0 34.1 %collective-permute-start.13 = (bf16[384,1024]{1,0:T(8,128)(2,1)S(1)}, bf16[384,1024]{1,0:T(8,128)(2,1)S(1)}, u32[]{:S(2)}, u32[]{:S(2)}) collective-permute-start(bf16[384,1024]{1,0:T(8,128)(2,1)S(1)} %copy-done), channel_id=1, source_target_pairs={{0,1},{1,2},{2,3},{3,0},{4,5},{5,6},{6,7},{7,4},{8,9},{9,10},{10,1... | collective-permute-start | bytes 2359304 | tf_op jit(solution)/shard_map/ppermute | solution.py:524
  192.0 34.1 %collective-permute-start.12 = (bf16[384,1024]{1,0:T(8,128)(2,1)S(1)}, bf16[384,1024]{1,0:T(8,128)(2,1)S(1)}, u32[]{:S(2)}, u32[]{:S(2)}) collective-permute-start(bf16[384,1024]{1,0:T(8,128)(2,1)S(1)} %copy-done), channel_id=1, source_target_pairs={{0,3},{1,0},{2,1},{3,2},{4,7},{5,4},{6,5},{7,6},{8,11},{9,8},{10,9... | collective-permute-start | bytes 2359304 | tf_op jit(solution)/shard_map/ppermute | solution.py:524
  209.3 46.2 %collective-permute-start.18 = (bf16[384,768]{1,0:T(8,128)(2,1)}, bf16[384,768]{1,0:T(8,128)(2,1)}, u32[]{:S(2)}, u32[]{:S(2)}) collective-permute-start(bf16[384,768]{1,0:T(8,128)(2,1)} %copy-done.16), channel_id=1, source_target_pairs={{0,2},{1,3},{2,0},{3,1},{4,6},{5,7},{6,4},{7,5},{8,10},{9,11},{10,... | collective-permute-start | bytes 1769480 | tf_op jit(solution)/shard_map/ppermute | solution.py:524
  210.8 36.3 %collective-permute-start.16 = (bf16[192,1024]{1,0:T(8,128)(2,1)S(1)}, bf16[192,1024]{1,0:T(8,128)(2,1)S(1)}, u32[]{:S(2)}, u32[]{:S(2)}) collective-permute-start(bf16[192,1024]{1,0:T(8,128)(2,1)S(1)} %slice.20), channel_id=1, source_target_pairs={{0,1},{1,2},{2,3},{3,0},{4,5},{5,6},{6,7},{7,4},{8,9},{9,10},{10,1... | collective-permute-start | bytes 1179656 | tf_op jit(solution)/shard_map/ppermute | solution.py:524
  212.3 34.7 %collective-permute-start.17 = (bf16[192,1024]{1,0:T(8,128)(2,1)S(1)}, bf16[192,1024]{1,0:T(8,128)(2,1)S(1)}, u32[]{:S(2)}, u32[]{:S(2)}) collective-permute-start(bf16[192,1024]{1,0:T(8,128)(2,1)S(1)} %slice.21), channel_id=1, source_target_pairs={{0,3},{1,0},{2,1},{3,2},{4,7},{5,4},{6,5},{7,6},{8,11},{9,8},{10,9... | collective-permute-start | bytes 1179656 | tf_op jit(solution)/shard_map/ppermute | solution.py:524
  213.5 28.0 %copy-start.1 = (bf16[384,1024]{1,0:T(8,128)(2,1)S(1)}, bf16[384,1024]{1,0:T(8,128)(2,1)}, u32[]{:S(2)}) copy-start(bf16[384,1024]{1,0:T(8,128)(2,1)} %get-tuple-element.96.r0) | copy-start | bytes 2359300
  213.5 28.0 %copy-start.9 = (bf16[384,768]{1,0:T(8,128)(2,1)S(1)}, bf16[384,768]{1,0:T(8,128)(2,1)}, u32[]{:S(2)}) copy-start(bf16[384,768]{1,0:T(8,128)(2,1)} %copy-done.8) | copy-start | bytes 1769476
  213.5 28.0 %copy-start.11 = (bf16[384,768]{1,0:T(8,128)(2,1)S(1)}, bf16[384,768]{1,0:T(8,128)(2,1)}, u32[]{:S(2)}) copy-start(bf16[384,768]{1,0:T(8,128)(2,1)} %copy-done.10) | copy-start | bytes 1769476
  227.7 19.4 %copy-start.4 = (bf16[384,768]{1,0:T(8,128)(2,1)S(1)}, bf16[384,768]{1,0:T(8,128)(2,1)}, u32[]{:S(2)}) copy-start(bf16[384,768]{1,0:T(8,128)(2,1)} %get-tuple-element.93.whole) | copy-start | bytes 1769476
  227.7 27.8 %collective-permute-start.19 = (bf16[192,1024]{1,0:T(8,128)(2,1)}, bf16[192,1024]{1,0:T(8,128)(2,1)S(1)}, u32[]{:S(2)}, u32[]{:S(2)}) collective-permute-start(bf16[192,1024]{1,0:T(8,128)(2,1)} %slice.22), channel_id=1, source_target_pairs={{0,1},{1,2},{2,3},{3,0},{4,5},{5,6},{6,7},{7,4},{8,9},{9,10},{10,1... | collective-permute-start | bytes 1179656 | tf_op jit(solution)/shard_map/ppermute | solution.py:524
  227.7 27.8 %collective-permute-start.20 = (bf16[192,1024]{1,0:T(8,128)(2,1)}, bf16[192,1024]{1,0:T(8,128)(2,1)}, u32[]{:S(2)}, u32[]{:S(2)}) collective-permute-start(bf16[192,1024]{1,0:T(8,128)(2,1)} %slice.23), channel_id=1, source_target_pairs={{0,3},{1,0},{2,1},{3,2},{4,7},{5,4},{6,5},{7,6},{8,11},{9,8},{10,9... | collective-permute-start | bytes 1179656 | tf_op jit(solution)/shard_map/ppermute | solution.py:524
  (12 other events, 26.1 us)

commit v5 on v4

--- a/solution.py
+++ b/solution.py
@@ -429,11 +429,14 @@
         last += dot(pick, got)
     put(3, last)
     extra = ret_ref[:, 3 * block :]
+    choice = iota((2, count), 0)
+    out = jnp.zeros((2, count), F32)
     for k in range(2):
         pair = dot(hits[k], extra)
         score = pair[:, 0:1] + pair[:, 1:2]
         row = jnp.sum(jnp.where(eye, score, 0.0), axis=0, keepdims=True)
-        droute_ref[k : k + 1, :] = (row / weight_ref[k : k + 1, :].astype(F32)).astype(BF16)
+        out = jnp.where(choice == k, row, out)
+    droute_ref[...] = (out / weight_ref[...].astype(F32)).astype(BF16)
 
 
 def combine(place, ids, weight, ret, count, width):
@@ -569,11 +572,11 @@
     h0, h1, h2a, h2b, h3 = far(hidden_near)
     t2 = shift(far_tokens, 2)
     down_near = outer_near((h0, h1, h3), (g0, g1, g3))
-    grads_near, down_near = lax.optimization_barrier((near(hidden_grad), down_near))
+    grad_down = outer_last(True, down_near, g2, h2a, h2b)
+    grads_near, grad_down = lax.optimization_barrier((near(hidden_grad), grad_down))
     d0, d1, d2a, d2b, d3 = far(grads_near)
     up_near = outer_near((wholes[0], t1, t3), (d0, d1, d3))
-    grad_down = outer_last(True, down_near, g2, h2a, h2b)
-    back, grad_down, up_near = lax.optimization_barrier((back, grad_down, up_near))
+    back, up_near = lax.optimization_barrier((back, up_near))
     d_tokens, d_route = combine(place, ids, weight, back, count, width)
     up_near, d_tokens, d_route = lax.optimization_barrier((up_near, d_tokens, d_route))
     grad_up = outer_last(False, up_near, t2, d2a, d2b)

time: 260 us -> 267 us (1.027)
  waiting for transfers between devices: 129 us -> 135 us
    ppermute x21, waiting for transfers between devices: 111 us -> 117 us  [shift(): lax.ppermute(values, 'cross', [(i, (i + by) % count) for i in range(count)])]
  transfers between devices with their start and end apart: 24 -> 24, of which waited for: 11 -> 9; matrix products, arithmetic and copies ran while one was open for 2% -> 2% of each run, Pallas kernels for 15% -> 14%
where the time goes in v5:
time: 267 us; the launch traced here: 264 us
  waiting for transfers between devices  135 us (51%)
  starting transfers between devices  69.6 us (26%)
  Pallas kernels  46 us (17%)
  local copies, waits for them, and re-layouts  13.1 us (5%)
    ppermute x21, waiting for transfers between devices, shift(): lax.ppermute(values, 'cross', [(i, (i + by) % count) for i in range(count)])  117 us
    ppermute x21, starting transfers between devices, shift(): lax.ppermute(values, 'cross', [(i, (i + by) % count) for i in range(count)])  38 us
    all_to_all x3, starting transfers between devices, exchange(): lax.all_to_all(blocks, 'expert', split_axis=0, concat_axis=0, tiled=True)  31.6 us
    all_to_all x3, waiting for transfers between devices, exchange(): lax.all_to_all(blocks, 'expert', split_axis=0, concat_axis=0, tiled=True)  18 us
    pallas_call x1, Pallas kernels, expert(): pl.pallas_call(expert_body, out_shape=[jax.ShapeDtypeStruct((rows, hidden...  12.8 us
    unnamed x40, local copies, waits for them, and re-layouts  8.23 us
    pallas_call x1, Pallas kernels, project(): pl.pallas_call(project_body, out_shape=[jax.ShapeDtypeStruct((rows, block...  7.34 us
    pallas_call x2, Pallas kernels, outer_near(): pl.pallas_call(near_body, out_shape=jax.ShapeDtypeStruct(shape, F32), in_...  7.33 us
  transfers between devices with their start and end apart: 24, of which 9 were waited for; matrix products, arithmetic and copies ran while one was open for 2% of the time, Pallas kernels for 14%

profile of v5, /device:TPU:1, one launch (start us, length us, event | category | flops | bytes accessed | tf_op | source)
XLA Modules:
  0.0 264.3 jit_solution(5248674542683772779)
XLA Ops:
  3.2 3.4 %collective-permute-start.2 = (bf16[144,768]{1,0:T(8,128)(2,1)S(1)}, bf16[144,768]{1,0:T(8,128)(2,1)S(1)}, u32[]{:S(2)}, u32[]{:S(2)}) collective-permute-start(bf16[144,768]{1,0:T(8,128)(2,1)S(1)} %get-tuple-element.57), channel_id=1, source_target_pairs={{0,3},{1,0},{2,1},{3,2},{4,7},{5,4},{6,5},{7,6},{8,11},{9,8},{10,9... | collective-permute-start | bytes 663560 | tf_op jit(solution)/shard_map/ppermute | solution.py:527
  7.7 7.8 %collective-permute-done.2.s1 = bf16[144,768]{1,0:T(8,128)(2,1)S(1)} collective-permute-done((bf16[144,768]{1,0:T(8,128)(2,1)S(1)}, bf16[144,768]{1,0:T(8,128)(2,1)S(1)}, u32[]{:S(2)}, u32[]{:S(2)}) %collective-permute-start.2) | collective-permute-done | bytes 221216 | tf_op jit(solution)/shard_map/ppermute | solution.py:527
  15.4 4.7 %collective-permute-done.4.s3 = bf16[144,768]{1,0:T(8,128)(2,1)S(1)} collective-permute-done((bf16[144,768]{1,0:T(8,128)(2,1)S(1)}, bf16[144,768]{1,0:T(8,128)(2,1)S(1)}, u32[]{:S(2)}, u32[]{:S(2)}) %collective-permute-start.4) | collective-permute-done | bytes 221216 | tf_op jit(solution)/shard_map/ppermute | solution.py:527
  20.1 2.5 shard_map.95
  22.6 12.1 %all-to-all-start.1 = ((bf16[64,8,2304]{2,1,0:T(8,128)(2,1)}), bf16[64,8,2304]{2,1,0:T(8,128)(2,1)S(1)}, u32[]{:S(2)}, u32[]{:S(2)}) async-start(bf16[64,8,2304]{2,1,0:T(8,128)(2,1)} %bitcast.6), calls=%async_computation.1 | async-start | bytes 4718592 | tf_op jit(solution)/shard_map/all_to_all | solution.py:546
  34.9 2.7 %collective-permute-start = (bf16[768,1024]{1,0:T(8,128)(2,1)}, bf16[768,1024]{1,0:T(8,128)(2,1)}, u32[]{:S(2)}, u32[]{:S(2)}) collective-permute-start(bf16[768,1024]{1,0:T(8,128)(2,1)} %bitcast.27), channel_id=1, source_target_pairs={{0,3},{1,0},{2,1},{3,2},{4,7},{5,4},{6,5},{7,6},{8,11},{9,8},{10,9... | collective-permute-start | bytes 4718600 | tf_op jit(solution)/shard_map/ppermute | solution.py:527
  37.5 3.7 %shard_map.93 = bf16[512,2304]{1,0:T(8,128)(2,1)} custom-call(s32[1]{0:T(128)} %bitcast.place_ref, s32[2,128]{1,0:T(2,128)} %bitcast.15, bf16[128,3072]{1,0:T(8,128)(2,1)} %values_ref.2), custom_call_target="tpu_custom_call" | custom-call | flops 603979776 | bytes 3145728 | tf_op jit(solution)/shard_map/pallas_call | solution.py:100
  41.2 30.7 %collective-permute-done.1.up3 = bf16[768,1024]{1,0:T(8,128)(2,1)} collective-permute-done((bf16[768,1024]{1,0:T(8,128)(2,1)}, bf16[768,1024]{1,0:T(8,128)(2,1)}, u32[]{:S(2)}, u32[]{:S(2)}) %collective-permute-start.1) | collective-permute-done | bytes 1572896 | tf_op jit(solution)/shard_map/ppermute | solution.py:527
  71.9 18.0 %all-to-all-done.1 = bf16[64,8,2304]{2,1,0:T(8,128)(2,1)S(1)} async-done(((bf16[64,8,2304]{2,1,0:T(8,128)(2,1)}), bf16[64,8,2304]{2,1,0:T(8,128)(2,1)S(1)}, u32[]{:S(2)}, u32[]{:S(2)}) %all-to-all-start.1) | async-done | bytes 2359328 | tf_op jit(solution)/shard_map/all_to_all | solution.py:546
  90.0 1.5 copy-done.17
  91.4 7.1 %all-to-all-start = ((bf16[64,8,2304]{2,1,0:T(8,128)(2,1)}), bf16[64,8,2304]{2,1,0:T(8,128)(2,1)S(1)}, u32[]{:S(2)}, u32[]{:S(2)}) async-start(bf16[64,8,2304]{2,1,0:T(8,128)(2,1)} %bitcast.20), calls=%async_computation | async-start | bytes 4718592 | tf_op jit(solution)/shard_map/all_to_all | solution.py:546
  99.8 2.1 slice.18
  101.8 2.7 %collective-permute-start.9 = (bf16[384,1024]{1,0:T(8,128)(2,1)S(1)}, bf16[384,1024]{1,0:T(8,128)(2,1)}, u32[]{:S(2)}, u32[]{:S(2)}) collective-permute-start(bf16[384,1024]{1,0:T(8,128)(2,1)S(1)} %slice.19), channel_id=1, source_target_pairs={{0,3},{1,0},{2,1},{3,2},{4,7},{5,4},{6,5},{7,6},{8,11},{9,8},{10,9... | collective-permute-start | bytes 2359304 | tf_op jit(solution)/shard_map/ppermute | solution.py:527
  104.5 7.3 %shard_map.96 = (bf16[384,768]{1,0:T(8,128)(2,1)}, bf16[384,768]{1,0:T(8,128)(2,1)}, bf16[384,768]{1,0:T(8,128)(2,1)}, bf16[384,768]{1,0:T(8,128)(2,1)}, f32[384...) custom-call(bf16[512,2304]{1,0:T(8,128)(2,1)} %bitcast.22, ...), custom_call_target="tpu_custom_call" | custom-call | flops 3019898880 | bytes 8257536 | tf_op jit(solution)/shard_map/pallas_call | solution.py:244
  113.3 24.9 %collective-permute-done.8.up2a = bf16[384,1024]{1,0:T(8,128)(2,1)} collective-permute-done((bf16[384,1024]{1,0:T(8,128)(2,1)}, bf16[384,1024]{1,0:T(8,128)(2,1)}, u32[]{:S(2)}, u32[]{:S(2)}) %collective-permute-start.8) | collective-permute-done | bytes 786464 | tf_op jit(solution)/shard_map/ppermute | solution.py:527
  140.0 15.7 %collective-permute-done.7.b3 = bf16[384,1024]{1,0:T(8,128)(2,1)} collective-permute-done((bf16[384,1024]{1,0:T(8,128)(2,1)}, bf16[384,1024]{1,0:T(8,128)(2,1)}, u32[]{:S(2)}, u32[]{:S(2)}) %collective-permute-start.7) | collective-permute-done | bytes 786464 | tf_op jit(solution)/shard_map/ppermute | solution.py:527
  155.7 2.0 shard_map.97
  159.4 1.2 collective-permute-start.11
  160.6 2.7 %collective-permute-start.10 = (bf16[384,768]{1,0:T(8,128)(2,1)}, bf16[384,768]{1,0:T(8,128)(2,1)}, u32[]{:S(2)}, u32[]{:S(2)}) collective-permute-start(bf16[384,768]{1,0:T(8,128)(2,1)} %get-tuple-element.71.x3), channel_id=1, source_target_pairs={{0,3},{1,0},{2,1},{3,2},{4,7},{5,4},{6,5},{7,6},{8,11},{9,8},{10,9... | collective-permute-start | bytes 1769480 | tf_op jit(solution)/shard_map/ppermute | solution.py:527
  163.3 12.8 %shard_map.98 = (bf16[384,1024]{1,0:T(8,128)(2,1)}, bf16[384,1024]{1,0:T(8,128)(2,1)}, bf16[512,2432]{1,0:T(8,128)(2,1)}) custom-call(bf16[384,768]{1,0:T(8,128)(2,1)} %copy-done.8, bf16[384,768]{1,0:T(8,128)(2,1)} %get-tuple-element.69.x1, bf16[384,768]{1,0:T(8,128)(2,1)} %copy-done.16, bf16[384,768]{1,0:T(8,128)(2,1)} %get-tuple-element.71.x3, ...), custom_call_target="tpu_custom_call" | custom-call | flops 6039797760 | bytes 18874368 | tf_op jit(solution)/shard_map/pallas_call | solution.py:376
  176.9 12.3 %all-to-all-start.2 = ((bf16[64,8,2432]{2,1,0:T(8,128)(2,1)}), bf16[64,8,2432]{2,1,0:T(8,128)(2,1)}, u32[]{:S(2)}, u32[]{:S(2)}) async-start(bf16[64,8,2432]{2,1,0:T(8,128)(2,1)} %bitcast.21), calls=%async_computation.2 | async-start | bytes 4980736 | tf_op jit(solution)/shard_map/all_to_all | solution.py:546
  189.3 2.6 collective-permute-start.14
  192.0 2.7 %collective-permute-start.12 = (bf16[384,1024]{1,0:T(8,128)(2,1)S(1)}, bf16[384,1024]{1,0:T(8,128)(2,1)S(1)}, u32[]{:S(2)}, u32[]{:S(2)}) collective-permute-start(bf16[384,1024]{1,0:T(8,128)(2,1)S(1)} %copy-done), channel_id=1, source_target_pairs={{0,3},{1,0},{2,1},{3,2},{4,7},{5,4},{6,5},{7,6},{8,11},{9,8},{10,9... | collective-permute-start | bytes 2359304 | tf_op jit(solution)/shard_map/ppermute | solution.py:527
  194.6 14.5 %collective-permute-done.15.l3 = bf16[384,1024]{1,0:T(8,128)(2,1)S(1)} collective-permute-done((bf16[384,1024]{1,0:T(8,128)(2,1)S(1)}, bf16[384,1024]{1,0:T(8,128)(2,1)S(1)}, u32[]{:S(2)}, u32[]{:S(2)}) %collective-permute-start.15) | collective-permute-done | bytes 786464 | tf_op jit(solution)/shard_map/ppermute | solution.py:527
  209.3 2.7 %collective-permute-start.17 = (bf16[192,1024]{1,0:T(8,128)(2,1)S(1)}, bf16[192,1024]{1,0:T(8,128)(2,1)S(1)}, u32[]{:S(2)}, u32[]{:S(2)}) collective-permute-start(bf16[192,1024]{1,0:T(8,128)(2,1)S(1)} %slice.21), channel_id=1, source_target_pairs={{0,3},{1,0},{2,1},{3,2},{4,7},{5,4},{6,5},{7,6},{8,11},{9,8},{10,9... | collective-permute-start | bytes 1179656 | tf_op jit(solution)/shard_map/ppermute | solution.py:527
  212.9 3.2 %shard_map.99.total_ref = f32[1024,768]{1,0:T(8,128)S(1)} custom-call(bf16[384,1024]{1,0:T(8,128)(2,1)S(1)} %copy-done.2, bf16[384,1024]{1,0:T(8,128)(2,1)S(1)} %collective-permute-done.14.l1, bf16[384,1024]{1,0:T(8,128)(2,1)S(1)} %collective-permute-done.15.l3, bf16[384,768]{1,0:T(8,128)(2,1)S(1)} %copy-done.5, bf16[384,768]{1,0:T(8,128)(2,1)S(1)} %copy-done.6, ...), custom_call_target="tpu_custom_call" | custom-call | flops 1811939328 | bytes 7274496 | tf_op jit(solution)/shard_map/pallas_call | solution.py:477
  216.1 18.3 %collective-permute-done.16.first = bf16[192,1024]{1,0:T(8,128)(2,1)S(1)} collective-permute-done((bf16[192,1024]{1,0:T(8,128)(2,1)S(1)}, bf16[192,1024]{1,0:T(8,128)(2,1)S(1)}, u32[]{:S(2)}, u32[]{:S(2)}) %collective-permute-start.16) | collective-permute-done | bytes 393248 | tf_op jit(solution)/shard_map/ppermute | solution.py:527
  234.5 2.8 %shard_map.100 = bf16[1024,768]{1,0:T(8,128)(2,1)} custom-call(f32[1024,768]{1,0:T(8,128)S(1)} %shard_map.99.total_ref, bf16[384,768]{1,0:T(8,128)(2,1)S(1)} %copy-done.4, bf16[192,1024]{1,0:T(8,128)(2,1)S(1)} %collective-permute-done.16.first, bf16[192,1024]{1,0:T(8,128)(2,1)S(1)} %collective-permute-done.17.second), custom_call_target="tpu_custom_call" | custom-call | flops 603979776 | bytes 6094848 | tf_op jit(solution)/shard_map/pallas_call | solution.py:511
  238.8 13.8 %collective-permute-start.20 = (bf16[192,1024]{1,0:T(8,128)(2,1)}, bf16[192,1024]{1,0:T(8,128)(2,1)}, u32[]{:S(2)}, u32[]{:S(2)}) collective-permute-start(bf16[192,1024]{1,0:T(8,128)(2,1)} %slice.23), channel_id=1, source_target_pairs={{0,3},{1,0},{2,1},{3,2},{4,7},{5,4},{6,5},{7,6},{8,11},{9,8},{10,9... | collective-permute-start | bytes 1179656 | tf_op jit(solution)/shard_map/ppermute | solution.py:527
  252.6 4.1 %shard_map.101.total_ref = f32[768,1024]{1,0:T(8,128)S(1)} custom-call(bf16[384,768]{1,0:T(8,128)(2,1)S(1)} %copy-done.9, bf16[384,768]{1,0:T(8,128)(2,1)} %collective-permute-done.10.l1, bf16[384,768]{1,0:T(8,128)(2,1)S(1)} %copy-done.11, bf16[384,1024]{1,0:T(8,128)(2,1)S(1)} %copy-done.1, bf16[384,1024]{1,0:T(8,128)(2,1)S(1)} %collective-permute-done.12.r1, ...), custom_call_target="tpu_custom_call" | custom-call | flops 1811939328 | bytes 7274496 | tf_op jit(solution)/shard_map/pallas_call | solution.py:477
  256.7 3.8 %shard_map.102 = (bf16[128,3072]{1,0:T(8,128)(2,1)}, bf16[2,128]{1,0:T(2,128)(2,1)}) custom-call(s32[1]{0:T(128)} %bitcast.place_ref, s32[2,128]{1,0:T(2,128)S(1)} %bitcast.17, bf16[2,128]{1,0:T(2,128)(2,1)S(1)} %bitcast.19, bf16[512,2432]{1,0:T(8,128)(2,1)} %bitcast.10.ret_ref), custom_call_target="tpu_custom_call" | custom-call | flops 805306368 | bytes 3276800 | tf_op jit(solution)/shard_map/pallas_call | solution.py:444
  260.5 3.7 %shard_map.103 = bf16[768,1024]{1,0:T(8,128)(2,1)} custom-call(f32[768,1024]{1,0:T(8,128)S(1)} %shard_map.101.total_ref, bf16[384,768]{1,0:T(8,128)(2,1)} %collective-permute-done.18.whole, bf16[192,1024]{1,0:T(8,128)(2,1)S(1)} %collective-permute-done.19.first, bf16[192,1024]{1,0:T(8,128)(2,1)} %collective-permute-done.20.second), custom_call_target="tpu_custom_call" | custom-call | flops 603979776 | bytes 6094848 | tf_op jit(solution)/shard_map/pallas_call | solution.py:511
  (73 shorter events, 13.5 us)
Async XLA Ops:
  3.2 12.3 %collective-permute-start.2 = (bf16[144,768]{1,0:T(8,128)(2,1)S(1)}, bf16[144,768]{1,0:T(8,128)(2,1)S(1)}, u32[]{:S(2)}, u32[]{:S(2)}) collective-permute-start(bf16[144,768]{1,0:T(8,128)(2,1)S(1)} %get-tuple-element.57), channel_id=1, source_target_pairs={{0,3},{1,0},{2,1},{3,2},{4,7},{5,4},{6,5},{7,6},{8,11},{9,8},{10,9... | collective-permute-start | bytes 663560 | tf_op jit(solution)/shard_map/ppermute | solution.py:527
  6.6 8.9 %collective-permute-start.3 = (bf16[144,768]{1,0:T(8,128)(2,1)S(1)}, bf16[144,768]{1,0:T(8,128)(2,1)S(1)}, u32[]{:S(2)}, u32[]{:S(2)}) collective-permute-start(bf16[144,768]{1,0:T(8,128)(2,1)S(1)} %get-tuple-element.58), channel_id=1, source_target_pairs={{0,2},{1,3},{2,0},{3,1},{4,6},{5,7},{6,4},{7,5},{8,10},{9,11},{10,... | collective-permute-start | bytes 663560 | tf_op jit(solution)/shard_map/ppermute | solution.py:527
  7.1 13.1 %collective-permute-start.4 = (bf16[144,768]{1,0:T(8,128)(2,1)S(1)}, bf16[144,768]{1,0:T(8,128)(2,1)S(1)}, u32[]{:S(2)}, u32[]{:S(2)}) collective-permute-start(bf16[144,768]{1,0:T(8,128)(2,1)S(1)} %get-tuple-element.59), channel_id=1, source_target_pairs={{0,1},{1,2},{2,3},{3,0},{4,5},{5,6},{6,7},{7,4},{8,9},{9,10},{10,1... | collective-permute-start | bytes 663560 | tf_op jit(solution)/shard_map/ppermute | solution.py:527
  22.6 67.3 %all-to-all-start.1 = ((bf16[64,8,2304]{2,1,0:T(8,128)(2,1)}), bf16[64,8,2304]{2,1,0:T(8,128)(2,1)S(1)}, u32[]{:S(2)}, u32[]{:S(2)}) async-start(bf16[64,8,2304]{2,1,0:T(8,128)(2,1)} %bitcast.6), calls=%async_computation.1 | async-start | bytes 4718592 | tf_op jit(solution)/shard_map/all_to_all | solution.py:546
  34.8 37.1 %collective-permute-start.1 = (bf16[768,1024]{1,0:T(8,128)(2,1)}, bf16[768,1024]{1,0:T(8,128)(2,1)}, u32[]{:S(2)}, u32[]{:S(2)}) collective-permute-start(bf16[768,1024]{1,0:T(8,128)(2,1)} %bitcast.26), channel_id=1, source_target_pairs={{0,1},{1,2},{2,3},{3,0},{4,5},{5,6},{6,7},{7,4},{8,9},{9,10},{10,1... | collective-permute-start | bytes 4718600 | tf_op jit(solution)/shard_map/ppermute | solution.py:527
  34.9 37.0 %collective-permute-start = (bf16[768,1024]{1,0:T(8,128)(2,1)}, bf16[768,1024]{1,0:T(8,128)(2,1)}, u32[]{:S(2)}, u32[]{:S(2)}) collective-permute-start(bf16[768,1024]{1,0:T(8,128)(2,1)} %bitcast.27), channel_id=1, source_target_pairs={{0,3},{1,0},{2,1},{3,2},{4,7},{5,4},{6,5},{7,6},{8,11},{9,8},{10,9... | collective-permute-start | bytes 4718600 | tf_op jit(solution)/shard_map/ppermute | solution.py:527
  91.4 64.3 %all-to-all-start = ((bf16[64,8,2304]{2,1,0:T(8,128)(2,1)}), bf16[64,8,2304]{2,1,0:T(8,128)(2,1)S(1)}, u32[]{:S(2)}, u32[]{:S(2)}) async-start(bf16[64,8,2304]{2,1,0:T(8,128)(2,1)} %bitcast.20), calls=%async_computation | async-start | bytes 4718592 | tf_op jit(solution)/shard_map/all_to_all | solution.py:546
  101.8 36.4 %collective-permute-start.8 = (bf16[384,1024]{1,0:T(8,128)(2,1)}, bf16[384,1024]{1,0:T(8,128)(2,1)}, u32[]{:S(2)}, u32[]{:S(2)}) collective-permute-start(bf16[384,1024]{1,0:T(8,128)(2,1)} %slice.18), channel_id=1, source_target_pairs={{0,1},{1,2},{2,3},{3,0},{4,5},{5,6},{6,7},{7,4},{8,9},{9,10},{10,1... | collective-permute-start | bytes 2359304 | tf_op jit(solution)/shard_map/ppermute | solution.py:527
  101.8 36.4 %collective-permute-start.9 = (bf16[384,1024]{1,0:T(8,128)(2,1)S(1)}, bf16[384,1024]{1,0:T(8,128)(2,1)}, u32[]{:S(2)}, u32[]{:S(2)}) collective-permute-start(bf16[384,1024]{1,0:T(8,128)(2,1)S(1)} %slice.19), channel_id=1, source_target_pairs={{0,3},{1,0},{2,1},{3,2},{4,7},{5,4},{6,5},{7,6},{8,11},{9,8},{10,9... | collective-permute-start | bytes 2359304 | tf_op jit(solution)/shard_map/ppermute | solution.py:527
  111.8 26.4 %collective-permute-start.5 = (bf16[384,1024]{1,0:T(8,128)(2,1)}, bf16[384,1024]{1,0:T(8,128)(2,1)S(1)}, u32[]{:S(2)}, u32[]{:S(2)}) collective-permute-start(bf16[384,1024]{1,0:T(8,128)(2,1)} %get-tuple-element.61), channel_id=1, source_target_pairs={{0,3},{1,0},{2,1},{3,2},{4,7},{5,4},{6,5},{7,6},{8,11},{9,8},{10,9... | collective-permute-start | bytes 2359304 | tf_op jit(solution)/shard_map/ppermute | solution.py:527
  111.9 26.4 %collective-permute-start.6 = (bf16[384,1024]{1,0:T(8,128)(2,1)}, bf16[384,1024]{1,0:T(8,128)(2,1)S(1)}, u32[]{:S(2)}, u32[]{:S(2)}) collective-permute-start(bf16[384,1024]{1,0:T(8,128)(2,1)} %get-tuple-element.62), channel_id=1, source_target_pairs={{0,2},{1,3},{2,0},{3,1},{4,6},{5,7},{6,4},{7,5},{8,10},{9,11},{10,... | collective-permute-start | bytes 2359304 | tf_op jit(solution)/shard_map/ppermute | solution.py:527
  112.4 43.3 %collective-permute-start.7 = (bf16[384,1024]{1,0:T(8,128)(2,1)}, bf16[384,1024]{1,0:T(8,128)(2,1)}, u32[]{:S(2)}, u32[]{:S(2)}) collective-permute-start(bf16[384,1024]{1,0:T(8,128)(2,1)} %get-tuple-element.63), channel_id=1, source_target_pairs={{0,1},{1,2},{2,3},{3,0},{4,5},{5,6},{6,7},{7,4},{8,9},{9,10},{10,1... | collective-permute-start | bytes 2359304 | tf_op jit(solution)/shard_map/ppermute | solution.py:527
  159.4 16.6 %collective-permute-start.11 = (bf16[384,768]{1,0:T(8,128)(2,1)}, bf16[384,768]{1,0:T(8,128)(2,1)S(1)}, u32[]{:S(2)}, u32[]{:S(2)}) collective-permute-start(bf16[384,768]{1,0:T(8,128)(2,1)} %get-tuple-element.69.x1), channel_id=1, source_target_pairs={{0,1},{1,2},{2,3},{3,0},{4,5},{5,6},{6,7},{7,4},{8,9},{9,10},{10,1... | collective-permute-start | bytes 1769480 | tf_op jit(solution)/shard_map/ppermute | solution.py:527
  160.6 16.3 %collective-permute-start.10 = (bf16[384,768]{1,0:T(8,128)(2,1)}, bf16[384,768]{1,0:T(8,128)(2,1)}, u32[]{:S(2)}, u32[]{:S(2)}) collective-permute-start(bf16[384,768]{1,0:T(8,128)(2,1)} %get-tuple-element.71.x3), channel_id=1, source_target_pairs={{0,3},{1,0},{2,1},{3,2},{4,7},{5,4},{6,5},{7,6},{8,11},{9,8},{10,9... | collective-permute-start | bytes 1769480 | tf_op jit(solution)/shard_map/ppermute | solution.py:527
  176.9 36.0 %copy-start.5 = (bf16[384,768]{1,0:T(8,128)(2,1)S(1)}, bf16[384,768]{1,0:T(8,128)(2,1)}, u32[]{:S(2)}) copy-start(bf16[384,768]{1,0:T(8,128)(2,1)} %get-tuple-element.90.r0) | copy-start | bytes 1769476
  176.9 36.0 %copy-start.6 = (bf16[384,768]{1,0:T(8,128)(2,1)S(1)}, bf16[384,768]{1,0:T(8,128)(2,1)}, u32[]{:S(2)}) copy-start(bf16[384,768]{1,0:T(8,128)(2,1)} %get-tuple-element.91.r1) | copy-start | bytes 1769476
  176.9 36.0 %copy-start.7 = (bf16[384,768]{1,0:T(8,128)(2,1)S(1)}, bf16[384,768]{1,0:T(8,128)(2,1)}, u32[]{:S(2)}) copy-start(bf16[384,768]{1,0:T(8,128)(2,1)} %get-tuple-element.92.r3) | copy-start | bytes 1769476
  176.9 79.8 %all-to-all-start.2 = ((bf16[64,8,2432]{2,1,0:T(8,128)(2,1)}), bf16[64,8,2432]{2,1,0:T(8,128)(2,1)}, u32[]{:S(2)}, u32[]{:S(2)}) async-start(bf16[64,8,2432]{2,1,0:T(8,128)(2,1)} %bitcast.21), calls=%async_computation.2 | async-start | bytes 4980736 | tf_op jit(solution)/shard_map/all_to_all | solution.py:546
  189.2 20.0 %collective-permute-start.15 = (bf16[384,1024]{1,0:T(8,128)(2,1)S(1)}, bf16[384,1024]{1,0:T(8,128)(2,1)S(1)}, u32[]{:S(2)}, u32[]{:S(2)}) collective-permute-start(bf16[384,1024]{1,0:T(8,128)(2,1)S(1)} %copy-done.2), channel_id=1, source_target_pairs={{0,1},{1,2},{2,3},{3,0},{4,5},{5,6},{6,7},{7,4},{8,9},{9,10},{10,1... | collective-permute-start | bytes 2359304 | tf_op jit(solution)/shard_map/ppermute | solution.py:527
  189.3 19.9 %collective-permute-start.14 = (bf16[384,1024]{1,0:T(8,128)(2,1)S(1)}, bf16[384,1024]{1,0:T(8,128)(2,1)S(1)}, u32[]{:S(2)}, u32[]{:S(2)}) collective-permute-start(bf16[384,1024]{1,0:T(8,128)(2,1)S(1)} %copy-done.2), channel_id=1, source_target_pairs={{0,3},{1,0},{2,1},{3,2},{4,7},{5,4},{6,5},{7,6},{8,11},{9,8},{10,9... | collective-permute-start | bytes 2359304 | tf_op jit(solution)/shard_map/ppermute | solution.py:527
  192.0 45.3 %collective-permute-start.13 = (bf16[384,1024]{1,0:T(8,128)(2,1)S(1)}, bf16[384,1024]{1,0:T(8,128)(2,1)S(1)}, u32[]{:S(2)}, u32[]{:S(2)}) collective-permute-start(bf16[384,1024]{1,0:T(8,128)(2,1)S(1)} %copy-done), channel_id=1, source_target_pairs={{0,1},{1,2},{2,3},{3,0},{4,5},{5,6},{6,7},{7,4},{8,9},{9,10},{10,1... | collective-permute-start | bytes 2359304 | tf_op jit(solution)/shard_map/ppermute | solution.py:527
  192.0 45.3 %collective-permute-start.12 = (bf16[384,1024]{1,0:T(8,128)(2,1)S(1)}, bf16[384,1024]{1,0:T(8,128)(2,1)S(1)}, u32[]{:S(2)}, u32[]{:S(2)}) collective-permute-start(bf16[384,1024]{1,0:T(8,128)(2,1)S(1)} %copy-done), channel_id=1, source_target_pairs={{0,3},{1,0},{2,1},{3,2},{4,7},{5,4},{6,5},{7,6},{8,11},{9,8},{10,9... | collective-permute-start | bytes 2359304 | tf_op jit(solution)/shard_map/ppermute | solution.py:527
  209.3 25.2 %collective-permute-start.16 = (bf16[192,1024]{1,0:T(8,128)(2,1)S(1)}, bf16[192,1024]{1,0:T(8,128)(2,1)S(1)}, u32[]{:S(2)}, u32[]{:S(2)}) collective-permute-start(bf16[192,1024]{1,0:T(8,128)(2,1)S(1)} %slice.20), channel_id=1, source_target_pairs={{0,1},{1,2},{2,3},{3,0},{4,5},{5,6},{6,7},{7,4},{8,9},{9,10},{10,1... | collective-permute-start | bytes 1179656 | tf_op jit(solution)/shard_map/ppermute | solution.py:527
  209.3 25.1 %collective-permute-start.17 = (bf16[192,1024]{1,0:T(8,128)(2,1)S(1)}, bf16[192,1024]{1,0:T(8,128)(2,1)S(1)}, u32[]{:S(2)}, u32[]{:S(2)}) collective-permute-start(bf16[192,1024]{1,0:T(8,128)(2,1)S(1)} %slice.21), channel_id=1, source_target_pairs={{0,3},{1,0},{2,1},{3,2},{4,7},{5,4},{6,5},{7,6},{8,11},{9,8},{10,9... | collective-permute-start | bytes 1179656 | tf_op jit(solution)/shard_map/ppermute | solution.py:527
  212.0 48.5 %collective-permute-start.18 = (bf16[384,768]{1,0:T(8,128)(2,1)}, bf16[384,768]{1,0:T(8,128)(2,1)}, u32[]{:S(2)}, u32[]{:S(2)}) collective-permute-start(bf16[384,768]{1,0:T(8,128)(2,1)} %copy-done.16), channel_id=1, source_target_pairs={{0,2},{1,3},{2,0},{3,1},{4,6},{5,7},{6,4},{7,5},{8,10},{9,11},{10,... | collective-permute-start | bytes 1769480 | tf_op jit(solution)/shard_map/ppermute | solution.py:527
  212.9 21.6 %copy-start.4 = (bf16[384,768]{1,0:T(8,128)(2,1)S(1)}, bf16[384,768]{1,0:T(8,128)(2,1)}, u32[]{:S(2)}) copy-start(bf16[384,768]{1,0:T(8,128)(2,1)} %get-tuple-element.93.whole) | copy-start | bytes 1769476
  234.5 18.1 %copy-start.1 = (bf16[384,1024]{1,0:T(8,128)(2,1)S(1)}, bf16[384,1024]{1,0:T(8,128)(2,1)}, u32[]{:S(2)}) copy-start(bf16[384,1024]{1,0:T(8,128)(2,1)} %get-tuple-element.94.r0) | copy-start | bytes 2359300
  234.5 18.1 %copy-start.9 = (bf16[384,768]{1,0:T(8,128)(2,1)S(1)}, bf16[384,768]{1,0:T(8,128)(2,1)}, u32[]{:S(2)}) copy-start(bf16[384,768]{1,0:T(8,128)(2,1)} %copy-done.8) | copy-start | bytes 1769476
  234.5 18.1 %copy-start.11 = (bf16[384,768]{1,0:T(8,128)(2,1)S(1)}, bf16[384,768]{1,0:T(8,128)(2,1)}, u32[]{:S(2)}) copy-start(bf16[384,768]{1,0:T(8,128)(2,1)} %copy-done.10) | copy-start | bytes 1769476
  238.8 17.9 %copy-start.15 = (bf16[128,2]{0,1:T(2,128)(2,1)S(1)}, bf16[128,2]{0,1:T(2,128)(2,1)}, u32[]{:S(2)}) copy-start(bf16[128,2]{0,1:T(2,128)(2,1)} %param.8) | copy-start | bytes 1540
  238.8 21.7 %collective-permute-start.19 = (bf16[192,1024]{1,0:T(8,128)(2,1)}, bf16[192,1024]{1,0:T(8,128)(2,1)S(1)}, u32[]{:S(2)}, u32[]{:S(2)}) collective-permute-start(bf16[192,1024]{1,0:T(8,128)(2,1)} %slice.22), channel_id=1, source_target_pairs={{0,1},{1,2},{2,3},{3,0},{4,5},{5,6},{6,7},{7,4},{8,9},{9,10},{10,1... | collective-permute-start | bytes 1179656 | tf_op jit(solution)/shard_map/ppermute | solution.py:527
  238.8 21.7 %collective-permute-start.20 = (bf16[192,1024]{1,0:T(8,128)(2,1)}, bf16[192,1024]{1,0:T(8,128)(2,1)}, u32[]{:S(2)}, u32[]{:S(2)}) collective-permute-start(bf16[192,1024]{1,0:T(8,128)(2,1)} %slice.23), channel_id=1, source_target_pairs={{0,3},{1,0},{2,1},{3,2},{4,7},{5,4},{6,5},{7,6},{8,11},{9,8},{10,9... | collective-permute-start | bytes 1179656 | tf_op jit(solution)/shard_map/ppermute | solution.py:527
  (12 other events, 53.5 us)

commit v6 on v4

--- a/solution.py
+++ b/solution.py
@@ -565,8 +565,8 @@
     hidden, hidden_grad, ret = expert(wholes, ups, backs, experts)
     ret, t1, t3 = lax.optimization_barrier((ret, t1, t3))
     back = exchange(ret, experts)
-    hidden_near, far_tokens = lax.optimization_barrier((near(hidden), wholes[2]))
-    h0, h1, h2a, h2b, h3 = far(hidden_near)
+    h0, h1, h2a, h2b, h3 = far(near(hidden))
+    h2a, h2b, far_tokens = lax.optimization_barrier((h2a, h2b, wholes[2]))
     t2 = shift(far_tokens, 2)
     down_near = outer_near((h0, h1, h3), (g0, g1, g3))
     grads_near, down_near = lax.optimization_barrier((near(hidden_grad), down_near))

time: 260 us -> 264 us (1.015)
  waiting for transfers between devices: 129 us -> 144 us
  starting transfers between devices: 70.3 us -> 59.2 us
    ppermute x21, waiting for transfers between devices: 111 us -> 126 us  [shift(): lax.ppermute(values, 'cross', [(i, (i + by) % count) for i in range(count)])]
    ppermute x21, starting transfers between devices: 38.7 us -> 27.6 us  [shift(): lax.ppermute(values, 'cross', [(i, (i + by) % count) for i in range(count)])]
  transfers between devices with their start and end apart: 24 -> 24, of which waited for: 11 -> 10; matrix products, arithmetic and copies ran while one was open for 2% -> 2% of each run, Pallas kernels for 15% -> 14%
where the time goes in v6:
time: 264 us
  waiting for transfers between devices  144 us (55%)
  starting transfers between devices  59.2 us (22%)
  Pallas kernels  46.1 us (17%)
  local copies, waits for them, and re-layouts  13.1 us (5%)
    ppermute x21, waiting for transfers between devices, shift(): lax.ppermute(values, 'cross', [(i, (i + by) % count) for i in range(count)])  126 us
    all_to_all x3, starting transfers between devices, exchange(): lax.all_to_all(blocks, 'expert', split_axis=0, concat_axis=0, tiled=True)  31.6 us
    ppermute x21, starting transfers between devices, shift(): lax.ppermute(values, 'cross', [(i, (i + by) % count) for i in range(count)])  27.6 us
    all_to_all x3, waiting for transfers between devices, exchange(): lax.all_to_all(blocks, 'expert', split_axis=0, concat_axis=0, tiled=True)  18 us
    pallas_call x1, Pallas kernels, expert(): pl.pallas_call(expert_body, out_shape=[jax.ShapeDtypeStruct((rows, hidden...  12.8 us
    unnamed x40, local copies, waits for them, and re-layouts  8.23 us
    pallas_call x1, Pallas kernels, project(): pl.pallas_call(project_body, out_shape=[jax.ShapeDtypeStruct((rows, block...  7.34 us
    pallas_call x2, Pallas kernels, outer_near(): pl.pallas_call(near_body, out_shape=jax.ShapeDtypeStruct(shape, F32), in_...  7.33 us
  transfers between devices with their start and end apart: 24, of which 10 were waited for; matrix products, arithmetic and copies ran while one was open for 2% of the time, Pallas kernels for 14%

profile of v6, /device:TPU:1, one launch (start us, length us, event | category | flops | bytes accessed | tf_op | source)
XLA Modules:
  0.0 263.7 jit_solution(15906325078401989039)
XLA Ops:
  3.2 3.4 %collective-permute-start.2 = (bf16[144,768]{1,0:T(8,128)(2,1)S(1)}, bf16[144,768]{1,0:T(8,128)(2,1)S(1)}, u32[]{:S(2)}, u32[]{:S(2)}) collective-permute-start(bf16[144,768]{1,0:T(8,128)(2,1)S(1)} %get-tuple-element.57), channel_id=1, source_target_pairs={{0,3},{1,0},{2,1},{3,2},{4,7},{5,4},{6,5},{7,6},{8,11},{9,8},{10,9... | collective-permute-start | bytes 663560 | tf_op jit(solution)/shard_map/ppermute | solution.py:524
  7.7 7.8 %collective-permute-done.2.s1 = bf16[144,768]{1,0:T(8,128)(2,1)S(1)} collective-permute-done((bf16[144,768]{1,0:T(8,128)(2,1)S(1)}, bf16[144,768]{1,0:T(8,128)(2,1)S(1)}, u32[]{:S(2)}, u32[]{:S(2)}) %collective-permute-start.2) | collective-permute-done | bytes 221216 | tf_op jit(solution)/shard_map/ppermute | solution.py:524
  15.4 4.7 %collective-permute-done.4.s3 = bf16[144,768]{1,0:T(8,128)(2,1)S(1)} collective-permute-done((bf16[144,768]{1,0:T(8,128)(2,1)S(1)}, bf16[144,768]{1,0:T(8,128)(2,1)S(1)}, u32[]{:S(2)}, u32[]{:S(2)}) %collective-permute-start.4) | collective-permute-done | bytes 221216 | tf_op jit(solution)/shard_map/ppermute | solution.py:524
  20.1 2.5 shard_map.95
  22.6 12.1 %all-to-all-start.1 = ((bf16[64,8,2304]{2,1,0:T(8,128)(2,1)}), bf16[64,8,2304]{2,1,0:T(8,128)(2,1)S(1)}, u32[]{:S(2)}, u32[]{:S(2)}) async-start(bf16[64,8,2304]{2,1,0:T(8,128)(2,1)} %bitcast.6), calls=%async_computation.1 | async-start | bytes 4718592 | tf_op jit(solution)/shard_map/all_to_all | solution.py:543
  34.9 2.7 %collective-permute-start = (bf16[768,1024]{1,0:T(8,128)(2,1)}, bf16[768,1024]{1,0:T(8,128)(2,1)}, u32[]{:S(2)}, u32[]{:S(2)}) collective-permute-start(bf16[768,1024]{1,0:T(8,128)(2,1)} %bitcast.27), channel_id=1, source_target_pairs={{0,3},{1,0},{2,1},{3,2},{4,7},{5,4},{6,5},{7,6},{8,11},{9,8},{10,9... | collective-permute-start | bytes 4718600 | tf_op jit(solution)/shard_map/ppermute | solution.py:524
  37.5 3.7 %shard_map.93 = bf16[512,2304]{1,0:T(8,128)(2,1)} custom-call(s32[1]{0:T(128)} %bitcast.place_ref, s32[2,128]{1,0:T(2,128)} %bitcast.15, bf16[128,3072]{1,0:T(8,128)(2,1)} %values_ref.2), custom_call_target="tpu_custom_call" | custom-call | flops 603979776 | bytes 3145728 | tf_op jit(solution)/shard_map/pallas_call | solution.py:100
  41.2 30.7 %collective-permute-done.1.up3 = bf16[768,1024]{1,0:T(8,128)(2,1)} collective-permute-done((bf16[768,1024]{1,0:T(8,128)(2,1)}, bf16[768,1024]{1,0:T(8,128)(2,1)}, u32[]{:S(2)}, u32[]{:S(2)}) %collective-permute-start.1) | collective-permute-done | bytes 1572896 | tf_op jit(solution)/shard_map/ppermute | solution.py:524
  71.9 18.0 %all-to-all-done.1 = bf16[64,8,2304]{2,1,0:T(8,128)(2,1)S(1)} async-done(((bf16[64,8,2304]{2,1,0:T(8,128)(2,1)}), bf16[64,8,2304]{2,1,0:T(8,128)(2,1)S(1)}, u32[]{:S(2)}, u32[]{:S(2)}) %all-to-all-start.1) | async-done | bytes 2359328 | tf_op jit(solution)/shard_map/all_to_all | solution.py:543
  90.0 1.5 copy-done.17
  91.4 7.1 %all-to-all-start = ((bf16[64,8,2304]{2,1,0:T(8,128)(2,1)}), bf16[64,8,2304]{2,1,0:T(8,128)(2,1)S(1)}, u32[]{:S(2)}, u32[]{:S(2)}) async-start(bf16[64,8,2304]{2,1,0:T(8,128)(2,1)} %bitcast.20), calls=%async_computation | async-start | bytes 4718592 | tf_op jit(solution)/shard_map/all_to_all | solution.py:543
  99.8 2.1 slice.18
  101.8 2.7 %collective-permute-start.9 = (bf16[384,1024]{1,0:T(8,128)(2,1)S(1)}, bf16[384,1024]{1,0:T(8,128)(2,1)}, u32[]{:S(2)}, u32[]{:S(2)}) collective-permute-start(bf16[384,1024]{1,0:T(8,128)(2,1)S(1)} %slice.19), channel_id=1, source_target_pairs={{0,3},{1,0},{2,1},{3,2},{4,7},{5,4},{6,5},{7,6},{8,11},{9,8},{10,9... | collective-permute-start | bytes 2359304 | tf_op jit(solution)/shard_map/ppermute | solution.py:524
  104.5 7.3 %shard_map.96 = (bf16[384,768]{1,0:T(8,128)(2,1)}, bf16[384,768]{1,0:T(8,128)(2,1)}, bf16[384,768]{1,0:T(8,128)(2,1)}, bf16[384,768]{1,0:T(8,128)(2,1)}, f32[384...) custom-call(bf16[512,2304]{1,0:T(8,128)(2,1)} %bitcast.22, ...), custom_call_target="tpu_custom_call" | custom-call | flops 3019898880 | bytes 8257536 | tf_op jit(solution)/shard_map/pallas_call | solution.py:244
  113.3 24.9 %collective-permute-done.8.up2a = bf16[384,1024]{1,0:T(8,128)(2,1)} collective-permute-done((bf16[384,1024]{1,0:T(8,128)(2,1)}, bf16[384,1024]{1,0:T(8,128)(2,1)}, u32[]{:S(2)}, u32[]{:S(2)}) %collective-permute-start.8) | collective-permute-done | bytes 786464 | tf_op jit(solution)/shard_map/ppermute | solution.py:524
  140.0 15.7 %collective-permute-done.7.b3 = bf16[384,1024]{1,0:T(8,128)(2,1)} collective-permute-done((bf16[384,1024]{1,0:T(8,128)(2,1)}, bf16[384,1024]{1,0:T(8,128)(2,1)}, u32[]{:S(2)}, u32[]{:S(2)}) %collective-permute-start.7) | collective-permute-done | bytes 786464 | tf_op jit(solution)/shard_map/ppermute | solution.py:524
  155.7 2.0 shard_map.97
  160.6 2.7 %collective-permute-start.10 = (bf16[384,768]{1,0:T(8,128)(2,1)}, bf16[384,768]{1,0:T(8,128)(2,1)}, u32[]{:S(2)}, u32[]{:S(2)}) collective-permute-start(bf16[384,768]{1,0:T(8,128)(2,1)} %get-tuple-element.71.x3), channel_id=1, source_target_pairs={{0,3},{1,0},{2,1},{3,2},{4,7},{5,4},{6,5},{7,6},{8,11},{9,8},{10,9... | collective-permute-start | bytes 1769480 | tf_op jit(solution)/shard_map/ppermute | solution.py:524
  163.3 12.8 %shard_map.98 = (bf16[384,1024]{1,0:T(8,128)(2,1)}, bf16[384,1024]{1,0:T(8,128)(2,1)}, bf16[512,2432]{1,0:T(8,128)(2,1)}) custom-call(bf16[384,768]{1,0:T(8,128)(2,1)} %copy-done.8, bf16[384,768]{1,0:T(8,128)(2,1)} %get-tuple-element.69.x1, bf16[384,768]{1,0:T(8,128)(2,1)} %copy-done.16, bf16[384,768]{1,0:T(8,128)(2,1)} %get-tuple-element.71.x3, ...), custom_call_target="tpu_custom_call" | custom-call | flops 6039797760 | bytes 18874368 | tf_op jit(solution)/shard_map/pallas_call | solution.py:376
  177.0 12.3 %all-to-all-start.2 = ((bf16[64,8,2432]{2,1,0:T(8,128)(2,1)}), bf16[64,8,2432]{2,1,0:T(8,128)(2,1)}, u32[]{:S(2)}, u32[]{:S(2)}) async-start(bf16[64,8,2432]{2,1,0:T(8,128)(2,1)} %bitcast.21), calls=%async_computation.2 | async-start | bytes 4980736 | tf_op jit(solution)/shard_map/all_to_all | solution.py:543
  189.4 2.7 %collective-permute-start.14 = (bf16[384,1024]{1,0:T(8,128)(2,1)S(1)}, bf16[384,1024]{1,0:T(8,128)(2,1)S(1)}, u32[]{:S(2)}, u32[]{:S(2)}) collective-permute-start(bf16[384,1024]{1,0:T(8,128)(2,1)S(1)} %copy-done.2), channel_id=1, source_target_pairs={{0,3},{1,0},{2,1},{3,2},{4,7},{5,4},{6,5},{7,6},{8,11},{9,8},{10,9... | collective-permute-start | bytes 2359304 | tf_op jit(solution)/shard_map/ppermute | solution.py:524
  192.0 2.7 %collective-permute-start.12 = (bf16[384,1024]{1,0:T(8,128)(2,1)S(1)}, bf16[384,1024]{1,0:T(8,128)(2,1)S(1)}, u32[]{:S(2)}, u32[]{:S(2)}) collective-permute-start(bf16[384,1024]{1,0:T(8,128)(2,1)S(1)} %copy-done), channel_id=1, source_target_pairs={{0,3},{1,0},{2,1},{3,2},{4,7},{5,4},{6,5},{7,6},{8,11},{9,8},{10,9... | collective-permute-start | bytes 2359304 | tf_op jit(solution)/shard_map/ppermute | solution.py:524
  194.7 14.5 %collective-permute-done.15.l3 = bf16[384,1024]{1,0:T(8,128)(2,1)S(1)} collective-permute-done((bf16[384,1024]{1,0:T(8,128)(2,1)S(1)}, bf16[384,1024]{1,0:T(8,128)(2,1)S(1)}, u32[]{:S(2)}, u32[]{:S(2)}) %collective-permute-start.15) | collective-permute-done | bytes 786464 | tf_op jit(solution)/shard_map/ppermute | solution.py:524
  209.4 2.7 %collective-permute-start.17 = (bf16[192,1024]{1,0:T(8,128)(2,1)S(1)}, bf16[192,1024]{1,0:T(8,128)(2,1)S(1)}, u32[]{:S(2)}, u32[]{:S(2)}) collective-permute-start(bf16[192,1024]{1,0:T(8,128)(2,1)S(1)} %slice.25), channel_id=1, source_target_pairs={{0,3},{1,0},{2,1},{3,2},{4,7},{5,4},{6,5},{7,6},{8,11},{9,8},{10,9... | collective-permute-start | bytes 1179656 | tf_op jit(solution)/shard_map/ppermute | solution.py:524
  212.1 22.4 %collective-permute-done.16.first = bf16[192,1024]{1,0:T(8,128)(2,1)S(1)} collective-permute-done((bf16[192,1024]{1,0:T(8,128)(2,1)S(1)}, bf16[192,1024]{1,0:T(8,128)(2,1)S(1)}, u32[]{:S(2)}, u32[]{:S(2)}) %collective-permute-start.16) | collective-permute-done | bytes 393248 | tf_op jit(solution)/shard_map/ppermute | solution.py:524
  236.0 3.2 %shard_map.99.total_ref = f32[1024,768]{1,0:T(8,128)S(1)} custom-call(bf16[384,1024]{1,0:T(8,128)(2,1)S(1)} %copy-done.2, bf16[384,1024]{1,0:T(8,128)(2,1)S(1)} %collective-permute-done.14.l1, bf16[384,1024]{1,0:T(8,128)(2,1)S(1)} %collective-permute-done.15.l3, bf16[384,768]{1,0:T(8,128)(2,1)S(1)} %copy-done.5, bf16[384,768]{1,0:T(8,128)(2,1)S(1)} %copy-done.6, ...), custom_call_target="tpu_custom_call" | custom-call | flops 1811939328 | bytes 7274496 | tf_op jit(solution)/shard_map/pallas_call | solution.py:474
  240.9 1.5 collective-permute-start.19
  243.5 4.1 %shard_map.101.total_ref = f32[768,1024]{1,0:T(8,128)S(1)} custom-call(bf16[384,768]{1,0:T(8,128)(2,1)S(1)} %copy-done.9, bf16[384,768]{1,0:T(8,128)(2,1)} %collective-permute-done.10.l1, bf16[384,768]{1,0:T(8,128)(2,1)S(1)} %copy-done.11, bf16[384,1024]{1,0:T(8,128)(2,1)S(1)} %copy-done.1, bf16[384,1024]{1,0:T(8,128)(2,1)S(1)} %collective-permute-done.12.r1, ...), custom_call_target="tpu_custom_call" | custom-call | flops 1811939328 | bytes 7274496 | tf_op jit(solution)/shard_map/pallas_call | solution.py:474
  247.7 2.8 %shard_map.100 = bf16[1024,768]{1,0:T(8,128)(2,1)} custom-call(f32[1024,768]{1,0:T(8,128)S(1)} %shard_map.99.total_ref, bf16[384,768]{1,0:T(8,128)(2,1)S(1)} %copy-done.4, bf16[192,1024]{1,0:T(8,128)(2,1)S(1)} %collective-permute-done.16.first, bf16[192,1024]{1,0:T(8,128)(2,1)S(1)} %collective-permute-done.17.second), custom_call_target="tpu_custom_call" | custom-call | flops 603979776 | bytes 6094848 | tf_op jit(solution)/shard_map/pallas_call | solution.py:508
  250.4 3.8 %shard_map.102 = (bf16[128,3072]{1,0:T(8,128)(2,1)}, bf16[2,128]{1,0:T(2,128)(2,1)}) custom-call(s32[1]{0:T(128)} %bitcast.place_ref, s32[2,128]{1,0:T(2,128)S(1)} %bitcast.17, bf16[2,128]{1,0:T(2,128)(2,1)S(1)} %bitcast.19, bf16[512,2432]{1,0:T(8,128)(2,1)} %bitcast.10.ret_ref), custom_call_target="tpu_custom_call" | custom-call | flops 805306368 | bytes 3276800 | tf_op jit(solution)/shard_map/pallas_call | solution.py:441
  254.3 5.7 %collective-permute-done.19.first = bf16[192,1024]{1,0:T(8,128)(2,1)S(1)} collective-permute-done((bf16[192,1024]{1,0:T(8,128)(2,1)}, bf16[192,1024]{1,0:T(8,128)(2,1)S(1)}, u32[]{:S(2)}, u32[]{:S(2)}) %collective-permute-start.19) | collective-permute-done | bytes 393248 | tf_op jit(solution)/shard_map/ppermute | solution.py:524
  259.9 3.7 %shard_map.103 = bf16[768,1024]{1,0:T(8,128)(2,1)} custom-call(f32[768,1024]{1,0:T(8,128)S(1)} %shard_map.101.total_ref, bf16[384,768]{1,0:T(8,128)(2,1)} %collective-permute-done.18.whole, bf16[192,1024]{1,0:T(8,128)(2,1)S(1)} %collective-permute-done.19.first, bf16[192,1024]{1,0:T(8,128)(2,1)} %collective-permute-done.20.second), custom_call_target="tpu_custom_call" | custom-call | flops 603979776 | bytes 6094848 | tf_op jit(solution)/shard_map/pallas_call | solution.py:508
  (73 shorter events, 16.4 us)
Async XLA Ops:
  3.2 12.3 %collective-permute-start.2 = (bf16[144,768]{1,0:T(8,128)(2,1)S(1)}, bf16[144,768]{1,0:T(8,128)(2,1)S(1)}, u32[]{:S(2)}, u32[]{:S(2)}) collective-permute-start(bf16[144,768]{1,0:T(8,128)(2,1)S(1)} %get-tuple-element.57), channel_id=1, source_target_pairs={{0,3},{1,0},{2,1},{3,2},{4,7},{5,4},{6,5},{7,6},{8,11},{9,8},{10,9... | collective-permute-start | bytes 663560 | tf_op jit(solution)/shard_map/ppermute | solution.py:524
  6.6 8.9 %collective-permute-start.3 = (bf16[144,768]{1,0:T(8,128)(2,1)S(1)}, bf16[144,768]{1,0:T(8,128)(2,1)S(1)}, u32[]{:S(2)}, u32[]{:S(2)}) collective-permute-start(bf16[144,768]{1,0:T(8,128)(2,1)S(1)} %get-tuple-element.58), channel_id=1, source_target_pairs={{0,2},{1,3},{2,0},{3,1},{4,6},{5,7},{6,4},{7,5},{8,10},{9,11},{10,... | collective-permute-start | bytes 663560 | tf_op jit(solution)/shard_map/ppermute | solution.py:524
  7.1 13.1 %collective-permute-start.4 = (bf16[144,768]{1,0:T(8,128)(2,1)S(1)}, bf16[144,768]{1,0:T(8,128)(2,1)S(1)}, u32[]{:S(2)}, u32[]{:S(2)}) collective-permute-start(bf16[144,768]{1,0:T(8,128)(2,1)S(1)} %get-tuple-element.59), channel_id=1, source_target_pairs={{0,1},{1,2},{2,3},{3,0},{4,5},{5,6},{6,7},{7,4},{8,9},{9,10},{10,1... | collective-permute-start | bytes 663560 | tf_op jit(solution)/shard_map/ppermute | solution.py:524
  22.6 67.3 %all-to-all-start.1 = ((bf16[64,8,2304]{2,1,0:T(8,128)(2,1)}), bf16[64,8,2304]{2,1,0:T(8,128)(2,1)S(1)}, u32[]{:S(2)}, u32[]{:S(2)}) async-start(bf16[64,8,2304]{2,1,0:T(8,128)(2,1)} %bitcast.6), calls=%async_computation.1 | async-start | bytes 4718592 | tf_op jit(solution)/shard_map/all_to_all | solution.py:543
  34.8 37.1 %collective-permute-start.1 = (bf16[768,1024]{1,0:T(8,128)(2,1)}, bf16[768,1024]{1,0:T(8,128)(2,1)}, u32[]{:S(2)}, u32[]{:S(2)}) collective-permute-start(bf16[768,1024]{1,0:T(8,128)(2,1)} %bitcast.26), channel_id=1, source_target_pairs={{0,1},{1,2},{2,3},{3,0},{4,5},{5,6},{6,7},{7,4},{8,9},{9,10},{10,1... | collective-permute-start | bytes 4718600 | tf_op jit(solution)/shard_map/ppermute | solution.py:524
  34.9 37.0 %collective-permute-start = (bf16[768,1024]{1,0:T(8,128)(2,1)}, bf16[768,1024]{1,0:T(8,128)(2,1)}, u32[]{:S(2)}, u32[]{:S(2)}) collective-permute-start(bf16[768,1024]{1,0:T(8,128)(2,1)} %bitcast.27), channel_id=1, source_target_pairs={{0,3},{1,0},{2,1},{3,2},{4,7},{5,4},{6,5},{7,6},{8,11},{9,8},{10,9... | collective-permute-start | bytes 4718600 | tf_op jit(solution)/shard_map/ppermute | solution.py:524
  91.4 64.3 %all-to-all-start = ((bf16[64,8,2304]{2,1,0:T(8,128)(2,1)}), bf16[64,8,2304]{2,1,0:T(8,128)(2,1)S(1)}, u32[]{:S(2)}, u32[]{:S(2)}) async-start(bf16[64,8,2304]{2,1,0:T(8,128)(2,1)} %bitcast.20), calls=%async_computation | async-start | bytes 4718592 | tf_op jit(solution)/shard_map/all_to_all | solution.py:543
  101.8 36.4 %collective-permute-start.8 = (bf16[384,1024]{1,0:T(8,128)(2,1)}, bf16[384,1024]{1,0:T(8,128)(2,1)}, u32[]{:S(2)}, u32[]{:S(2)}) collective-permute-start(bf16[384,1024]{1,0:T(8,128)(2,1)} %slice.18), channel_id=1, source_target_pairs={{0,1},{1,2},{2,3},{3,0},{4,5},{5,6},{6,7},{7,4},{8,9},{9,10},{10,1... | collective-permute-start | bytes 2359304 | tf_op jit(solution)/shard_map/ppermute | solution.py:524
  101.8 36.4 %collective-permute-start.9 = (bf16[384,1024]{1,0:T(8,128)(2,1)S(1)}, bf16[384,1024]{1,0:T(8,128)(2,1)}, u32[]{:S(2)}, u32[]{:S(2)}) collective-permute-start(bf16[384,1024]{1,0:T(8,128)(2,1)S(1)} %slice.19), channel_id=1, source_target_pairs={{0,3},{1,0},{2,1},{3,2},{4,7},{5,4},{6,5},{7,6},{8,11},{9,8},{10,9... | collective-permute-start | bytes 2359304 | tf_op jit(solution)/shard_map/ppermute | solution.py:524
  111.8 26.4 %collective-permute-start.5 = (bf16[384,1024]{1,0:T(8,128)(2,1)}, bf16[384,1024]{1,0:T(8,128)(2,1)S(1)}, u32[]{:S(2)}, u32[]{:S(2)}) collective-permute-start(bf16[384,1024]{1,0:T(8,128)(2,1)} %get-tuple-element.61), channel_id=1, source_target_pairs={{0,3},{1,0},{2,1},{3,2},{4,7},{5,4},{6,5},{7,6},{8,11},{9,8},{10,9... | collective-permute-start | bytes 2359304 | tf_op jit(solution)/shard_map/ppermute | solution.py:524
  111.9 26.4 %collective-permute-start.6 = (bf16[384,1024]{1,0:T(8,128)(2,1)}, bf16[384,1024]{1,0:T(8,128)(2,1)S(1)}, u32[]{:S(2)}, u32[]{:S(2)}) collective-permute-start(bf16[384,1024]{1,0:T(8,128)(2,1)} %get-tuple-element.62), channel_id=1, source_target_pairs={{0,2},{1,3},{2,0},{3,1},{4,6},{5,7},{6,4},{7,5},{8,10},{9,11},{10,... | collective-permute-start | bytes 2359304 | tf_op jit(solution)/shard_map/ppermute | solution.py:524
  112.4 43.3 %collective-permute-start.7 = (bf16[384,1024]{1,0:T(8,128)(2,1)}, bf16[384,1024]{1,0:T(8,128)(2,1)}, u32[]{:S(2)}, u32[]{:S(2)}) collective-permute-start(bf16[384,1024]{1,0:T(8,128)(2,1)} %get-tuple-element.63), channel_id=1, source_target_pairs={{0,1},{1,2},{2,3},{3,0},{4,5},{5,6},{6,7},{7,4},{8,9},{9,10},{10,1... | collective-permute-start | bytes 2359304 | tf_op jit(solution)/shard_map/ppermute | solution.py:524
  159.4 16.7 %collective-permute-start.11 = (bf16[384,768]{1,0:T(8,128)(2,1)}, bf16[384,768]{1,0:T(8,128)(2,1)S(1)}, u32[]{:S(2)}, u32[]{:S(2)}) collective-permute-start(bf16[384,768]{1,0:T(8,128)(2,1)} %get-tuple-element.69.x1), channel_id=1, source_target_pairs={{0,1},{1,2},{2,3},{3,0},{4,5},{5,6},{6,7},{7,4},{8,9},{9,10},{10,1... | collective-permute-start | bytes 1769480 | tf_op jit(solution)/shard_map/ppermute | solution.py:524
  160.6 16.3 %collective-permute-start.10 = (bf16[384,768]{1,0:T(8,128)(2,1)}, bf16[384,768]{1,0:T(8,128)(2,1)}, u32[]{:S(2)}, u32[]{:S(2)}) collective-permute-start(bf16[384,768]{1,0:T(8,128)(2,1)} %get-tuple-element.71.x3), channel_id=1, source_target_pairs={{0,3},{1,0},{2,1},{3,2},{4,7},{5,4},{6,5},{7,6},{8,11},{9,8},{10,9... | collective-permute-start | bytes 1769480 | tf_op jit(solution)/shard_map/ppermute | solution.py:524
  176.9 12.3 %copy-start.2 = (bf16[384,1024]{1,0:T(8,128)(2,1)S(1)}, bf16[384,1024]{1,0:T(8,128)(2,1)}, u32[]{:S(2)}) copy-start(bf16[384,1024]{1,0:T(8,128)(2,1)} %get-tuple-element.84.l0) | copy-start | bytes 2359300
  176.9 15.1 %copy-start = (bf16[384,1024]{1,0:T(8,128)(2,1)S(1)}, bf16[384,1024]{1,0:T(8,128)(2,1)}, u32[]{:S(2)}) copy-start(bf16[384,1024]{1,0:T(8,128)(2,1)} %get-tuple-element.94.r0) | copy-start | bytes 2359300
  177.0 59.0 %copy-start.5 = (bf16[384,768]{1,0:T(8,128)(2,1)S(1)}, bf16[384,768]{1,0:T(8,128)(2,1)}, u32[]{:S(2)}) copy-start(bf16[384,768]{1,0:T(8,128)(2,1)} %get-tuple-element.85.r0) | copy-start | bytes 1769476
  177.0 59.0 %copy-start.6 = (bf16[384,768]{1,0:T(8,128)(2,1)S(1)}, bf16[384,768]{1,0:T(8,128)(2,1)}, u32[]{:S(2)}) copy-start(bf16[384,768]{1,0:T(8,128)(2,1)} %get-tuple-element.86.r1) | copy-start | bytes 1769476
  177.0 59.0 %copy-start.7 = (bf16[384,768]{1,0:T(8,128)(2,1)S(1)}, bf16[384,768]{1,0:T(8,128)(2,1)}, u32[]{:S(2)}) copy-start(bf16[384,768]{1,0:T(8,128)(2,1)} %get-tuple-element.87.r3) | copy-start | bytes 1769476
  177.0 73.5 %all-to-all-start.2 = ((bf16[64,8,2432]{2,1,0:T(8,128)(2,1)}), bf16[64,8,2432]{2,1,0:T(8,128)(2,1)}, u32[]{:S(2)}, u32[]{:S(2)}) async-start(bf16[64,8,2432]{2,1,0:T(8,128)(2,1)} %bitcast.21), calls=%async_computation.2 | async-start | bytes 4980736 | tf_op jit(solution)/shard_map/all_to_all | solution.py:543
  189.3 20.0 %collective-permute-start.15 = (bf16[384,1024]{1,0:T(8,128)(2,1)S(1)}, bf16[384,1024]{1,0:T(8,128)(2,1)S(1)}, u32[]{:S(2)}, u32[]{:S(2)}) collective-permute-start(bf16[384,1024]{1,0:T(8,128)(2,1)S(1)} %copy-done.2), channel_id=1, source_target_pairs={{0,1},{1,2},{2,3},{3,0},{4,5},{5,6},{6,7},{7,4},{8,9},{9,10},{10,1... | collective-permute-start | bytes 2359304 | tf_op jit(solution)/shard_map/ppermute | solution.py:524
  189.4 20.0 %collective-permute-start.14 = (bf16[384,1024]{1,0:T(8,128)(2,1)S(1)}, bf16[384,1024]{1,0:T(8,128)(2,1)S(1)}, u32[]{:S(2)}, u32[]{:S(2)}) collective-permute-start(bf16[384,1024]{1,0:T(8,128)(2,1)S(1)} %copy-done.2), channel_id=1, source_target_pairs={{0,3},{1,0},{2,1},{3,2},{4,7},{5,4},{6,5},{7,6},{8,11},{9,8},{10,9... | collective-permute-start | bytes 2359304 | tf_op jit(solution)/shard_map/ppermute | solution.py:524
  192.0 47.2 %collective-permute-start.13 = (bf16[384,1024]{1,0:T(8,128)(2,1)S(1)}, bf16[384,1024]{1,0:T(8,128)(2,1)S(1)}, u32[]{:S(2)}, u32[]{:S(2)}) collective-permute-start(bf16[384,1024]{1,0:T(8,128)(2,1)S(1)} %copy-done), channel_id=1, source_target_pairs={{0,1},{1,2},{2,3},{3,0},{4,5},{5,6},{6,7},{7,4},{8,9},{9,10},{10,1... | collective-permute-start | bytes 2359304 | tf_op jit(solution)/shard_map/ppermute | solution.py:524
  192.0 47.2 %collective-permute-start.12 = (bf16[384,1024]{1,0:T(8,128)(2,1)S(1)}, bf16[384,1024]{1,0:T(8,128)(2,1)S(1)}, u32[]{:S(2)}, u32[]{:S(2)}) collective-permute-start(bf16[384,1024]{1,0:T(8,128)(2,1)S(1)} %copy-done), channel_id=1, source_target_pairs={{0,3},{1,0},{2,1},{3,2},{4,7},{5,4},{6,5},{7,6},{8,11},{9,8},{10,9... | collective-permute-start | bytes 2359304 | tf_op jit(solution)/shard_map/ppermute | solution.py:524
  209.3 25.2 %collective-permute-start.16 = (bf16[192,1024]{1,0:T(8,128)(2,1)S(1)}, bf16[192,1024]{1,0:T(8,128)(2,1)S(1)}, u32[]{:S(2)}, u32[]{:S(2)}) collective-permute-start(bf16[192,1024]{1,0:T(8,128)(2,1)S(1)} %slice.24), channel_id=1, source_target_pairs={{0,1},{1,2},{2,3},{3,0},{4,5},{5,6},{6,7},{7,4},{8,9},{9,10},{10,1... | collective-permute-start | bytes 1179656 | tf_op jit(solution)/shard_map/ppermute | solution.py:524
  209.4 25.1 %collective-permute-start.17 = (bf16[192,1024]{1,0:T(8,128)(2,1)S(1)}, bf16[192,1024]{1,0:T(8,128)(2,1)S(1)}, u32[]{:S(2)}, u32[]{:S(2)}) collective-permute-start(bf16[192,1024]{1,0:T(8,128)(2,1)S(1)} %slice.25), channel_id=1, source_target_pairs={{0,3},{1,0},{2,1},{3,2},{4,7},{5,4},{6,5},{7,6},{8,11},{9,8},{10,9... | collective-permute-start | bytes 1179656 | tf_op jit(solution)/shard_map/ppermute | solution.py:524
  234.5 25.4 %collective-permute-start.18 = (bf16[384,768]{1,0:T(8,128)(2,1)}, bf16[384,768]{1,0:T(8,128)(2,1)}, u32[]{:S(2)}, u32[]{:S(2)}) collective-permute-start(bf16[384,768]{1,0:T(8,128)(2,1)} %copy-done.16), channel_id=1, source_target_pairs={{0,2},{1,3},{2,0},{3,1},{4,6},{5,7},{6,4},{7,5},{8,10},{9,11},{10,... | collective-permute-start | bytes 1769480 | tf_op jit(solution)/shard_map/ppermute | solution.py:524
  236.0 7.6 %copy-start.1 = (bf16[384,1024]{1,0:T(8,128)(2,1)S(1)}, bf16[384,1024]{1,0:T(8,128)(2,1)}, u32[]{:S(2)}) copy-start(bf16[384,1024]{1,0:T(8,128)(2,1)} %get-tuple-element.94.r0) | copy-start | bytes 2359300
  236.0 7.5 %copy-start.9 = (bf16[384,768]{1,0:T(8,128)(2,1)S(1)}, bf16[384,768]{1,0:T(8,128)(2,1)}, u32[]{:S(2)}) copy-start(bf16[384,768]{1,0:T(8,128)(2,1)} %copy-done.8) | copy-start | bytes 1769476
  236.0 7.5 %copy-start.11 = (bf16[384,768]{1,0:T(8,128)(2,1)S(1)}, bf16[384,768]{1,0:T(8,128)(2,1)}, u32[]{:S(2)}) copy-start(bf16[384,768]{1,0:T(8,128)(2,1)} %copy-done.10) | copy-start | bytes 1769476
  240.9 19.1 %collective-permute-start.19 = (bf16[192,1024]{1,0:T(8,128)(2,1)}, bf16[192,1024]{1,0:T(8,128)(2,1)S(1)}, u32[]{:S(2)}, u32[]{:S(2)}) collective-permute-start(bf16[192,1024]{1,0:T(8,128)(2,1)} %slice.22), channel_id=1, source_target_pairs={{0,1},{1,2},{2,3},{3,0},{4,5},{5,6},{6,7},{7,4},{8,9},{9,10},{10,1... | collective-permute-start | bytes 1179656 | tf_op jit(solution)/shard_map/ppermute | solution.py:524
  242.3 17.6 %collective-permute-start.20 = (bf16[192,1024]{1,0:T(8,128)(2,1)}, bf16[192,1024]{1,0:T(8,128)(2,1)}, u32[]{:S(2)}, u32[]{:S(2)}) collective-permute-start(bf16[192,1024]{1,0:T(8,128)(2,1)} %slice.23), channel_id=1, source_target_pairs={{0,3},{1,0},{2,1},{3,2},{4,7},{5,4},{6,5},{7,6},{8,11},{9,8},{10,9... | collective-permute-start | bytes 1179656 | tf_op jit(solution)/shard_map/ppermute | solution.py:524
  (12 other events, 20.6 us)
